TPU v7x, 256 devices: a whole 4x4x8 slice. The times are simulated.
256 devices in a mesh: gx: 8 (over x, z_hi), gy: 32 (over y, z_lo, core).
Axes of the slice: x: 4, y: 4, z: 8 (z_hi: 2, z_lo: 4; z = z_hi * 4 + z_lo), core: 2. Of those that a mesh axis runs over, the one named last changes fastest.
Arguments:
- positions: float32 [48, 32, 3, 128], P('gx', 'gy'), may hold values from 0 to 288, as said below
- species: int32 [48, 32, 128], P('gx', 'gy'), may hold values from 0 to 88
- pair_codes: int32 [8, 32, 26], P('gx', 'gy'), may hold values from 0 to 53, as said below
- pair_count: int32 [8, 32], P('gx', 'gy'), may hold values from 1 to 26, as said below
- embed_table: bfloat16 [89, 128], replicated, may hold values from -6 to 6
- scalar_radial_one: float32 [4, 128], replicated, may hold values from -6 to 6
- vector_radial_one: float32 [4, 128], replicated, may hold values from -6 to 6
- scalar_radial_two: float32 [4, 128], replicated, may hold values from -6 to 6
- vector_radial_two: float32 [4, 128], replicated, may hold values from -6 to 6
- mixing_scalar_one: bfloat16 [128, 128], replicated, may hold values from -0.5 to 0.5
- mixing_vector_one: bfloat16 [128, 128], replicated, may hold values from -0.5 to 0.5
- mixing_two: bfloat16 [128, 128], replicated, may hold values from -0.5 to 0.5
- readout: float32 [128], replicated, may hold values from -0.5 to 0.5
Outputs:
- atom_energy: float32 [48, 32, 128], P('gx', 'gy')
- forces: float32 [48, 32, 3, 128], P('gx', 'gy')
Inputs may be any that keep to these rules, and one draw needn't show every extreme that they name: `positions`: each atom lies in its block: x in [6 x_block, 6 x_block + 6), y in [6 y_block, 6 y_block + 6), z in [0, 24). `pair_codes`: the first pair_count entries of a device's list are distinct codes whose far block lies inside the grid of 48 x 32 blocks; entries after them are codes of the same range that take no part. `pair_count`: some device holds 26 pairs in every draw.
All inputs are finite; a program needn't handle non-finite values.
Results may differ from a plain program's by a relative error of at most 0.004.
Values may be sent and summed in bfloat16 or wider, within the bound.
No kernel may reach another device: no remote copies, remote signals or barrier semaphores. Data moves between devices by JAX's collectives and lax.ppermute only.
A program may use at most 64 MiB of HBM per device.

v0:
```python
import jax
import jax.numpy as jnp
from jax import lax
from jax.sharding import PartitionSpec as P

soften = 0.25
cutoff = 6.0
spread = 1.5
message_scale = 0.125


def passed_along(block, axis, distance):
    devices = range(lax.axis_size(axis))
    route = [(i - distance, i) for i in devices if i - distance in devices]
    return lax.ppermute(block, axis, route)


def extended_2(x, sides, width):
    for axis, dim in sides:
        size, length = (lax.axis_size(axis), x.shape[dim])
        up = [(i, (i + 1) % size) for i in range(size - 1)]
        down = [(j, i) for i, j in up]
        last = lax.slice_in_dim(x, length - width, length, axis=dim)
        leading = lax.slice_in_dim(x, 0, width, axis=dim)
        before = lax.ppermute(last, axis, up)
        after = lax.ppermute(leading, axis, down)
        x = jnp.concatenate([before, x, after], axis=dim)
    return x


def geometry(home_pos, other_pos, self_flag, radial_count):
    offset = other_pos[:, None, :] - home_pos[:, :, None]
    squared = jnp.sum(offset * offset, axis=0)
    softened = jnp.sqrt(squared + soften)
    tapering = jnp.maximum(1.0 - squared / (cutoff * cutoff), 0.0)
    atoms_here = home_pos.shape[1]
    row_ids = lax.broadcasted_iota(jnp.int32, (atoms_here, atoms_here), 0)
    col_ids = lax.broadcasted_iota(jnp.int32, (atoms_here, atoms_here), 1)
    diagonal = (row_ids == col_ids).astype(jnp.float32)
    envelope = tapering * tapering * (1.0 - self_flag * diagonal)
    centres = cutoff * (jnp.arange(radial_count, dtype=jnp.float32) + 0.5) / radial_count
    radial = envelope[None] * jnp.exp(
        -jnp.square((softened[None] - centres[:, None, None]) / spread)
    )
    direction = offset / softened[None]
    return (radial, direction)


def tiles(radial, direction):
    plain_tile = radial.astype(jnp.bfloat16)
    tilted = (radial[:, None] * direction[None]).astype(jnp.bfloat16)
    return (plain_tile, tilted)


def layer_one(radial, direction, source, scalar_w, vector_w):
    plain_tile, tilted = tiles(radial, direction)
    scalar_part = jnp.einsum("kab,bc->kac", plain_tile, source, preferred_element_type=jnp.float32)
    vector_part = jnp.einsum("kdab,bc->kdac", tilted, source, preferred_element_type=jnp.float32)
    return (
        jnp.sum(scalar_w[:, None, :] * scalar_part, axis=0),
        jnp.sum(vector_w[:, None, None, :] * vector_part, axis=0),
    )


def layer_two(radial, direction, source, scalar_w, vector_w):
    plain_tile, tilted = tiles(radial, direction)
    scalar_part = jnp.einsum(
        "kab,bc->kac", plain_tile, source[0], preferred_element_type=jnp.float32
    )
    tensor_part = jnp.einsum(
        "kdab,dbc->kac", tilted, source[1:], preferred_element_type=jnp.float32
    )
    return jnp.sum(scalar_w[:, None, :] * scalar_part + vector_w[:, None, :] * tensor_part, axis=0)


def pull_back(pullback, radial, direction, plain_grad, tilted_grad):
    radial_grad = plain_grad + jnp.sum(tilted_grad * direction[None], axis=1)
    direction_grad = jnp.sum(tilted_grad * radial[:, None], axis=0)
    return pullback((radial_grad, direction_grad))


def back_one(home_pos, other_pos, self_flag, source, scalar_in, vector_in, scalar_w, vector_w):
    radial_count = scalar_w.shape[0]
    (radial, direction), pullback = jax.vjp(
        lambda home_side, far_side: geometry(home_side, far_side, self_flag, radial_count),
        home_pos,
        other_pos,
    )
    scalar_cot = (scalar_w[:, None, :] * scalar_in[None]).astype(jnp.bfloat16)
    vector_cot = (vector_w[:, None, None, :] * vector_in[None]).astype(jnp.bfloat16)
    plain_grad = jnp.einsum("kac,bc->kab", scalar_cot, source, preferred_element_type=jnp.float32)
    tilted_grad = jnp.einsum(
        "kdac,bc->kdab", vector_cot, source, preferred_element_type=jnp.float32
    )
    return pull_back(pullback, radial, direction, plain_grad, tilted_grad)


def two_cotangents(gradient_in, scalar_w, vector_w):
    scalar_cot = (scalar_w[:, None, :] * gradient_in[None]).astype(jnp.bfloat16)
    tensor_cot = (vector_w[:, None, :] * gradient_in[None]).astype(jnp.bfloat16)
    return (scalar_cot, tensor_cot)


def far_terms(plain_tile, tilted, scalar_cot, tensor_cot):
    scalar_grad = jnp.einsum(
        "kab,kac->bc", plain_tile, scalar_cot, preferred_element_type=jnp.float32
    )
    vector_grad = jnp.einsum(
        "kdab,kac->dbc", tilted, tensor_cot, preferred_element_type=jnp.float32
    )
    return jnp.concatenate([scalar_grad[None], vector_grad], axis=0)


def back_two(home_pos, other_pos, self_flag, source, gradient_in, scalar_w, vector_w):
    radial_count = scalar_w.shape[0]
    (radial, direction), pullback = jax.vjp(
        lambda home_side, far_side: geometry(home_side, far_side, self_flag, radial_count),
        home_pos,
        other_pos,
    )
    scalar_cot, tensor_cot = two_cotangents(gradient_in, scalar_w, vector_w)
    plain_grad = jnp.einsum(
        "kac,bc->kab", scalar_cot, source[0], preferred_element_type=jnp.float32
    )
    tilted_grad = jnp.einsum(
        "kac,dbc->kdab", tensor_cot, source[1:], preferred_element_type=jnp.float32
    )
    home_grad, other_grad = pull_back(pullback, radial, direction, plain_grad, tilted_grad)
    plain_tile, tilted = tiles(radial, direction)
    return (home_grad, other_grad, far_terms(plain_tile, tilted, scalar_cot, tensor_cot))


def silu_slope(value):
    sigma = jax.nn.sigmoid(value)
    return sigma * (1.0 + value * (1.0 - sigma))


def decode(pair_code):
    block_index = pair_code // 9
    offset = pair_code % 9
    return (block_index, block_index + offset // 3, offset % 3, (offset == 4).astype(jnp.float32))


def fold_features(extended):
    blocks_x = extended.shape[0] - 2
    upward = passed_along(extended[:, 2].astype(jnp.bfloat16), "gy", 1).astype(jnp.float32)
    downward = passed_along(extended[:, 0].astype(jnp.bfloat16), "gy", -1).astype(jnp.float32)
    middle = extended[:, 1] + upward + downward
    from_left = passed_along(middle[blocks_x + 1].astype(jnp.bfloat16), "gx", 1).astype(jnp.float32)
    from_right = passed_along(middle[0].astype(jnp.bfloat16), "gx", -1).astype(jnp.float32)
    centre = middle[1 : blocks_x + 1].at[0].add(from_left).at[blocks_x - 1].add(from_right)
    return centre[:, None]


def fold_motion(extended):
    blocks_x = extended.shape[0] - 2
    upward = passed_along(extended[:, 2], "gy", 1)
    downward = passed_along(extended[:, 0], "gy", -1)
    middle = extended[:, 1] + upward + downward
    from_left = passed_along(middle[blocks_x + 1], "gx", 1)
    from_right = passed_along(middle[0], "gx", -1)
    centre = middle[1 : blocks_x + 1].at[0].add(from_left).at[blocks_x - 1].add(from_right)
    return centre[:, None]


def local(
    positions,
    species,
    pair_codes,
    pair_count,
    embed_table,
    scalar_radial_one,
    vector_radial_one,
    scalar_radial_two,
    vector_radial_two,
    mixing_scalar_one,
    mixing_vector_one,
    mixing_two,
    readout,
):
    blocks_x = positions.shape[0]
    atoms_n = positions.shape[3]
    width = embed_table.shape[1]
    radial_count = scalar_radial_one.shape[0]
    species_count = embed_table.shape[0]
    packed = jnp.concatenate([positions, species.astype(jnp.float32)[:, :, None, :]], axis=2)
    extended = extended_2(packed, (("gx", 0), ("gy", 1)), 1)
    ext_positions = extended[:, :, :3]
    kinds = extended[:, :, 3]
    species_hot = (kinds[..., None] == jnp.arange(species_count, dtype=jnp.float32)).astype(
        jnp.bfloat16
    )
    initial = jnp.dot(species_hot, embed_table, preferred_element_type=jnp.float32).astype(
        jnp.bfloat16
    )
    listing = pair_codes[0, 0]
    pair_total = pair_count[0, 0]

    def locate(place):
        block_index, far_x, far_y, self_flag = decode(listing[place])
        return (
            block_index,
            ext_positions[block_index + 1, 1],
            ext_positions[far_x, far_y],
            far_x,
            far_y,
            self_flag,
        )

    def first_forward(place, totals):
        block_index, home_pos, other_pos, far_x, far_y, self_flag = locate(place)
        radial, direction = geometry(home_pos, other_pos, self_flag, radial_count)
        scalar_add, vector_add = layer_one(
            radial, direction, initial[far_x, far_y], scalar_radial_one, vector_radial_one
        )
        return (
            totals[0].at[block_index, 0].add(scalar_add),
            totals[1].at[block_index, 0].add(vector_add),
        )

    scalar_msg, vector_msg = lax.fori_loop(
        0,
        pair_total,
        first_forward,
        (
            jnp.zeros((blocks_x, 1, atoms_n, width), jnp.float32),
            jnp.zeros((blocks_x, 1, 3, atoms_n, width), jnp.float32),
        ),
    )
    own_initial = initial[1 : blocks_x + 1, 1:2]
    first_pre = jnp.dot(
        (scalar_msg * message_scale).astype(jnp.bfloat16),
        mixing_scalar_one,
        preferred_element_type=jnp.float32,
    )
    scalar_one = (own_initial.astype(jnp.float32) + jax.nn.silu(first_pre)).astype(jnp.bfloat16)
    vector_one = jnp.dot(
        (vector_msg * message_scale).astype(jnp.bfloat16),
        mixing_vector_one,
        preferred_element_type=jnp.float32,
    ).astype(jnp.bfloat16)
    features = jnp.concatenate([scalar_one[:, :, None], vector_one], axis=2)
    ext_features = extended_2(features, (("gx", 0), ("gy", 1)), 1)

    def second_forward(place, totals):
        block_index, home_pos, other_pos, far_x, far_y, self_flag = locate(place)
        radial, direction = geometry(home_pos, other_pos, self_flag, radial_count)
        return totals.at[block_index, 0].add(
            layer_two(
                radial, direction, ext_features[far_x, far_y], scalar_radial_two, vector_radial_two
            )
        )

    second_msg = lax.fori_loop(
        0, pair_total, second_forward, jnp.zeros((blocks_x, 1, atoms_n, width), jnp.float32)
    )
    second_pre = jnp.dot(
        (second_msg * message_scale).astype(jnp.bfloat16),
        mixing_two,
        preferred_element_type=jnp.float32,
    )
    atom_energy = jnp.sum(
        (scalar_one.astype(jnp.float32) + jax.nn.silu(second_pre)) * readout, axis=-1
    )
    second_slope = (readout * silu_slope(second_pre)).astype(jnp.bfloat16)
    second_in = (
        jnp.dot(second_slope, mixing_two.T, preferred_element_type=jnp.float32) * message_scale
    )

    def second_back_full(place, totals):
        block_index, home_pos, other_pos, far_x, far_y, self_flag = locate(place)
        home_grad, other_grad, feature_add = back_two(
            home_pos,
            other_pos,
            self_flag,
            ext_features[far_x, far_y],
            second_in[block_index, 0],
            scalar_radial_two,
            vector_radial_two,
        )
        position_grad = (
            totals[0].at[block_index + 1, 1].add(home_grad).at[far_x, far_y].add(other_grad)
        )
        return (position_grad, totals[1].at[far_x, far_y].add(feature_add))

    motion_zero = jnp.zeros((blocks_x + 2, 3, 3, atoms_n), jnp.float32)
    ext_motion, ext_feature_grad = lax.fori_loop(
        0,
        pair_total,
        second_back_full,
        (motion_zero, jnp.zeros((blocks_x + 2, 3, 4, atoms_n, width), jnp.float32)),
    )
    feature_grad = fold_features(ext_feature_grad)
    first_slope = (readout + feature_grad[:, :, 0]) * silu_slope(first_pre)
    first_in = (
        jnp.dot(
            first_slope.astype(jnp.bfloat16),
            mixing_scalar_one.T,
            preferred_element_type=jnp.float32,
        )
        * message_scale
    )
    vector_in = (
        jnp.dot(
            feature_grad[:, :, 1:].astype(jnp.bfloat16),
            mixing_vector_one.T,
            preferred_element_type=jnp.float32,
        )
        * message_scale
    )

    def first_back(place, totals):
        block_index, home_pos, other_pos, far_x, far_y, self_flag = locate(place)
        home_grad, other_grad = back_one(
            home_pos,
            other_pos,
            self_flag,
            initial[far_x, far_y],
            first_in[block_index, 0],
            vector_in[block_index, 0],
            scalar_radial_one,
            vector_radial_one,
        )
        return totals.at[block_index + 1, 1].add(home_grad).at[far_x, far_y].add(other_grad)

    early_motion = fold_motion(ext_motion)
    later_motion = lax.fori_loop(0, pair_total, first_back, jnp.zeros_like(ext_motion))
    motion_total = early_motion + fold_motion(later_motion)
    return (atom_energy, -motion_total)


def solution(mesh):
    in_specs = (
        P("gx", "gy", None, None),
        P("gx", "gy", None),
        P("gx", "gy", None),
        P("gx", "gy"),
        P(),
        P(),
        P(),
        P(),
        P(),
        P(),
        P(),
        P(),
        P(),
    )
    out_specs = (P("gx", "gy", None), P("gx", "gy", None, None))
    return jax.shard_map(local, mesh=mesh, in_specs=in_specs, out_specs=out_specs, check_vma=False)
```

profile of v0, /device:TPU:18, one launch (start us, length us, event | category | flops | bytes accessed | tf_op | source)
XLA Modules:
  0.0 1070.2 jit_solution(8167377666537616635)
XLA Ops:
  2.0 9.1 collective-permute-start.1
  11.1 1.9 collective-permute-start
  13.1 8.3 collective-permute-done
  21.4 1.9 collective-permute-start.3
  23.3 2.4 collective-permute-start.2
  25.8 5.3 collective-permute-done.2
  33.0 190.7 %while.70 = (s32[]{:T(128)}, f32[6,1,128,128]{3,2,1,0:T(8,128)S(1)}, f32[6,1,3,128,128]{4,3,2,1,0:T(8,128)S(1)}, s32[]{:T(128)}, s32[26]{0:T(128)S(1)}, /*index=...) while((s32[]{:T(128)}, ...), condition=%wide.region_6.7_spmd, body=%wide.region_0.6_spmd.sunk | while | flops 69189728 | bytes 2639179 | solution.py:221
  225.7 2.3 collective-permute-start.5
  228.0 7.5 collective-permute-start.4
  236.5 3.2 collective-permute-done.4
  239.8 1.9 collective-permute-start.7
  241.8 2.4 collective-permute-start.6
  244.2 19.4 %collective-permute-done.7 = bf16[8,1,4,128,128]{4,3,2,0,1:T(8,128)(2,1)} collective-permute-done((bf16[8,1,4,128,128]{4,3,2,0,1:T(8,128)(2,1)S(1)}, bf16[8,1,4,128,128]{4,3,2,0,1:T(8,128)(2,1)}, u32[]{:S(2)}, u32[]{:S(2)}) %collective-permute-start.7) | collective-permute-done | bytes 1048608 | tf_op jit(solution)/shard_map/ppermute | solution.py:26
  263.6 2.3 collective-permute-done.6
  265.9 1.8 pad_maximum_fusion
  267.6 2.1 copy.142
  269.8 187.5 %while.71 = (s32[]{:T(128)}, f32[6,1,128,128]{3,2,1,0:T(8,128)S(1)}, s32[]{:T(128)}, s32[26]{0:T(128)S(1)}, f32[4,128]{1,0:T(4,128)S(1)}, /*index=5*/f32[8,3,3,1...) while((s32[]{:T(128)}, ...), condition=%wide.region_11.12_spmd, body=%wide.region_7.11_spmd.sunk | while | flops 68878408 | bytes 2441997 | solution.py:254
  458.1 3.4 broadcast_in_dim.124.clone
  461.5 345.3 %while.72 = (s32[]{:T(128)}, f32[8,3,3,128]{3,2,1,0:T(4,128)S(1)}, f32[8,3,4,128,128]{3,4,2,0,1:T(8,128)}, s32[]{:T(128)}, s32[26]{0:T(128)S(1)}, /*index=5*/bf1...) while((s32[]{:T(128)}, f32[8,3,3,128]{3,2,1,0:T(4,128)S(1)}, ...), condition=%wide.region_25.26_spmd, body=%wide.region_13.25_spmd.sunk | while | flops 138904816 | bytes 9286557 | solution.py:287
  465.6 1.2 multiply_reduce_fusion.6
  518.7 1.2 multiply_reduce_fusion.6
  545.1 1.2 multiply_reduce_fusion.6
  598.2 1.2 multiply_reduce_fusion.6
  624.7 1.2 multiply_reduce_fusion.6
  651.2 1.2 multiply_reduce_fusion.6
  730.7 1.2 multiply_reduce_fusion.6
  770.5 1.2 multiply_reduce_fusion.6
  797.0 1.2 multiply_reduce_fusion.6
  806.8 3.5 convert.17
  810.3 1.5 slice_bitcast_fusion.1
  811.7 4.3 collective-permute-start.13
  816.1 1.9 collective-permute-start.12
  818.0 6.3 collective-permute-start.9
  824.4 1.9 collective-permute-start.8
  826.9 13.8 %collective-permute-done.9 = f32[8,3,128]{2,1,0:T(4,128)S(1)} collective-permute-done((f32[8,3,128]{2,1,0:T(4,128)S(1)}, f32[8,3,128]{2,1,0:T(4,128)S(1)}, u32[]{:S(2)}, u32[]{:S(2)}) %collective-permute-start.9) | collective-permute-done | bytes 12320 | tf_op jit(solution)/shard_map/ppermute | solution.py:15
  840.7 2.1 fusion.147
  842.8 6.7 collective-permute-start.14
  849.5 4.1 collective-permute-start.10
  853.6 6.6 collective-permute-start.11
  860.3 3.1 collective-permute-start.15
  863.6 8.1 collective-permute-done.15
  872.5 171.5 %while.73 = (s32[]{:T(128)}, f32[8,3,3,128]{3,2,1,0:T(4,128)S(1)}, s32[]{:T(128)}, s32[26]{0:T(128)S(1)}, f32[4,128]{1,0:T(4,128)S(1)}, /*index=5*/f32[6,1,3,128...) while((s32[]{:T(128)}, f32[8,3,3,128]{3,2,1,0:T(4,128)S(1)}, ...), condition=%wide.region_37.38_spmd, body=%wide.region_26.37_spmd.sunk | while | flops 70812904 | bytes 4299031 | solution.py:327
  1044.1 3.8 collective-permute-start.17
  1048.0 1.9 collective-permute-start.16
  1050.0 5.7 collective-permute-done.16
  1055.8 4.4 collective-permute-start.18
  1060.2 6.3 collective-permute-start.19
  1066.5 3.0 collective-permute-done.19
  (1984 shorter events, 613.4 us)
Async XLA Ops:
  0.6 224.8 %copy-start = (bf16[128,128]{1,0:T(8,128)(2,1)S(1)}, bf16[128,128]{1,0:T(8,128)(2,1)}, u32[]{:S(2)}) copy-start(bf16[128,128]{1,0:T(8,128)(2,1)} %param.59) | copy-start | bytes 98308
  2.0 11.0 %collective-permute-start.1 = (f32[1,1,4,128]{3,0,2,1:T(1,128)S(1)}, f32[1,1,4,128]{3,0,2,1:T(1,128)S(1)}, u32[]{:S(2)}, u32[]{:S(2)}) collective-permute-start(f32[1,1,4,128]{3,0,2,1:T(1,128)S(1)} %get-tuple-element.1131), channel_id=1, source_target_pairs={{32,0},{64,32},{96,64},{128,96},{160,128},{192,160},{224,192},{33,... | collective-permute-start | bytes 6152 | tf_op jit(solution)/shard_map/ppermute | solution.py:26
  11.1 10.3 collective-permute-start
  21.4 4.3 collective-permute-start.3
  23.3 7.8 collective-permute-start.2
  31.1 1.8 copy-start.6
  31.1 1.8 copy-start.7
  31.1 1.8 copy-start.12
  31.1 1.8 copy-start.14
  31.2 1.8 copy-start.16
  33.0 190.7 %copy-start.10 = (bf16[128,128]{1,0:T(8,128)(2,1)S(1)}, bf16[128,128]{1,0:T(8,128)(2,1)}, u32[]{:S(2)}) copy-start(bf16[128,128]{1,0:T(8,128)(2,1)} %param.58) | copy-start | bytes 98308
  224.7 0.7 copy-start.2
  225.7 10.8 %collective-permute-start.5 = (bf16[1,1,4,128,128]{4,3,2,0,1:T(8,128)(2,1)S(1)}, bf16[1,1,4,128,128]{4,3,2,0,1:T(8,128)(2,1)S(1)}, u32[]{:S(2)}, u32[]{:S(2)}) collective-permute-start(bf16[1,1,4,128,128]{4,3,2,0,1:T(8,128)(2,1)S(1)} %get-tuple-element.1121), channel_id=1, source_target_pairs={{32,0},{64,32},{96,64},{128,96},{160,128},{192,160},{224,192},{33,... | collective-permute-start | bytes 393224 | tf_op jit(solution)/shard_map/ppermute | solution.py:26
  228.0 11.7 %collective-permute-start.4 = (bf16[1,1,4,128,128]{4,3,2,0,1:T(8,128)(2,1)S(1)}, bf16[1,1,4,128,128]{4,3,2,0,1:T(8,128)(2,1)S(1)}, u32[]{:S(2)}, u32[]{:S(2)}) collective-permute-start(bf16[1,1,4,128,128]{4,3,2,0,1:T(8,128)(2,1)S(1)} %get-tuple-element.1120), channel_id=1, source_target_pairs={{0,32},{32,64},{64,96},{96,128},{128,160},{160,192},{192,224},{1,3... | collective-permute-start | bytes 393224 | tf_op jit(solution)/shard_map/ppermute | solution.py:25
  239.8 23.7 %collective-permute-start.7 = (bf16[8,1,4,128,128]{4,3,2,0,1:T(8,128)(2,1)S(1)}, bf16[8,1,4,128,128]{4,3,2,0,1:T(8,128)(2,1)}, u32[]{:S(2)}, u32[]{:S(2)}) collective-permute-start(bf16[8,1,4,128,128]{4,3,2,0,1:T(8,128)(2,1)S(1)} %pad_maximum_fusion.1), channel_id=1, source_target_pairs={{1,0},{2,1},{3,2},{4,3},{5,4},{6,5},{7,6},{8,7},{9,8},{10,9},{11,1... | collective-permute-start | bytes 3145736 | tf_op jit(solution)/shard_map/ppermute | solution.py:26
  241.8 24.1 %collective-permute-start.6 = (bf16[8,1,4,128,128]{4,3,2,0,1:T(8,128)(2,1)S(1)}, bf16[8,1,4,128,128]{4,3,2,0,1:T(8,128)(2,1)}, u32[]{:S(2)}, u32[]{:S(2)}) collective-permute-start(bf16[8,1,4,128,128]{4,3,2,0,1:T(8,128)(2,1)S(1)} %pad_maximum_fusion.1), channel_id=1, source_target_pairs={{0,1},{1,2},{2,3},{3,4},{4,5},{5,6},{6,7},{7,8},{8,9},{9,10},{10,1... | collective-permute-start | bytes 3145736 | tf_op jit(solution)/shard_map/ppermute | solution.py:25
  267.6 2.2 copy-start.1
  267.6 2.2 copy-start.11
  269.8 187.5 %copy-start.3 = (bf16[6,1,128,128]{2,3,1,0:T(8,128)(2,1)S(1)}, bf16[6,1,128,128]{2,3,1,0:T(8,128)(2,1)}, u32[]{:S(2)}) copy-start(bf16[6,1,128,128]{2,3,1,0:T(8,128)(2,1)} %copy-done.2) | copy-start | bytes 589828
  269.8 187.5 %copy-start.9 = (bf16[128,128]{1,0:T(8,128)(2,1)S(1)}, bf16[128,128]{1,0:T(8,128)(2,1)}, u32[]{:S(2)}) copy-start(bf16[128,128]{1,0:T(8,128)(2,1)} %param.60) | copy-start | bytes 98308
  269.8 187.5 %copy-start.13 = (f32[128]{0:T(128)S(1)}, f32[128]{0:T(128)}, u32[]{:S(2)}) copy-start(f32[128]{0:T(128)} %param.61) | copy-start | bytes 1540
  458.1 3.5 copy-start.8
  458.1 3.5 copy-start.15
  811.7 29.0 %collective-permute-start.13 = (bf16[8,4,128,128]{2,3,1,0:T(8,128)(2,1)}, bf16[8,4,128,128]{2,3,1,0:T(8,128)(2,1)S(1)}, u32[]{:S(2)}, u32[]{:S(2)}) collective-permute-start(bf16[8,4,128,128]{2,3,1,0:T(8,128)(2,1)} %get-tuple-element.1117), channel_id=1, source_target_pairs={{1,0},{2,1},{3,2},{4,3},{5,4},{6,5},{7,6},{8,7},{9,8},{10,9},{11,1... | collective-permute-start | bytes 3145736 | tf_op jit(solution)/shard_map/ppermute | solution.py:15
  816.1 24.6 %collective-permute-start.12 = (bf16[8,4,128,128]{2,3,1,0:T(8,128)(2,1)}, bf16[8,4,128,128]{2,3,1,0:T(8,128)(2,1)S(1)}, u32[]{:S(2)}, u32[]{:S(2)}) collective-permute-start(bf16[8,4,128,128]{2,3,1,0:T(8,128)(2,1)} %get-tuple-element.1116), channel_id=1, source_target_pairs={{0,1},{1,2},{2,3},{3,4},{4,5},{5,6},{6,7},{7,8},{8,9},{9,10},{10,1... | collective-permute-start | bytes 3145736 | tf_op jit(solution)/shard_map/ppermute | solution.py:15
  818.0 22.6 %collective-permute-start.9 = (f32[8,3,128]{2,1,0:T(4,128)S(1)}, f32[8,3,128]{2,1,0:T(4,128)S(1)}, u32[]{:S(2)}, u32[]{:S(2)}) collective-permute-start(f32[8,3,128]{2,1,0:T(4,128)S(1)} %get-tuple-element.1125), channel_id=1, source_target_pairs={{1,0},{2,1},{3,2},{4,3},{5,4},{6,5},{7,6},{8,7},{9,8},{10,9},{11,1... | collective-permute-start | bytes 36872 | tf_op jit(solution)/shard_map/ppermute | solution.py:15
  824.4 16.3 %collective-permute-start.8 = (f32[8,3,128]{2,1,0:T(4,128)S(1)}, f32[8,3,128]{2,1,0:T(4,128)S(1)}, u32[]{:S(2)}, u32[]{:S(2)}) collective-permute-start(f32[8,3,128]{2,1,0:T(4,128)S(1)} %get-tuple-element.1124), channel_id=1, source_target_pairs={{0,1},{1,2},{2,3},{3,4},{4,5},{5,6},{6,7},{7,8},{8,9},{9,10},{10,1... | collective-permute-start | bytes 36872 | tf_op jit(solution)/shard_map/ppermute | solution.py:15
  840.7 8.8 copy-start.4
  842.8 20.6 %collective-permute-start.14 = (bf16[4,128,128]{1,2,0:T(8,128)(2,1)S(1)}, bf16[4,128,128]{1,2,0:T(8,128)(2,1)S(1)}, u32[]{:S(2)}, u32[]{:S(2)}) collective-permute-start(bf16[4,128,128]{1,2,0:T(8,128)(2,1)S(1)} %get-tuple-element.1119), channel_id=1, source_target_pairs={{0,32},{32,64},{64,96},{96,128},{128,160},{160,192},{192,224},{1,3... | collective-permute-start | bytes 393224 | tf_op jit(solution)/shard_map/ppermute | solution.py:15
  849.5 200.4 %collective-permute-start.10 = (f32[3,128]{1,0:T(4,128)S(1)}, f32[3,128]{1,0:T(4,128)S(1)}, u32[]{:S(2)}, u32[]{:S(2)}) collective-permute-start(f32[3,128]{1,0:T(4,128)S(1)} %get-tuple-element.1129), channel_id=1, source_target_pairs={{0,32},{32,64},{64,96},{96,128},{128,160},{160,192},{192,224},{1,3... | collective-permute-start | bytes 4616 | tf_op jit(solution)/shard_map/ppermute | solution.py:15
  853.6 206.5 %collective-permute-start.11 = (f32[3,128]{1,0:T(4,128)S(1)}, f32[3,128]{1,0:T(4,128)S(1)}, u32[]{:S(2)}, u32[]{:S(2)}) collective-permute-start(f32[3,128]{1,0:T(4,128)S(1)} %get-tuple-element.1128), channel_id=1, source_target_pairs={{32,0},{64,32},{96,64},{128,96},{160,128},{192,160},{224,192},{33,... | collective-permute-start | bytes 4616 | tf_op jit(solution)/shard_map/ppermute | solution.py:15
  860.3 11.4 %collective-permute-start.15 = (bf16[4,128,128]{1,2,0:T(8,128)(2,1)S(1)}, bf16[4,128,128]{1,2,0:T(8,128)(2,1)S(1)}, u32[]{:S(2)}, u32[]{:S(2)}) collective-permute-start(bf16[4,128,128]{1,2,0:T(8,128)(2,1)S(1)} %get-tuple-element.1118), channel_id=1, source_target_pairs={{32,0},{64,32},{96,64},{128,96},{160,128},{192,160},{224,192},{33,... | collective-permute-start | bytes 393224 | tf_op jit(solution)/shard_map/ppermute | solution.py:15
  863.6 8.5 copy-start.17
  872.5 177.4 %copy-start.5 = (f32[8,3,128]{2,1,0:T(4,128)S(1)}, f32[8,3,128]{2,1,0:T(4,128)}, u32[]{:S(2)}) copy-start(f32[8,3,128]{2,1,0:T(4,128)} %copy-done.4) | copy-start | bytes 36868
  872.5 177.4 %slice-start = ((f32[8,3,128]{2,1,0:T(4,128)}), f32[6,3,128]{2,1,0:T(4,128)S(1)}, s32[]{:S(2)}) async-start(f32[8,3,128]{2,1,0:T(4,128)} %copy-done.4), calls=%async_computation | async-start | bytes 24576 | tf_op jit(solution)/shard_map/slice | solution.py:162
  1044.1 5.9 collective-permute-start.17
  1048.0 7.8 collective-permute-start.16
  1055.8 10.7 %collective-permute-start.18 = (f32[3,128]{1,0:T(4,128)S(1)}, f32[3,128]{1,0:T(4,128)S(1)}, u32[]{:S(2)}, u32[]{:S(2)}) collective-permute-start(f32[3,128]{1,0:T(4,128)S(1)} %get-tuple-element.1127), channel_id=1, source_target_pairs={{0,32},{32,64},{64,96},{96,128},{128,160},{160,192},{192,224},{1,3... | collective-permute-start | bytes 4616 | tf_op jit(solution)/shard_map/ppermute | solution.py:15
  1060.2 9.4 collective-permute-start.19
where the time goes:
time: 1080 us; the launch traced here: 1070 us
  other arithmetic  331 us (31%)
  loops' own time  280 us (26%)
  matrix products  162 us (15%)
  local copies, waits for them, and re-layouts  145 us (13%)
  starting transfers between devices  80.8 us (7%)
  waiting for transfers between devices  70.2 us (6%)
    another operation x184, other arithmetic  140 us
    another operation x1, loops' own time, local(): lax.fori_loop(0, pair_total, second_back_full, (motion_zero, jnp.zeros((b...  75.6 us
    another operation x1, loops' own time, local(): lax.fori_loop(0, pair_total, first_forward, (jnp.zeros((blocks_x, 1, atom...  72.5 us
    another operation x1, loops' own time, local(): lax.fori_loop(0, pair_total, first_back, jnp.zeros_like(ext_motion))  66.5 us
    another operation x1, loops' own time, local(): lax.fori_loop(0, pair_total, second_forward, jnp.zeros((blocks_x, 1, atom...  65.5 us
    dynamic_slice x104, local copies, waits for them, and re-layouts, locate(): block_index, far_x, far_y, self_flag = decode(listing[place])  60.7 us
    ppermute x12, starting transfers between devices, passed_along(): return lax.ppermute(block, axis, route)  51.3 us
    scatter-add x52, other arithmetic, second_back_full(): totals[0].at[block_index + 1, 1].add(home_grad).at[far_x, far_y]  35 us
  transfers between devices with their start and end apart: 20, of which 10 were waited for; matrix products, arithmetic and copies ran while one was open for 10% of the time, Pallas kernels for 0%

commit v1 on v0

v1 whole, which is shorter than its diff:
```python
import jax
import jax.numpy as jnp
from jax import lax
from jax.experimental import pallas as pl
from jax.experimental.pallas import tpu as pltpu
from jax.sharding import PartitionSpec as P

BX = 6
EX = 8
A = 128
C = 128
K = 4
ROWS = 32
F32 = jnp.float32
BF16 = jnp.bfloat16
SIGMA = 1.5
NT = (((1,), (1,)), ((), ()))

HOME_PAIRS = [
    (h, (o % 3) * EX + h + o // 3, EX + 1 + h, o) for h in range(BX) for o in range(9)
]
FAR_PAIRS = [
    (f, (2 - o % 3) * EX + f + 2 - o // 3, (2 - o % 3) * EX + f + 2 - o // 3, o)
    for f in range(BX)
    for o in range(9)
]


def dot(a, b):
    return jnp.dot(a, b, preferred_element_type=F32)


def dot_nt(a, b):
    return lax.dot_general(a, b, NT, preferred_element_type=F32)


def pack_kernel(pos_ref, species_ref, codes_ref, count_ref, out_ref):
    block_id = lax.broadcasted_iota(jnp.int32, (8, 128), 0)
    mask = jnp.zeros((8, 128), jnp.int32)
    for p in range(codes_ref.shape[1]):
        code = codes_ref[0, p]
        block = lax.shift_right_logical(code * 57, 9)
        bit = jnp.where(p < count_ref[0, 0], lax.shift_left(1, code - 9 * block), 0)
        mask = mask + jnp.where(block_id == block, bit, 0)
    mask = mask.astype(F32)
    for h in range(BX):
        out_ref[h, 0:3, :] = pos_ref[h]
        out_ref[h, 3:4, :] = species_ref[h : h + 1, :].astype(F32)
        out_ref[h, 4:5, :] = mask[h : h + 1, :]
        out_ref[h, 5:8, :] = jnp.zeros((3, 128), F32)


def gather_ext(lo_ref, mid_ref, hi_ref, ext_ref):
    for row, ref in enumerate((lo_ref, mid_ref, hi_ref)):
        for x in range(EX):
            ext_ref[row * EX + x] = ref[x]


def send_masks(ext_ref, maskv_ref, masks_ref, sem):
    for e in range(3 * EX):
        maskv_ref[e : e + 1, :] = ext_ref[e, 4:5, :].astype(jnp.int32)
    copy = pltpu.make_async_copy(maskv_ref, masks_ref, sem)
    copy.start()
    return copy


def make_list(pairs, masks_ref, list_ref):
    n = jnp.int32(0)
    for own, other, lister, o in pairs:
        list_ref[n] = own + other * 8 + (256 if o == 4 else 0)
        n = n + (lax.shift_right_logical(masks_ref[lister, 0], o) & 1)
    return n


def entry(list_ref, p):
    code = list_ref[p]
    own = code & 7
    other = lax.shift_right_logical(code, 3) & 31
    bias = jnp.where(code >= 256, 0, 1024)
    return own, other, bias


def columns(ext_ref, col_ref, blocks, parts):
    for i, e in enumerate(blocks):
        turned = ext_ref[e].T
        for d in range(parts):
            col_ref[i, d] = jnp.broadcast_to(turned[:, d : d + 1], (A, 128))


def embed_all(ext_ref, table_ref, init_ref, blocks):
    lanes = lax.broadcasted_iota(jnp.int32, (A, 128), 1).astype(F32)
    for e in blocks:
        kind = jnp.broadcast_to(ext_ref[e].T[:, 3:4], (A, 128))
        hot = (kind == lanes).astype(BF16)
        init_ref[e] = dot(hot, table_ref[...]).astype(BF16)


def geometry(col_ref, i, row, r, sign, bias, rows=ROWS):
    off = [sign * (row[d] - col_ref[i, d, pl.ds(r, rows), :]) for d in range(3)]
    squared = off[0] * off[0] + off[1] * off[1] + off[2] * off[2]
    soft = squared + 0.25
    inv = lax.rsqrt(soft)
    s = soft * inv
    taper = jnp.maximum(1.0 - squared * (1.0 / 36.0), 0.0)
    at = lax.broadcasted_iota(jnp.int32, (rows, 128), 0) + (r + bias)
    lane = lax.broadcasted_iota(jnp.int32, (rows, 128), 1)
    taper = jnp.where(at == lane, 0.0, taper)
    u = jnp.minimum(s, 6.25) * (1.0 / SIGMA) - 0.5
    base = taper * jnp.exp(-u * u)
    step = jnp.exp(2.0 * u - 1.0)
    q = [base]
    for k in range(1, K):
        q.append(q[-1] * (step * EXPS[k]))
    return off, inv, taper, u, q


EXPS = [1.0, 1.0, 0.1353352832366127, 0.01831563888873418]


def store_tiles(put, off, inv, taper, q):
    direction = [o * inv for o in off]
    for k in range(K):
        radial = taper * q[k]
        put(0, k, radial.astype(BF16))
        for d in range(3):
            put(1 + d, k, (radial * direction[d]).astype(BF16))


def pull_back(grads, off, inv, taper, u, q):
    direction = [o * inv for o in off]
    s0 = s1 = turn = None
    dg = [None] * 3
    for k in range(K):
        radial = taper * q[k]
        tilted = [grads(1 + d, k) for d in range(3)]
        along = tilted[0] * direction[0] + tilted[1] * direction[1] + tilted[2] * direction[2]
        p = (grads(0, k) + along) * q[k]
        w = along * radial
        s0 = p if s0 is None else s0 + p
        if k:
            s1 = p * float(k) if s1 is None else s1 + p * float(k)
        turn = w if turn is None else turn + w
        for d in range(3):
            v = tilted[d] * radial
            dg[d] = v if dg[d] is None else dg[d] + v
    bend = (2.0 / SIGMA) * taper * (u * s0 - s1) + turn * inv
    weight = -(s0 * (1.0 / 9.0)) - inv * bend
    return [dg[d] * inv + weight * off[d] for d in range(3)]


def rows_of(ext_ref, e):
    return [ext_ref[e, d : d + 1, :] for d in range(3)]


def scaled(feature, weights_ref, k):
    return (feature.astype(F32) * weights_ref[k : k + 1, :]).astype(BF16)


def forward_kernel(
    lo_ref, mid_ref, hi_ref, table_ref, ws1_ref, wv1_ref, ws2_ref, wv2_ref, ms_ref, mv_ref,
    pre_ref, feat_ref, out_lo_ref, out_mid_ref, out_hi_ref,
    ext_ref, col_ref, init_ref, scaled_s_ref, scaled_v_ref, acc_ref, tile_ref, wide_ref, ready_ref,
    total_ref, maskv_ref, masks_ref, list1_ref, list2_ref, sem,
):
    gather_ext(lo_ref, mid_ref, hi_ref, ext_ref)
    copy = send_masks(ext_ref, maskv_ref, masks_ref, sem)
    columns(ext_ref, col_ref, range(3 * EX), 3)
    embed_all(ext_ref, table_ref, init_ref, range(3 * EX))

    def scale_block(e, carry):
        for k in range(K):
            scaled_s_ref[e, pl.ds(k * A, A), :] = scaled(init_ref[e], ws1_ref, k)
            scaled_v_ref[e, pl.ds(k * A, A), :] = scaled(init_ref[e], wv1_ref, k)
        return carry

    lax.fori_loop(0, 3 * EX, scale_block, 0)
    acc_ref[...] = jnp.zeros_like(acc_ref)
    total_ref[...] = jnp.zeros_like(total_ref)
    copy.wait()
    n1 = make_list(HOME_PAIRS, masks_ref, list1_ref)
    n2 = make_list(FAR_PAIRS, masks_ref, list2_ref)

    def first(p, carry):
        own, other, bias = entry(list1_ref, p)
        row = rows_of(ext_ref, other)
        for r in range(0, A, ROWS):
            off, inv, taper, u, q = geometry(col_ref, own + EX + 1, row, r, 1.0, bias)

            def put(g, k, tile):
                tile_ref[pl.ds(g * A + r, ROWS), pl.ds(k * A, A)] = tile

            store_tiles(put, off, inv, taper, q)
        acc_ref[own, 0:A, :] += dot(tile_ref[0:A, :], scaled_s_ref[other])
        acc_ref[own, A : 4 * A, :] += dot(tile_ref[A : 4 * A, :], scaled_v_ref[other])
        return carry

    lax.fori_loop(0, n1, first, 0)

    def mix(h, carry):
        pre = dot((acc_ref[h, 0:A, :] * 0.125).astype(BF16), ms_ref[...])
        pre_ref[h] = pre
        scalar = (init_ref[h + EX + 1].astype(F32) + pre * jax.nn.sigmoid(pre)).astype(BF16)
        vector = dot((acc_ref[h, A : 4 * A, :] * 0.125).astype(BF16), mv_ref[...]).astype(BF16)
        feat_ref[h, 0:A, :] = scalar
        feat_ref[h, A : 4 * A, :] = vector
        for k in range(K):
            ready_ref[h, pl.ds(k * A, A), :] = scaled(scalar, ws2_ref, k)
            for d in range(3):
                ready_ref[h, pl.ds(((1 + d) * K + k) * A, A), :] = scaled(
                    vector[d * A : (d + 1) * A, :], wv2_ref, k
                )
        return carry

    lax.fori_loop(0, BX, mix, 0)

    def second(p, carry):
        own, other, bias = entry(list2_ref, p)
        row = rows_of(ext_ref, own + EX + 1)
        for r in range(0, A, ROWS):
            off, inv, taper, u, q = geometry(col_ref, other, row, r, 1.0, bias)

            def put(g, k, tile):
                wide_ref[pl.ds(r, ROWS), pl.ds((g * K + k) * A, A)] = tile

            store_tiles(put, off, inv, taper, q)
        total_ref[other] += dot(wide_ref[...], ready_ref[own])
        return carry

    lax.fori_loop(0, n2, second, 0)
    for x in range(EX):
        out_lo_ref[x] = total_ref[x].astype(BF16)
        out_mid_ref[x] = total_ref[EX + x]
        out_hi_ref[x] = total_ref[2 * EX + x].astype(BF16)


def slope_of(value):
    sigma = jax.nn.sigmoid(value)
    return sigma * (1.0 + value * (1.0 - sigma))


def middle_kernel(
    mid_ref, below_ref, above_ref, left_ref, right_ref, feat_ref, mix_ref, readout_ref,
    energy_ref, second_in_ref,
):
    for h in range(BX):
        msg = mid_ref[h + 1] + below_ref[h + 1].astype(F32) + above_ref[h + 1].astype(F32)
        if h == 0:
            msg = msg + left_ref[0].astype(F32)
        if h == BX - 1:
            msg = msg + right_ref[0].astype(F32)
        pre = dot((msg * 0.125).astype(BF16), mix_ref[...])
        sigma = jax.nn.sigmoid(pre)
        part = (feat_ref[h, 0:A, :].astype(F32) + pre * sigma) * readout_ref[...]
        energy_ref[h : h + 1, :] = jnp.sum(part.T, axis=0, keepdims=True)
        grad = (readout_ref[...] * (sigma * (1.0 + pre * (1.0 - sigma)))).astype(BF16)
        second_in_ref[h] = (dot_nt(grad, mix_ref[...]) * 0.125).astype(BF16)


def backward_kernel(
    lo_ref, mid_ref, hi_ref, in_lo_ref, in_mid_ref, in_hi_ref, feat_ref, pre_ref, table_ref,
    ws1_ref, wv1_ref, ws2_ref, wv2_ref, ms_ref, mv_ref, readout_ref,
    out_lo_ref, out_mid_ref, out_hi_ref,
    ext_ref, col_ref, init_ref, scaled_s_ref, scaled_v_ref, cot_s_ref, cot_v_ref, acc_ref, tile_ref,
    grad_ref, inward_ref, down_ref, across_ref, maskv_ref, masks_ref, list1_ref, list2_ref, sem,
):
    gather_ext(lo_ref, mid_ref, hi_ref, ext_ref)
    copy = send_masks(ext_ref, maskv_ref, masks_ref, sem)
    columns(ext_ref, col_ref, range(EX + 1, EX + 1 + BX), 3)
    embed_all(ext_ref, table_ref, init_ref, range(3 * EX))

    def scale_block(e, carry):
        for k in range(K):
            scaled_s_ref[e, pl.ds(k * A, A), :] = scaled(init_ref[e], ws1_ref, k)
            scaled_v_ref[e, pl.ds(k * A, A), :] = scaled(init_ref[e], wv1_ref, k)
        return carry

    lax.fori_loop(0, 3 * EX, scale_block, 0)
    for row, ref in enumerate((in_lo_ref, in_mid_ref, in_hi_ref)):

        def cot_block(x, carry, row=row, ref=ref):
            for k in range(K):
                cot_s_ref[row * EX + x, pl.ds(k * A, A), :] = scaled(ref[x], ws2_ref, k)
                cot_v_ref[row * EX + x, pl.ds(k * A, A), :] = scaled(ref[x], wv2_ref, k)
            return carry

        lax.fori_loop(0, EX, cot_block, 0)
    acc_ref[...] = jnp.zeros_like(acc_ref)
    down_ref[...] = jnp.zeros_like(down_ref)
    across_ref[...] = jnp.zeros_like(across_ref)
    copy.wait()
    n1 = make_list(HOME_PAIRS, masks_ref, list1_ref)
    n2 = make_list(FAR_PAIRS, masks_ref, list2_ref)

    def move(own, other, r, off, inv, taper, u, q, own_sign):
        def grads(g, k):
            return grad_ref[pl.ds(g * A + r, ROWS), pl.ds(k * A, A)]

        moved = pull_back(grads, off, inv, taper, u, q)
        for d in range(3):
            across_ref[own, d, pl.ds(r, ROWS), :] += own_sign * moved[d]
            part = moved[d][0:8]
            for i in range(8, ROWS, 8):
                part = part + moved[d][i : i + 8]
            down_ref[other, d] -= own_sign * part

    def second_back(p, carry):
        own, other, bias = entry(list2_ref, p)
        row = rows_of(ext_ref, other)
        grad_ref[0:A, :] = dot_nt(feat_ref[own, 0:A, :], cot_s_ref[other])
        grad_ref[A : 4 * A, :] = dot_nt(feat_ref[own, A : 4 * A, :], cot_v_ref[other])
        for r in range(0, A, ROWS):
            off, inv, taper, u, q = geometry(col_ref, own, row, r, -1.0, bias)

            def put(g, k, tile):
                tile_ref[pl.ds(g * A + r, ROWS), pl.ds(k * A, A)] = tile

            store_tiles(put, off, inv, taper, q)
            move(own, other, r, off, inv, taper, u, q, 1.0)
        acc_ref[own, 0:A, :] += dot(tile_ref[0:A, :], cot_s_ref[other])
        acc_ref[own, A : 4 * A, :] += dot(tile_ref[A : 4 * A, :], cot_v_ref[other])
        return carry

    lax.fori_loop(0, n2, second_back, 0)

    def inward(h, carry):
        slope = (readout_ref[...] + acc_ref[h, 0:A, :]) * slope_of(pre_ref[h])
        inward_ref[h, 0:A, :] = (dot_nt(slope.astype(BF16), ms_ref[...]) * 0.125).astype(BF16)
        inward_ref[h, A : 4 * A, :] = (
            dot_nt(acc_ref[h, A : 4 * A, :].astype(BF16), mv_ref[...]) * 0.125
        ).astype(BF16)
        return carry

    lax.fori_loop(0, BX, inward, 0)

    def first_back(p, carry):
        own, other, bias = entry(list1_ref, p)
        row = rows_of(ext_ref, other)
        grad_ref[0:A, :] = dot_nt(inward_ref[own, 0:A, :], scaled_s_ref[other])
        grad_ref[A : 4 * A, :] = dot_nt(inward_ref[own, A : 4 * A, :], scaled_v_ref[other])
        for r in range(0, A, ROWS):
            off, inv, taper, u, q = geometry(col_ref, own, row, r, 1.0, bias)
            move(own, other, r, off, inv, taper, u, q, -1.0)
        return carry

    lax.fori_loop(0, n1, first_back, 0)
    for row, ref in enumerate((out_lo_ref, out_mid_ref, out_hi_ref)):
        for x in range(EX):
            for d in range(3):
                line = jnp.sum(down_ref[row * EX + x, d], axis=0, keepdims=True)
                if row == 1 and 1 <= x <= BX:
                    line = line + jnp.sum(across_ref[x - 1, d].T, axis=0, keepdims=True)
                ref[x, d : d + 1, :] = line


VMEM = pl.BlockSpec(memory_space=pltpu.VMEM)
SMEM = pl.BlockSpec(memory_space=pltpu.SMEM)
PARAMS = pltpu.CompilerParams(vmem_limit_bytes=56 * 1024 * 1024)


def call(kernel, args, outs, scratch=(), in_specs=None):
    return pl.pallas_call(
        kernel,
        out_shape=[jax.ShapeDtypeStruct(s, d) for s, d in outs],
        in_specs=in_specs or [VMEM] * len(args),
        out_specs=[VMEM] * len(outs),
        scratch_shapes=list(scratch),
        compiler_params=PARAMS,
    )(*args)


def along(block, axis, step):
    size = lax.axis_size(axis)
    return lax.ppermute(block, axis, [(i, i + step) for i in range(size) if 0 <= i + step < size])


def halo(own):
    left = along(own[BX - 1 : BX], "gx", 1)
    right = along(own[0:1], "gx", -1)
    mid = jnp.concatenate([left, own, right], axis=0)
    return along(mid, "gy", 1), mid, along(mid, "gy", -1)


def fold(lo, mid, hi, dtype):
    above = along(lo, "gy", -1)
    below = along(hi, "gy", 1)
    edge = lambda x: (mid[x : x + 1] + below[x : x + 1] + above[x : x + 1]).astype(dtype)
    right = along(edge(0), "gx", -1)
    left = along(edge(EX - 1), "gx", 1)
    return mid, below, above, left, right


E = 3 * EX


def local(
    positions, species, pair_codes, pair_count, embed_table, ws1, wv1, ws2, wv2, ms, mv, m2, readout
):
    (packed,) = call(
        pack_kernel,
        (positions.reshape(BX, 3, A), species.reshape(BX, A), pair_codes.reshape(1, -1), pair_count),
        [((BX, 8, A), F32)],
        in_specs=[VMEM, VMEM, SMEM, SMEM],
    )
    ext = halo(packed)
    table = jnp.pad(embed_table, ((0, 128 - embed_table.shape[0]), (0, 0)))
    readout = readout.reshape(1, C)
    lists = [
        pltpu.VMEM((E, 128), jnp.int32),
        pltpu.SMEM((E, 128), jnp.int32),
        pltpu.SMEM((64,), jnp.int32),
        pltpu.SMEM((64,), jnp.int32),
        pltpu.SemaphoreType.DMA,
    ]
    pre, feat, lo, mid, hi = call(
        forward_kernel,
        (*ext, table, ws1, wv1, ws2, wv2, ms, mv),
        [
            ((BX, A, C), F32),
            ((BX, 4 * A, C), BF16),
            ((EX, A, C), BF16),
            ((EX, A, C), F32),
            ((EX, A, C), BF16),
        ],
        [
            pltpu.VMEM((E, 8, A), F32),
            pltpu.VMEM((E, 3, A, 128), F32),
            pltpu.VMEM((E, A, C), BF16),
            pltpu.VMEM((E, K * A, C), BF16),
            pltpu.VMEM((E, K * A, C), BF16),
            pltpu.VMEM((BX, 4 * A, C), F32),
            pltpu.VMEM((4 * A, K * A), BF16),
            pltpu.VMEM((A, 4 * K * A), BF16),
            pltpu.VMEM((BX, 4 * K * A, C), BF16),
            pltpu.VMEM((E, A, C), F32),
            *lists,
        ],
    )
    energy, second_in = call(
        middle_kernel,
        (*fold(lo, mid, hi, BF16), feat, m2, readout),
        [((BX, A), F32), ((BX, A, C), BF16)],
    )
    inner = halo(second_in)
    lo, mid, hi = call(
        backward_kernel,
        (*ext, *inner, feat, pre, table, ws1, wv1, ws2, wv2, ms, mv, readout),
        [((EX, 3, A), F32)] * 3,
        [
            pltpu.VMEM((E, 8, A), F32),
            pltpu.VMEM((BX, 3, A, 128), F32),
            pltpu.VMEM((E, A, C), BF16),
            pltpu.VMEM((E, K * A, C), BF16),
            pltpu.VMEM((E, K * A, C), BF16),
            pltpu.VMEM((E, K * A, C), BF16),
            pltpu.VMEM((E, K * A, C), BF16),
            pltpu.VMEM((BX, 4 * A, C), F32),
            pltpu.VMEM((4 * A, K * A), BF16),
            pltpu.VMEM((4 * A, K * A), F32),
            pltpu.VMEM((BX, 4 * A, C), BF16),
            pltpu.VMEM((E, 3, 8, A), F32),
            pltpu.VMEM((BX, 3, A, 128), F32),
            *lists,
        ],
    )
    mid, below, above, left, right = fold(lo, mid, hi, F32)
    total = mid[1 : BX + 1] + below[1 : BX + 1] + above[1 : BX + 1]
    total = total + jnp.concatenate([left, jnp.zeros((BX - 2, 3, A), F32), right], axis=0)
    return energy.reshape(BX, 1, A), -total.reshape(BX, 1, 3, A)


def solution(mesh):
    in_specs = (
        P("gx", "gy", None, None),
        P("gx", "gy", None),
        P("gx", "gy", None),
        P("gx", "gy"),
        *[P()] * 9,
    )
    out_specs = (P("gx", "gy", None), P("gx", "gy", None, None))
    return jax.shard_map(local, mesh=mesh, in_specs=in_specs, out_specs=out_specs, check_vma=False)
```

time: 1080 us -> 190 us (0.18)
  other arithmetic: 331 us -> 2.56 us
  loops' own time: 280 us -> 0 us
  matrix products: 162 us -> 0 us
  local copies, waits for them, and re-layouts: 145 us -> 7.35 us
  Pallas kernels: 0 us -> 67 us
  waiting for transfers between devices: 70.2 us -> 30.8 us
    another operation x4 -> x0, loops' own time: 280 us -> none  [the longest x1 75.6 us: local(): lax.fori_loop(0, pair_total, second_back_full, (motion_zero, jnp.zeros((b...]
    dot_general x267 -> x0, matrix products: 162 us -> none  [the longest x26 31.4 us: back_two(): jnp.einsum('kac,dbc->kdab', tensor_cot, source[1:], preferred_element_typ...]
    another operation x184 -> x0, other arithmetic: 140 us -> none
    scatter-add x188 -> x0, other arithmetic: 123 us -> none  [the longest x52 35 us: second_back_full(): totals[0].at[block_index + 1, 1].add(home_grad).at[far_x, far_y]]
    pallas_call x0 -> x4, Pallas kernels: none -> 67 us  [call(): pl.pallas_call(kernel, out_shape=[jax.ShapeDtypeStruct(s, d) for s, d in...]
    dynamic_slice x104 -> x0, local copies, waits for them, and re-layouts: 60.7 us -> none  [locate(): block_index, far_x, far_y, self_flag = decode(listing[place])]
    ppermute x20 -> x16, waiting for transfers between devices: 70.2 us -> 30.8 us  [along(): lax.ppermute(block, axis, [(i, i + step) for i in range(size) if 0 <= i +...]
    another operation x110 -> x0, local copies, waits for them, and re-layouts: 33.3 us -> none
  transfers between devices with their start and end apart: 20 -> 16, of which waited for: 10 -> 10; matrix products, arithmetic and copies ran while one was open for 10% -> 1% of each run, Pallas kernels for 0% -> 0%
where the time goes in v1:
time: 190 us; the launch traced here: 187 us
  starting transfers between devices  77.6 us (41%)
  Pallas kernels  67 us (35%)
  waiting for transfers between devices  30.8 us (16%)
  local copies, waits for them, and re-layouts  7.35 us (4%)
  other arithmetic  2.56 us (1%)
    ppermute x16, starting transfers between devices, along(): lax.ppermute(block, axis, [(i, i + step) for i in range(size) if 0 <= i +...  77.6 us
    pallas_call x4, Pallas kernels, call(): pl.pallas_call(kernel, out_shape=[jax.ShapeDtypeStruct(s, d) for s, d in...  67 us
    ppermute x16, waiting for transfers between devices, along(): lax.ppermute(block, axis, [(i, i + step) for i in range(size) if 0 <= i +...  30.8 us
    unnamed x36, local copies, waits for them, and re-layouts  5.13 us
  transfers between devices with their start and end apart: 16, of which 10 were waited for; matrix products, arithmetic and copies ran while one was open for 1% of the time, Pallas kernels for 0%

profile of v1, /device:TPU:18, one launch (start us, length us, event | category | flops | bytes accessed | tf_op | source)
XLA Modules:
  0.0 186.8 jit_solution(9785653143912567314)
XLA Ops:
  0.6 1.3 copy.21
  1.9 0.6 copy.22
  3.2 1.5 shard_map.140
  4.7 0.7 fusion.4
  5.3 9.1 %collective-permute-start = (f32[1,8,128]{2,1,0:T(8,128)S(1)}, f32[1,8,128]{2,1,0:T(8,128)S(1)}, u32[]{:S(2)}, u32[]{:S(2)}) collective-permute-start(f32[1,8,128]{2,1,0:T(8,128)S(1)} %get-tuple-element.30), channel_id=1, source_target_pairs={{0,32},{32,64},{64,96},{96,128},{128,160},{160,192},{192,224},{1,3... | collective-permute-start | bytes 12296 | tf_op jit(solution)/shard_map/ppermute | solution.py:373
  14.4 0.0 copy-start.11
  14.4 1.9 %collective-permute-start.1 = (f32[1,8,128]{2,1,0:T(8,128)S(1)}, f32[1,8,128]{2,1,0:T(8,128)S(1)}, u32[]{:S(2)}, u32[]{:S(2)}) collective-permute-start(f32[1,8,128]{2,1,0:T(8,128)S(1)} %get-tuple-element.31), channel_id=1, source_target_pairs={{32,0},{64,32},{96,64},{128,96},{160,128},{192,160},{224,192},{33,... | collective-permute-start | bytes 12296 | tf_op jit(solution)/shard_map/ppermute | solution.py:373
  16.4 7.5 %collective-permute-done.1 = f32[1,8,128]{2,1,0:T(8,128)S(1)} collective-permute-done((f32[1,8,128]{2,1,0:T(8,128)S(1)}, f32[1,8,128]{2,1,0:T(8,128)S(1)}, u32[]{:S(2)}, u32[]{:S(2)}) %collective-permute-start.1) | collective-permute-done | bytes 4128 | tf_op jit(solution)/shard_map/ppermute | solution.py:373
  23.9 0.7 pad_maximum_fusion.mid_ref
  24.6 1.9 %collective-permute-start.2 = (f32[8,8,128]{2,1,0:T(8,128)S(1)}, f32[8,8,128]{2,1,0:T(8,128)S(1)}, u32[]{:S(2)}, u32[]{:S(2)}) collective-permute-start(f32[8,8,128]{2,1,0:T(8,128)S(1)} %pad_maximum_fusion.mid_ref), channel_id=1, source_target_pairs={{0,1},{1,2},{2,3},{3,4},{4,5},{5,6},{6,7},{7,8},{8,9},{9,10},{10,1... | collective-permute-start | bytes 98312 | tf_op jit(solution)/shard_map/ppermute | solution.py:373
  26.6 6.3 %collective-permute-start.3 = (f32[8,8,128]{2,1,0:T(8,128)S(1)}, f32[8,8,128]{2,1,0:T(8,128)S(1)}, u32[]{:S(2)}, u32[]{:S(2)}) collective-permute-start(f32[8,8,128]{2,1,0:T(8,128)S(1)} %pad_maximum_fusion.mid_ref), channel_id=1, source_target_pairs={{1,0},{2,1},{3,2},{4,3},{5,4},{6,5},{7,6},{8,7},{9,8},{10,9},{11,1... | collective-permute-start | bytes 98312 | tf_op jit(solution)/shard_map/ppermute | solution.py:373
  32.9 0.6 pad.4.table_ref
  33.5 1.0 collective-permute-done.3.hi_ref
  34.5 0.6 copy-done.8
  35.1 27.3 %shard_map.141 = (f32[6,128,128]{2,1,0:T(8,128)}, bf16[6,512,128]{2,1,0:T(8,128)(2,1)}, bf16[8,128,128]{2,1,0:T(8,128)(2,1)}, f32[8,128,128]{2,1,0:T(8,128)}, bf16[8,128,128]{2,1,0:T(8,128)(2,1)}) custom-call(f32[8,8,128]{2,1,0:T(8,128)} %copy-done.7, f32[8,8,128]{2,1,0:T(8,128)} %copy-done.4, f32[8,8,128]{2,1,0:T(8,128)} %copy-done.8, ...), custom_call_target="tpu_custom_call" | custom-call | tf_op jit(solution)/shard_map/pallas_call | solution.py:361
  62.4 1.9 %collective-permute-start.4 = (bf16[8,128,128]{2,1,0:T(8,128)(2,1)}, bf16[8,128,128]{2,1,0:T(8,128)(2,1)S(1)}, u32[]{:S(2)}, u32[]{:S(2)}) collective-permute-start(bf16[8,128,128]{2,1,0:T(8,128)(2,1)} %get-tuple-element.13), channel_id=1, source_target_pairs={{0,1},{1,2},{2,3},{3,4},{4,5},{5,6},{6,7},{7,8},{8,9},{9,10},{10,1... | collective-permute-start | bytes 786440 | tf_op jit(solution)/shard_map/ppermute | solution.py:373
  64.3 7.1 %collective-permute-start.5 = (bf16[8,128,128]{2,1,0:T(8,128)(2,1)}, bf16[8,128,128]{2,1,0:T(8,128)(2,1)S(1)}, u32[]{:S(2)}, u32[]{:S(2)}) collective-permute-start(bf16[8,128,128]{2,1,0:T(8,128)(2,1)} %get-tuple-element.14), channel_id=1, source_target_pairs={{1,0},{2,1},{3,2},{4,3},{5,4},{6,5},{7,6},{8,7},{9,8},{10,9},{11,1... | collective-permute-start | bytes 786440 | tf_op jit(solution)/shard_map/ppermute | solution.py:373
  71.5 2.5 %collective-permute-done.4.below_ref = bf16[8,128,128]{2,1,0:T(8,128)(2,1)S(1)} collective-permute-done((bf16[8,128,128]{2,1,0:T(8,128)(2,1)}, bf16[8,128,128]{2,1,0:T(8,128)(2,1)S(1)}, u32[]{:S(2)}, u32[]{:S(2)}) %collective-permute-start.4) | collective-permute-done | bytes 262176 | tf_op jit(solution)/shard_map/ppermute | solution.py:373
  73.9 1.8 collective-permute-done.5.above_ref
  75.8 1.0 add_convert_fusion
  76.7 2.3 %collective-permute-start.6 = (bf16[1,128,128]{2,1,0:T(8,128)(2,1)S(1)}, bf16[1,128,128]{2,1,0:T(8,128)(2,1)S(1)}, u32[]{:S(2)}, u32[]{:S(2)}) collective-permute-start(bf16[1,128,128]{2,1,0:T(8,128)(2,1)S(1)} %get-tuple-element.25), channel_id=1, source_target_pairs={{0,32},{32,64},{64,96},{96,128},{128,160},{160,192},{192,224},{1,3... | collective-permute-start | bytes 98312 | tf_op jit(solution)/shard_map/ppermute | solution.py:373
  79.0 8.4 %collective-permute-start.7 = (bf16[1,128,128]{2,1,0:T(8,128)(2,1)S(1)}, bf16[1,128,128]{2,1,0:T(8,128)(2,1)S(1)}, u32[]{:S(2)}, u32[]{:S(2)}) collective-permute-start(bf16[1,128,128]{2,1,0:T(8,128)(2,1)S(1)} %get-tuple-element.24), channel_id=1, source_target_pairs={{32,0},{64,32},{96,64},{128,96},{160,128},{192,160},{224,192},{33,... | collective-permute-start | bytes 98312 | tf_op jit(solution)/shard_map/ppermute | solution.py:373
  87.4 2.5 %collective-permute-done.7.right_ref = bf16[1,128,128]{2,1,0:T(8,128)(2,1)S(1)} collective-permute-done((bf16[1,128,128]{2,1,0:T(8,128)(2,1)S(1)}, bf16[1,128,128]{2,1,0:T(8,128)(2,1)S(1)}, u32[]{:S(2)}, u32[]{:S(2)}) %collective-permute-start.7) | collective-permute-done | bytes 32800 | tf_op jit(solution)/shard_map/ppermute | solution.py:373
  90.0 0.6 copy-done.10
  90.6 2.8 %shard_map.142 = (f32[6,128]{1,0:T(8,128)}, bf16[6,128,128]{2,1,0:T(8,128)(2,1)}) custom-call(f32[8,128,128]{2,1,0:T(8,128)} %get-tuple-element.12.mid_ref, bf16[8,128,128]{2,1,0:T(8,128)(2,1)} %copy-done, bf16[8,128,128]{2,1,0:T(8,128)(2,1)} %copy-done.1, bf16[1,128,128]{2,1,0:T(8,128)(2,1)} %copy-done.9, bf16[1,128,128]{2,1,0:T(8,128)(2,1)} %copy-done.10, ...), custom_call_target="tpu_custom_call" | custom-call | tf_op jit(solution)/shard_map/pallas_call | solution.py:361
  93.4 0.8 fusion.3
  94.2 8.4 %collective-permute-start.8 = (bf16[1,128,128]{2,1,0:T(8,128)(2,1)S(1)}, bf16[1,128,128]{2,1,0:T(8,128)(2,1)S(1)}, u32[]{:S(2)}, u32[]{:S(2)}) collective-permute-start(bf16[1,128,128]{2,1,0:T(8,128)(2,1)S(1)} %get-tuple-element.27), channel_id=1, source_target_pairs={{0,32},{32,64},{64,96},{96,128},{128,160},{160,192},{192,224},{1,3... | collective-permute-start | bytes 98312 | tf_op jit(solution)/shard_map/ppermute | solution.py:373
  102.6 2.3 %collective-permute-start.9 = (bf16[1,128,128]{2,1,0:T(8,128)(2,1)S(1)}, bf16[1,128,128]{2,1,0:T(8,128)(2,1)S(1)}, u32[]{:S(2)}, u32[]{:S(2)}) collective-permute-start(bf16[1,128,128]{2,1,0:T(8,128)(2,1)S(1)} %get-tuple-element.26), channel_id=1, source_target_pairs={{32,0},{64,32},{96,64},{128,96},{160,128},{192,160},{224,192},{33,... | collective-permute-start | bytes 98312 | tf_op jit(solution)/shard_map/ppermute | solution.py:373
  104.9 0.1 collective-permute-done.8
  105.0 7.5 %collective-permute-done.9 = bf16[1,128,128]{2,1,0:T(8,128)(2,1)S(1)} collective-permute-done((bf16[1,128,128]{2,1,0:T(8,128)(2,1)S(1)}, bf16[1,128,128]{2,1,0:T(8,128)(2,1)S(1)}, u32[]{:S(2)}, u32[]{:S(2)}) %collective-permute-start.9) | collective-permute-done | bytes 32800 | tf_op jit(solution)/shard_map/ppermute | solution.py:373
  112.4 1.9 %collective-permute-start.10 = (bf16[8,128,128]{2,1,0:T(8,128)(2,1)S(1)}, bf16[8,128,128]{2,1,0:T(8,128)(2,1)S(1)}, u32[]{:S(2)}, u32[]{:S(2)}) collective-permute-start(bf16[8,128,128]{2,1,0:T(8,128)(2,1)S(1)} %constant_dynamic-update-slice_fusion.in_mid_ref), channel_id=1, source_target_pairs={{0,1},{1,2},{2,3},{3,4},{4,5},{5,6},{6,7},{7,8},{8,9},{9,10},{10,1... | collective-permute-start | bytes 786440 | tf_op jit(solution)/shard_map/ppermute | solution.py:373
  114.4 6.3 %collective-permute-start.11 = (bf16[8,128,128]{2,1,0:T(8,128)(2,1)S(1)}, bf16[8,128,128]{2,1,0:T(8,128)(2,1)S(1)}, u32[]{:S(2)}, u32[]{:S(2)}) collective-permute-start(bf16[8,128,128]{2,1,0:T(8,128)(2,1)S(1)} %constant_dynamic-update-slice_fusion.in_mid_ref), channel_id=1, source_target_pairs={{1,0},{2,1},{3,2},{4,3},{5,4},{6,5},{7,6},{8,7},{9,8},{10,9},{11,1... | collective-permute-start | bytes 786440 | tf_op jit(solution)/shard_map/ppermute | solution.py:373
  120.7 4.5 %collective-permute-done.10.in_lo_ref = bf16[8,128,128]{2,1,0:T(8,128)(2,1)S(1)} collective-permute-done((bf16[8,128,128]{2,1,0:T(8,128)(2,1)S(1)}, bf16[8,128,128]{2,1,0:T(8,128)(2,1)S(1)}, u32[]{:S(2)}, u32[]{:S(2)}) %collective-permute-start.10) | collective-permute-done | bytes 262176 | tf_op jit(solution)/shard_map/ppermute | solution.py:373
  125.2 0.7 copy-done.5
  125.9 0.1 copy-done.6
  126.0 35.4 %shard_map.143 = (f32[8,3,128]{2,1,0:T(4,128)}, f32[8,3,128]{2,1,0:T(4,128)}, f32[8,3,128]{2,1,0:T(4,128)}) custom-call(f32[8,8,128]{2,1,0:T(8,128)} %copy-done.7, f32[8,8,128]{2,1,0:T(8,128)} %copy-done.4, f32[8,8,128]{2,1,0:T(8,128)} %copy-done.8, bf16[8,128,128]{2,1,0:T(8,128)(2,1)} %copy-done.5, bf16[8,128,128]{2,1,0:T(8,128)(2,1)} %copy-done.3, ...), custom_call_target="tpu_custom_call" | custom-call | tf_op jit(solution)/shard_map/pallas_call | solution.py:361
  161.4 1.9 %collective-permute-start.12 = (f32[8,3,128]{2,1,0:T(4,128)}, f32[8,3,128]{2,1,0:T(4,128)S(1)}, u32[]{:S(2)}, u32[]{:S(2)}) collective-permute-start(f32[8,3,128]{2,1,0:T(4,128)} %get-tuple-element.20), channel_id=1, source_target_pairs={{0,1},{1,2},{2,3},{3,4},{4,5},{5,6},{6,7},{7,8},{8,9},{9,10},{10,1... | collective-permute-start | bytes 36872 | tf_op jit(solution)/shard_map/ppermute | solution.py:373
  163.3 7.2 %collective-permute-start.13 = (f32[8,3,128]{2,1,0:T(4,128)}, f32[8,3,128]{2,1,0:T(4,128)S(1)}, u32[]{:S(2)}, u32[]{:S(2)}) collective-permute-start(f32[8,3,128]{2,1,0:T(4,128)} %get-tuple-element.21), channel_id=1, source_target_pairs={{1,0},{2,1},{3,2},{4,3},{5,4},{6,5},{7,6},{8,7},{9,8},{10,9},{11,1... | collective-permute-start | bytes 36872 | tf_op jit(solution)/shard_map/ppermute | solution.py:373
  170.5 1.6 collective-permute-done.13
  172.2 0.8 slice_add_fusion.4
  172.9 1.9 %collective-permute-start.14 = (f32[1,3,128]{2,1,0:T(4,128)S(1)}, f32[1,3,128]{2,1,0:T(4,128)S(1)}, u32[]{:S(2)}, u32[]{:S(2)}) collective-permute-start(f32[1,3,128]{2,1,0:T(4,128)S(1)} %get-tuple-element.28), channel_id=1, source_target_pairs={{0,32},{32,64},{64,96},{96,128},{128,160},{160,192},{192,224},{1,3... | collective-permute-start | bytes 4616 | tf_op jit(solution)/shard_map/ppermute | solution.py:373
  174.8 0.0 copy-start.13
  174.8 8.7 %collective-permute-start.15 = (f32[1,3,128]{2,1,0:T(4,128)S(1)}, f32[1,3,128]{2,1,0:T(4,128)S(1)}, u32[]{:S(2)}, u32[]{:S(2)}) collective-permute-start(f32[1,3,128]{2,1,0:T(4,128)S(1)} %get-tuple-element.29), channel_id=1, source_target_pairs={{32,0},{64,32},{96,64},{128,96},{160,128},{192,160},{224,192},{33,... | collective-permute-start | bytes 4616 | tf_op jit(solution)/shard_map/ppermute | solution.py:373
  183.6 0.1 pad.6.clone
  183.7 0.6 copy.15
  184.2 1.9 collective-permute-done.15
  186.1 0.1 fusion.2
  186.2 0.6 copy.16
  (34 shorter events, 0.1 us)
Async XLA Ops:
  0.6 1.3 copy-start.14
  5.3 11.0 %collective-permute-start = (f32[1,8,128]{2,1,0:T(8,128)S(1)}, f32[1,8,128]{2,1,0:T(8,128)S(1)}, u32[]{:S(2)}, u32[]{:S(2)}) collective-permute-start(f32[1,8,128]{2,1,0:T(8,128)S(1)} %get-tuple-element.30), channel_id=1, source_target_pairs={{0,32},{32,64},{64,96},{96,128},{128,160},{160,192},{192,224},{1,3... | collective-permute-start | bytes 12296 | tf_op jit(solution)/shard_map/ppermute | solution.py:373
  14.4 18.5 %copy-start.11 = (bf16[89,128]{1,0:T(8,128)(2,1)S(1)}, bf16[89,128]{1,0:T(8,128)(2,1)}, u32[]{:S(2)}) copy-start(bf16[89,128]{1,0:T(8,128)(2,1)} %param.17) | copy-start | bytes 68356
  14.4 9.4 %collective-permute-start.1 = (f32[1,8,128]{2,1,0:T(8,128)S(1)}, f32[1,8,128]{2,1,0:T(8,128)S(1)}, u32[]{:S(2)}, u32[]{:S(2)}) collective-permute-start(f32[1,8,128]{2,1,0:T(8,128)S(1)} %get-tuple-element.31), channel_id=1, source_target_pairs={{32,0},{64,32},{96,64},{128,96},{160,128},{192,160},{224,192},{33,... | collective-permute-start | bytes 12296 | tf_op jit(solution)/shard_map/ppermute | solution.py:373
  24.6 9.8 %copy-start.4 = (f32[8,8,128]{2,1,0:T(8,128)}, f32[8,8,128]{2,1,0:T(8,128)S(1)}, u32[]{:S(2)}) copy-start(f32[8,8,128]{2,1,0:T(8,128)S(1)} %pad_maximum_fusion.mid_ref) | copy-start | bytes 98308
  24.6 8.9 %collective-permute-start.2 = (f32[8,8,128]{2,1,0:T(8,128)S(1)}, f32[8,8,128]{2,1,0:T(8,128)S(1)}, u32[]{:S(2)}, u32[]{:S(2)}) collective-permute-start(f32[8,8,128]{2,1,0:T(8,128)S(1)} %pad_maximum_fusion.mid_ref), channel_id=1, source_target_pairs={{0,1},{1,2},{2,3},{3,4},{4,5},{5,6},{6,7},{7,8},{8,9},{9,10},{10,1... | collective-permute-start | bytes 98312 | tf_op jit(solution)/shard_map/ppermute | solution.py:373
  26.6 7.9 %collective-permute-start.3 = (f32[8,8,128]{2,1,0:T(8,128)S(1)}, f32[8,8,128]{2,1,0:T(8,128)S(1)}, u32[]{:S(2)}, u32[]{:S(2)}) collective-permute-start(f32[8,8,128]{2,1,0:T(8,128)S(1)} %pad_maximum_fusion.mid_ref), channel_id=1, source_target_pairs={{1,0},{2,1},{3,2},{4,3},{5,4},{6,5},{7,6},{8,7},{9,8},{10,9},{11,1... | collective-permute-start | bytes 98312 | tf_op jit(solution)/shard_map/ppermute | solution.py:373
  33.5 1.0 copy-start.7
  34.5 0.6 copy-start.8
  62.4 11.5 %collective-permute-start.4 = (bf16[8,128,128]{2,1,0:T(8,128)(2,1)}, bf16[8,128,128]{2,1,0:T(8,128)(2,1)S(1)}, u32[]{:S(2)}, u32[]{:S(2)}) collective-permute-start(bf16[8,128,128]{2,1,0:T(8,128)(2,1)} %get-tuple-element.13), channel_id=1, source_target_pairs={{0,1},{1,2},{2,3},{3,4},{4,5},{5,6},{6,7},{7,8},{8,9},{9,10},{10,1... | collective-permute-start | bytes 786440 | tf_op jit(solution)/shard_map/ppermute | solution.py:373
  64.3 11.4 %collective-permute-start.5 = (bf16[8,128,128]{2,1,0:T(8,128)(2,1)}, bf16[8,128,128]{2,1,0:T(8,128)(2,1)S(1)}, u32[]{:S(2)}, u32[]{:S(2)}) collective-permute-start(bf16[8,128,128]{2,1,0:T(8,128)(2,1)} %get-tuple-element.14), channel_id=1, source_target_pairs={{1,0},{2,1},{3,2},{4,3},{5,4},{6,5},{7,6},{8,7},{9,8},{10,9},{11,1... | collective-permute-start | bytes 786440 | tf_op jit(solution)/shard_map/ppermute | solution.py:373
  73.9 16.1 %copy-start = (bf16[8,128,128]{2,1,0:T(8,128)(2,1)}, bf16[8,128,128]{2,1,0:T(8,128)(2,1)S(1)}, u32[]{:S(2)}) copy-start(bf16[8,128,128]{2,1,0:T(8,128)(2,1)S(1)} %collective-permute-done.4.below_ref) | copy-start | bytes 786436
  75.8 14.2 %copy-start.1 = (bf16[8,128,128]{2,1,0:T(8,128)(2,1)}, bf16[8,128,128]{2,1,0:T(8,128)(2,1)S(1)}, u32[]{:S(2)}) copy-start(bf16[8,128,128]{2,1,0:T(8,128)(2,1)S(1)} %collective-permute-done.5.above_ref) | copy-start | bytes 786436
  76.7 10.7 %collective-permute-start.6 = (bf16[1,128,128]{2,1,0:T(8,128)(2,1)S(1)}, bf16[1,128,128]{2,1,0:T(8,128)(2,1)S(1)}, u32[]{:S(2)}, u32[]{:S(2)}) collective-permute-start(bf16[1,128,128]{2,1,0:T(8,128)(2,1)S(1)} %get-tuple-element.25), channel_id=1, source_target_pairs={{0,32},{32,64},{64,96},{96,128},{128,160},{160,192},{192,224},{1,3... | collective-permute-start | bytes 98312 | tf_op jit(solution)/shard_map/ppermute | solution.py:373
  79.0 11.0 %collective-permute-start.7 = (bf16[1,128,128]{2,1,0:T(8,128)(2,1)S(1)}, bf16[1,128,128]{2,1,0:T(8,128)(2,1)S(1)}, u32[]{:S(2)}, u32[]{:S(2)}) collective-permute-start(bf16[1,128,128]{2,1,0:T(8,128)(2,1)S(1)} %get-tuple-element.24), channel_id=1, source_target_pairs={{32,0},{64,32},{96,64},{128,96},{160,128},{192,160},{224,192},{33,... | collective-permute-start | bytes 98312 | tf_op jit(solution)/shard_map/ppermute | solution.py:373
  87.4 2.6 %copy-start.9 = (bf16[1,128,128]{2,1,0:T(8,128)(2,1)}, bf16[1,128,128]{2,1,0:T(8,128)(2,1)S(1)}, u32[]{:S(2)}) copy-start(bf16[1,128,128]{2,1,0:T(8,128)(2,1)S(1)} %collective-permute-done.6.left_ref) | copy-start | bytes 98308
  90.0 0.6 copy-start.10
  93.4 11.6 %copy-start.2 = (bf16[6,128,128]{2,1,0:T(8,128)(2,1)S(1)}, bf16[6,128,128]{2,1,0:T(8,128)(2,1)}, u32[]{:S(2)}) copy-start(bf16[6,128,128]{2,1,0:T(8,128)(2,1)} %get-tuple-element.17) | copy-start | bytes 589828
  94.2 10.7 %collective-permute-start.8 = (bf16[1,128,128]{2,1,0:T(8,128)(2,1)S(1)}, bf16[1,128,128]{2,1,0:T(8,128)(2,1)S(1)}, u32[]{:S(2)}, u32[]{:S(2)}) collective-permute-start(bf16[1,128,128]{2,1,0:T(8,128)(2,1)S(1)} %get-tuple-element.27), channel_id=1, source_target_pairs={{0,32},{32,64},{64,96},{96,128},{128,160},{160,192},{192,224},{1,3... | collective-permute-start | bytes 98312 | tf_op jit(solution)/shard_map/ppermute | solution.py:373
  102.6 9.8 %collective-permute-start.9 = (bf16[1,128,128]{2,1,0:T(8,128)(2,1)S(1)}, bf16[1,128,128]{2,1,0:T(8,128)(2,1)S(1)}, u32[]{:S(2)}, u32[]{:S(2)}) collective-permute-start(bf16[1,128,128]{2,1,0:T(8,128)(2,1)S(1)} %get-tuple-element.26), channel_id=1, source_target_pairs={{32,0},{64,32},{96,64},{128,96},{160,128},{192,160},{224,192},{33,... | collective-permute-start | bytes 98312 | tf_op jit(solution)/shard_map/ppermute | solution.py:373
  112.4 12.8 %copy-start.3 = (bf16[8,128,128]{2,1,0:T(8,128)(2,1)}, bf16[8,128,128]{2,1,0:T(8,128)(2,1)S(1)}, u32[]{:S(2)}) copy-start(bf16[8,128,128]{2,1,0:T(8,128)(2,1)S(1)} %constant_dynamic-update-slice_fusion.in_mid_ref) | copy-start | bytes 786436
  112.4 12.8 %collective-permute-start.10 = (bf16[8,128,128]{2,1,0:T(8,128)(2,1)S(1)}, bf16[8,128,128]{2,1,0:T(8,128)(2,1)S(1)}, u32[]{:S(2)}, u32[]{:S(2)}) collective-permute-start(bf16[8,128,128]{2,1,0:T(8,128)(2,1)S(1)} %constant_dynamic-update-slice_fusion.in_mid_ref), channel_id=1, source_target_pairs={{0,1},{1,2},{2,3},{3,4},{4,5},{5,6},{6,7},{7,8},{8,9},{9,10},{10,1... | collective-permute-start | bytes 786440 | tf_op jit(solution)/shard_map/ppermute | solution.py:373
  114.4 10.8 %collective-permute-start.11 = (bf16[8,128,128]{2,1,0:T(8,128)(2,1)S(1)}, bf16[8,128,128]{2,1,0:T(8,128)(2,1)S(1)}, u32[]{:S(2)}, u32[]{:S(2)}) collective-permute-start(bf16[8,128,128]{2,1,0:T(8,128)(2,1)S(1)} %constant_dynamic-update-slice_fusion.in_mid_ref), channel_id=1, source_target_pairs={{1,0},{2,1},{3,2},{4,3},{5,4},{6,5},{7,6},{8,7},{9,8},{10,9},{11,1... | collective-permute-start | bytes 786440 | tf_op jit(solution)/shard_map/ppermute | solution.py:373
  125.2 0.7 copy-start.5
  125.2 0.8 copy-start.6
  161.4 9.1 %collective-permute-start.12 = (f32[8,3,128]{2,1,0:T(4,128)}, f32[8,3,128]{2,1,0:T(4,128)S(1)}, u32[]{:S(2)}, u32[]{:S(2)}) collective-permute-start(f32[8,3,128]{2,1,0:T(4,128)} %get-tuple-element.20), channel_id=1, source_target_pairs={{0,1},{1,2},{2,3},{3,4},{4,5},{5,6},{6,7},{7,8},{8,9},{9,10},{10,1... | collective-permute-start | bytes 36872 | tf_op jit(solution)/shard_map/ppermute | solution.py:373
  163.3 8.8 %collective-permute-start.13 = (f32[8,3,128]{2,1,0:T(4,128)}, f32[8,3,128]{2,1,0:T(4,128)S(1)}, u32[]{:S(2)}, u32[]{:S(2)}) collective-permute-start(f32[8,3,128]{2,1,0:T(4,128)} %get-tuple-element.21), channel_id=1, source_target_pairs={{1,0},{2,1},{3,2},{4,3},{5,4},{6,5},{7,6},{8,7},{9,8},{10,9},{11,1... | collective-permute-start | bytes 36872 | tf_op jit(solution)/shard_map/ppermute | solution.py:373
  172.1 14.0 %copy-start.12 = (f32[8,3,128]{2,1,0:T(4,128)S(1)}, f32[8,3,128]{2,1,0:T(4,128)}, u32[]{:S(2)}) copy-start(f32[8,3,128]{2,1,0:T(4,128)} %get-tuple-element.19) | copy-start | bytes 36868
  172.9 11.3 %collective-permute-start.14 = (f32[1,3,128]{2,1,0:T(4,128)S(1)}, f32[1,3,128]{2,1,0:T(4,128)S(1)}, u32[]{:S(2)}, u32[]{:S(2)}) collective-permute-start(f32[1,3,128]{2,1,0:T(4,128)S(1)} %get-tuple-element.28), channel_id=1, source_target_pairs={{0,32},{32,64},{64,96},{96,128},{128,160},{160,192},{192,224},{1,3... | collective-permute-start | bytes 4616 | tf_op jit(solution)/shard_map/ppermute | solution.py:373
  174.8 8.8 %copy-start.13 = (f32[6,128]{1,0:T(8,128)S(1)}, f32[6,128]{1,0:T(8,128)}, u32[]{:S(2)}) copy-start(f32[6,128]{1,0:T(8,128)} %get-tuple-element.16) | copy-start | bytes 9220
  174.8 11.3 %collective-permute-start.15 = (f32[1,3,128]{2,1,0:T(4,128)S(1)}, f32[1,3,128]{2,1,0:T(4,128)S(1)}, u32[]{:S(2)}, u32[]{:S(2)}) collective-permute-start(f32[1,3,128]{2,1,0:T(4,128)S(1)} %get-tuple-element.29), channel_id=1, source_target_pairs={{32,0},{64,32},{96,64},{128,96},{160,128},{192,160},{224,192},{33,... | collective-permute-start | bytes 4616 | tf_op jit(solution)/shard_map/ppermute | solution.py:373

commit v2 on v1

v2 whole, which is shorter than its diff:
```python
import jax
import jax.numpy as jnp
from jax import lax
from jax.experimental import pallas as pl
from jax.experimental.pallas import tpu as pltpu
from jax.sharding import PartitionSpec as P

BX = 6
EX = 8
A = 128
C = 128
K = 4
ROWS = 32
F32 = jnp.float32
BF16 = jnp.bfloat16
SIGMA = 1.5
NT = (((1,), (1,)), ((), ()))
E = 3 * EX

HOME_PAIRS = [
    (h, (o % 3) * EX + h + o // 3, EX + 1 + h, o) for h in range(BX) for o in range(9)
]
FAR_PAIRS = [
    (f, (2 - o % 3) * EX + f + 2 - o // 3, (2 - o % 3) * EX + f + 2 - o // 3, o)
    for f in range(BX)
    for o in range(9)
]


def dot(a, b):
    return jnp.dot(a, b, preferred_element_type=F32)


def dot_nt(a, b):
    return lax.dot_general(a, b, NT, preferred_element_type=F32)


def pack_kernel(pos_ref, species_ref, codes_ref, count_ref, first_ref, out_ref, last_ref):
    block_id = lax.broadcasted_iota(jnp.int32, (8, 128), 0)
    mask = jnp.zeros((8, 128), jnp.int32)
    for p in range(codes_ref.shape[2]):
        code = codes_ref[0, 0, p]
        block = lax.shift_right_logical(code * 57, 9)
        bit = jnp.where(p < count_ref[0, 0], lax.shift_left(1, code - 9 * block), 0)
        mask = mask + jnp.where(block_id == block, bit, 0)
    mask = mask.astype(F32)
    for h in range(BX):
        places = [(out_ref, h)]
        if h == 0:
            places.append((first_ref, 0))
        if h == BX - 1:
            places.append((last_ref, 0))
        for ref, i in places:
            ref[i, 0:3, :] = pos_ref[h, 0]
            ref[i, 3:4, :] = species_ref[h].astype(F32)
            ref[i, 4:5, :] = mask[h : h + 1, :]
            ref[i, 5:8, :] = jnp.zeros((3, 128), F32)


def gather_ext(lo_ref, mid_ref, hi_ref, ext_ref):
    for row, ref in enumerate((lo_ref, mid_ref, hi_ref)):
        for x in range(EX):
            ext_ref[row * EX + x] = ref[x]
    ext_ref[E : E + 8] = jnp.full((8, 8, A), 1.0e4, F32)


def send_masks(ext_ref, maskv_ref, masks_ref, sem):
    for e in range(E):
        maskv_ref[e : e + 1, :] = ext_ref[e, 4:5, :].astype(jnp.int32)
    copy = pltpu.make_async_copy(maskv_ref, masks_ref, sem)
    copy.start()
    return copy


def make_list(pairs, masks_ref, list_ref):
    n = jnp.int32(0)
    for own, other, lister, o in pairs:
        list_ref[n] = own + other * 8 + (256 if o == 4 else 0)
        n = n + (lax.shift_right_logical(masks_ref[lister, 0], o) & 1)
    for i in range(3):
        list_ref[n + i] = E * 8
    return n


def entry(list_ref, p):
    code = list_ref[p]
    own = code & 7
    other = lax.shift_right_logical(code, 3) & 31
    bias = jnp.where(code >= 256, 0, 1024)
    return own, other, bias


def turned_blocks(ext_ref):
    return [ext_ref[0:16].reshape(128, A).T, ext_ref[16:32].reshape(128, A).T]


def spread_lane(turned, e, d):
    lane = 8 * (e % 16) + d
    return jnp.broadcast_to(turned[e // 16][:, lane : lane + 1], (A, 128))


def geometry(col_ref, i, row, r, sign, bias, rows=ROWS):
    off = [sign * (row[d] - col_ref[i, d, pl.ds(r, rows), :]) for d in range(3)]
    squared = off[0] * off[0] + off[1] * off[1] + off[2] * off[2]
    soft = squared + 0.25
    inv = lax.rsqrt(soft)
    s = soft * inv
    taper = jnp.maximum(1.0 - squared * (1.0 / 36.0), 0.0)
    at = lax.broadcasted_iota(jnp.int32, (rows, 128), 0) + (r + bias)
    lane = lax.broadcasted_iota(jnp.int32, (rows, 128), 1)
    taper = jnp.where(at == lane, 0.0, taper)
    u = jnp.minimum(s, 6.25) * (1.0 / SIGMA) - 0.5
    base = taper * jnp.exp(-u * u)
    step = jnp.exp(2.0 * u - 1.0)
    q = [base]
    for k in range(1, K):
        q.append(q[-1] * (step * EXPS[k]))
    return off, inv, taper, u, q


EXPS = [1.0, 1.0, 0.1353352832366127, 0.01831563888873418]


def store_tiles(put, off, inv, taper, q):
    direction = [o * inv for o in off]
    for k in range(K):
        radial = taper * q[k]
        put(0, k, radial.astype(BF16))
        for d in range(3):
            put(1 + d, k, (radial * direction[d]).astype(BF16))


def pull_back(grads, off, inv, taper, u, q):
    direction = [o * inv for o in off]
    s0 = s1 = turn = None
    dg = [None] * 3
    for k in range(K):
        radial = taper * q[k]
        tilted = [grads(1 + d, k) for d in range(3)]
        along = tilted[0] * direction[0] + tilted[1] * direction[1] + tilted[2] * direction[2]
        p = (grads(0, k) + along) * q[k]
        w = along * radial
        s0 = p if s0 is None else s0 + p
        if k:
            s1 = p * float(k) if s1 is None else s1 + p * float(k)
        turn = w if turn is None else turn + w
        for d in range(3):
            v = tilted[d] * radial
            dg[d] = v if dg[d] is None else dg[d] + v
    bend = (2.0 / SIGMA) * taper * (u * s0 - s1) + turn * inv
    weight = -(s0 * (1.0 / 9.0)) - inv * bend
    return [dg[d] * inv + weight * off[d] for d in range(3)]


def rows_of(ext_ref, e):
    return [ext_ref[e, d : d + 1, :] for d in range(3)]


def scaled(feature, weights_ref, k):
    return (feature.astype(F32) * weights_ref[k : k + 1, :]).astype(BF16)


def forward_kernel(
    lo_ref, mid_ref, hi_ref, table_ref, ws1_ref, wv1_ref, ws2_ref, wv2_ref, ms_ref, mv_ref,
    pre_ref, feat_ref, out_lo_ref, out_mid_ref, out_hi_ref, keep_s_ref, keep_v_ref,
    ext_ref, col_ref, init_ref, scaled_s_ref, scaled_v_ref, acc_ref, tile_a_ref, tile_b_ref,
    wide_a_ref, wide_b_ref, ready_ref, total_ref, maskv_ref, masks_ref, list1_ref, list2_ref, sem,
    sem_s, sem_v,
):
    gather_ext(lo_ref, mid_ref, hi_ref, ext_ref)
    copy = send_masks(ext_ref, maskv_ref, masks_ref, sem)
    turned = turned_blocks(ext_ref)
    lanes = lax.broadcasted_iota(jnp.int32, (A, 128), 1).astype(F32)
    for e in range(E):
        for d in range(3):
            col_ref[e, d] = spread_lane(turned, e, d)
        hot = (spread_lane(turned, e, 3) == lanes).astype(BF16)
        init_ref[e] = dot(hot, table_ref[...]).astype(BF16)
    col_ref[E] = jnp.full((3, A, 128), 1.0e4, F32)

    def scale_block(e, carry):
        for k in range(K):
            scaled_s_ref[e, pl.ds(k * A, A), :] = scaled(init_ref[e], ws1_ref, k)
            scaled_v_ref[e, pl.ds(k * A, A), :] = scaled(init_ref[e], wv1_ref, k)
        return carry

    lax.fori_loop(0, E, scale_block, 0)
    scaled_s_ref[E] = jnp.zeros((K * A, C), BF16)
    scaled_v_ref[E] = jnp.zeros((K * A, C), BF16)
    keep_s = pltpu.make_async_copy(scaled_s_ref.at[0:E], keep_s_ref, sem_s)
    keep_s.start()
    keep_v = pltpu.make_async_copy(scaled_v_ref.at[0:E], keep_v_ref, sem_v)
    keep_v.start()
    acc_ref[...] = jnp.zeros_like(acc_ref)
    total_ref[...] = jnp.zeros_like(total_ref)
    copy.wait()
    n1 = make_list(HOME_PAIRS, masks_ref, list1_ref)
    n2 = make_list(FAR_PAIRS, masks_ref, list2_ref)

    def first_tiles(p, tile_ref):
        own, other, bias = entry(list1_ref, p)
        row = rows_of(ext_ref, other)
        for r in range(0, A, ROWS):
            off, inv, taper, u, q = geometry(col_ref, own + EX + 1, row, r, 1.0, bias)

            def put(g, k, tile):
                tile_ref[pl.ds(g * A + r, ROWS), pl.ds(k * A, A)] = tile

            store_tiles(put, off, inv, taper, q)

    def first_sum(p, tile_ref):
        own, other, _ = entry(list1_ref, p)
        acc_ref[own, 0:A, :] += dot(tile_ref[0:A, :], scaled_s_ref[other])
        acc_ref[own, A : 4 * A, :] += dot(tile_ref[A : 4 * A, :], scaled_v_ref[other])

    def first(i, carry):
        p = 2 * i
        first_sum(p, tile_a_ref)
        first_tiles(p + 1, tile_b_ref)
        first_sum(p + 1, tile_b_ref)
        first_tiles(p + 2, tile_a_ref)
        return carry

    first_tiles(0, tile_a_ref)
    lax.fori_loop(0, lax.shift_right_logical(n1 + 1, 1), first, 0)

    def mix(h, carry):
        pre = dot((acc_ref[h, 0:A, :] * 0.125).astype(BF16), ms_ref[...])
        pre_ref[h] = pre
        scalar = (init_ref[h + EX + 1].astype(F32) + pre * jax.nn.sigmoid(pre)).astype(BF16)
        vector = dot((acc_ref[h, A : 4 * A, :] * 0.125).astype(BF16), mv_ref[...]).astype(BF16)
        feat_ref[h, 0:A, :] = scalar
        feat_ref[h, A : 4 * A, :] = vector
        for k in range(K):
            ready_ref[h, pl.ds(k * A, A), :] = scaled(scalar, ws2_ref, k)
            for d in range(3):
                ready_ref[h, pl.ds(((1 + d) * K + k) * A, A), :] = scaled(
                    vector[d * A : (d + 1) * A, :], wv2_ref, k
                )
        return carry

    lax.fori_loop(0, BX, mix, 0)

    def second_tiles(p, wide_ref):
        own, other, bias = entry(list2_ref, p)
        row = rows_of(ext_ref, own + EX + 1)
        for r in range(0, A, ROWS):
            off, inv, taper, u, q = geometry(col_ref, other, row, r, 1.0, bias)

            def put(g, k, tile):
                wide_ref[pl.ds(r, ROWS), pl.ds((g * K + k) * A, A)] = tile

            store_tiles(put, off, inv, taper, q)

    def second_sum(p, wide_ref):
        own, other, _ = entry(list2_ref, p)
        total_ref[other] += dot(wide_ref[...], ready_ref[own])

    def second(i, carry):
        p = 2 * i
        second_sum(p, wide_a_ref)
        second_tiles(p + 1, wide_b_ref)
        second_sum(p + 1, wide_b_ref)
        second_tiles(p + 2, wide_a_ref)
        return carry

    second_tiles(0, wide_a_ref)
    lax.fori_loop(0, lax.shift_right_logical(n2 + 1, 1), second, 0)
    for x in range(EX):
        out_lo_ref[x] = total_ref[x].astype(BF16)
        out_mid_ref[x] = total_ref[EX + x]
        out_hi_ref[x] = total_ref[2 * EX + x].astype(BF16)
    keep_s.wait()
    keep_v.wait()


def slope_of(value):
    sigma = jax.nn.sigmoid(value)
    return sigma * (1.0 + value * (1.0 - sigma))


def middle_kernel(
    mid_ref, below_ref, above_ref, left_ref, right_ref, feat_ref, mix_ref, readout_ref,
    energy_ref, second_in_ref, second_own_ref,
):
    for x in range(EX):
        msg = mid_ref[x] + below_ref[x].astype(F32) + above_ref[x].astype(F32)
        if x < 2:
            msg = msg + left_ref[x].astype(F32)
        if x >= EX - 2:
            msg = msg + right_ref[x - EX + 2].astype(F32)
        pre = dot((msg * 0.125).astype(BF16), mix_ref[...])
        sigma = jax.nn.sigmoid(pre)
        if 1 <= x <= BX:
            part = (feat_ref[x - 1, 0:A, :].astype(F32) + pre * sigma) * readout_ref[...]
            energy_ref[x - 1] = jnp.sum(part.T, axis=0, keepdims=True)
        grad = (readout_ref[...] * (sigma * (1.0 + pre * (1.0 - sigma)))).astype(BF16)
        second = dot_nt(grad, mix_ref[...]) * 0.125
        second_own_ref[x] = second
        second_in_ref[x] = second.astype(BF16)


def backward_kernel(
    lo_ref, mid_ref, hi_ref, in_lo_ref, in_mid_ref, in_hi_ref, feat_ref, pre_ref, keep_s_ref,
    keep_v_ref, ws2_ref, wv2_ref, ms_ref, mv_ref, readout_ref,
    out_lo_ref, out_mid_ref, out_hi_ref,
    ext_ref, col_ref, scaled_s_ref, scaled_v_ref, cot_s_ref, cot_v_ref, acc_ref, tile_a_ref,
    tile_b_ref, grad_a_ref, grad_b_ref, inward_ref, down_ref, across_ref, maskv_ref, masks_ref,
    list1_ref, list2_ref, sem, sem_s, sem_v,
):
    keep_s = pltpu.make_async_copy(keep_s_ref, scaled_s_ref.at[0:E], sem_s)
    keep_s.start()
    keep_v = pltpu.make_async_copy(keep_v_ref, scaled_v_ref.at[0:E], sem_v)
    keep_v.start()
    gather_ext(lo_ref, mid_ref, hi_ref, ext_ref)
    copy = send_masks(ext_ref, maskv_ref, masks_ref, sem)
    turned = turned_blocks(ext_ref)
    for h in range(BX):
        for d in range(3):
            col_ref[h, d] = spread_lane(turned, EX + 1 + h, d)
    for row, ref in enumerate((in_lo_ref, in_mid_ref, in_hi_ref)):

        def cot_block(x, carry, row=row, ref=ref):
            for k in range(K):
                cot_s_ref[row * EX + x, pl.ds(k * A, A), :] = scaled(ref[x], ws2_ref, k)
                cot_v_ref[row * EX + x, pl.ds(k * A, A), :] = scaled(ref[x], wv2_ref, k)
            return carry

        lax.fori_loop(0, EX, cot_block, 0)
    for ref in (cot_s_ref, cot_v_ref, scaled_s_ref, scaled_v_ref):
        ref[E] = jnp.zeros((K * A, C), BF16)
    tile_b_ref[...] = jnp.zeros_like(tile_b_ref)
    acc_ref[...] = jnp.zeros_like(acc_ref)
    down_ref[...] = jnp.zeros_like(down_ref)
    across_ref[...] = jnp.zeros_like(across_ref)
    copy.wait()
    n1 = make_list(HOME_PAIRS, masks_ref, list1_ref)
    n2 = make_list(FAR_PAIRS, masks_ref, list2_ref)

    def move(own, other, r, off, inv, taper, u, q, own_sign, grad_ref):
        def grads(g, k):
            return grad_ref[pl.ds(g * A + r, ROWS), pl.ds(k * A, A)]

        moved = pull_back(grads, off, inv, taper, u, q)
        parts = []
        for d in range(3):
            across_ref[own, d, pl.ds(r, ROWS), :] += own_sign * moved[d]
            part = moved[d][0:8]
            for i in range(8, ROWS, 8):
                part = part + moved[d][i : i + 8]
            parts.append(part)
        return parts

    def add_down(other, own_sign, sums):
        for d in range(3):
            down_ref[other, d] -= own_sign * sums[d]

    def plus(sums, parts):
        return parts if sums is None else [a + b for a, b in zip(sums, parts)]

    def second_grads(p, grad_ref):
        own, other, _ = entry(list2_ref, p)
        grad_ref[0:A, :] = dot_nt(feat_ref[own, 0:A, :], cot_s_ref[other])
        grad_ref[A : 4 * A, :] = dot_nt(feat_ref[own, A : 4 * A, :], cot_v_ref[other])

    def second_move(p, grad_ref, tile_ref):
        own, other, bias = entry(list2_ref, p)
        row = rows_of(ext_ref, other)
        sums = None
        for r in range(0, A, ROWS):
            off, inv, taper, u, q = geometry(col_ref, own, row, r, -1.0, bias)

            def put(g, k, tile):
                tile_ref[pl.ds(g * A + r, ROWS), pl.ds(k * A, A)] = tile

            store_tiles(put, off, inv, taper, q)
            sums = plus(sums, move(own, other, r, off, inv, taper, u, q, 1.0, grad_ref))
        add_down(other, 1.0, sums)

    def second_sum(own, other, tile_ref):
        acc_ref[own, 0:A, :] += dot(tile_ref[0:A, :], cot_s_ref[other])
        acc_ref[own, A : 4 * A, :] += dot(tile_ref[A : 4 * A, :], cot_v_ref[other])

    def second_back(i, carry):
        p = 2 * i
        own, other, _ = entry(list2_ref, p)
        second_sum(*carry, tile_b_ref)
        second_grads(p + 1, grad_b_ref)
        second_move(p, grad_a_ref, tile_a_ref)
        second_sum(own, other, tile_a_ref)
        second_grads(p + 2, grad_a_ref)
        second_move(p + 1, grad_b_ref, tile_b_ref)
        own, other, _ = entry(list2_ref, p + 1)
        return own, other

    second_grads(0, grad_a_ref)
    last = lax.fori_loop(
        0, lax.shift_right_logical(n2 + 1, 1), second_back, (jnp.int32(0), jnp.int32(E))
    )
    second_sum(*last, tile_b_ref)

    def inward(h, carry):
        slope = (readout_ref[...] + acc_ref[h, 0:A, :]) * slope_of(pre_ref[h])
        inward_ref[h, 0:A, :] = (dot_nt(slope.astype(BF16), ms_ref[...]) * 0.125).astype(BF16)
        inward_ref[h, A : 4 * A, :] = (
            dot_nt(acc_ref[h, A : 4 * A, :].astype(BF16), mv_ref[...]) * 0.125
        ).astype(BF16)
        return carry

    lax.fori_loop(0, BX, inward, 0)
    keep_s.wait()
    keep_v.wait()

    def first_grads(p, grad_ref):
        own, other, _ = entry(list1_ref, p)
        grad_ref[0:A, :] = dot_nt(inward_ref[own, 0:A, :], scaled_s_ref[other])
        grad_ref[A : 4 * A, :] = dot_nt(inward_ref[own, A : 4 * A, :], scaled_v_ref[other])

    def first_move(p, grad_ref):
        own, other, bias = entry(list1_ref, p)
        row = rows_of(ext_ref, other)
        sums = None
        for r in range(0, A, ROWS):
            off, inv, taper, u, q = geometry(col_ref, own, row, r, 1.0, bias)
            sums = plus(sums, move(own, other, r, off, inv, taper, u, q, -1.0, grad_ref))
        add_down(other, -1.0, sums)

    def first_back(i, carry):
        p = 2 * i
        first_grads(p + 1, grad_b_ref)
        first_move(p, grad_a_ref)
        first_grads(p + 2, grad_a_ref)
        first_move(p + 1, grad_b_ref)
        return carry

    first_grads(0, grad_a_ref)
    lax.fori_loop(0, lax.shift_right_logical(n1 + 1, 1), first_back, 0)
    for row, ref in enumerate((out_lo_ref, out_mid_ref, out_hi_ref)):
        for x in range(EX):
            for d in range(3):
                line = jnp.sum(down_ref[row * EX + x, d], axis=0, keepdims=True)
                if row == 1 and 1 <= x <= BX:
                    line = line + jnp.sum(across_ref[x - 1, d].T, axis=0, keepdims=True)
                ref[x, d : d + 1, :] = line


def final_kernel(mid_ref, below_ref, above_ref, left_ref, right_ref, out_ref):
    for h in range(BX):
        total = mid_ref[h + 1] + below_ref[h + 1] + above_ref[h + 1]
        if h == 0:
            total = total + left_ref[0]
        if h == BX - 1:
            total = total + right_ref[0]
        out_ref[h, 0] = -total


ANY = pl.BlockSpec(memory_space=pl.ANY)
VMEM = pl.BlockSpec(memory_space=pltpu.VMEM)
SMEM = pl.BlockSpec(memory_space=pltpu.SMEM)
PARAMS = pltpu.CompilerParams(vmem_limit_bytes=56 * 1024 * 1024)


def call(kernel, args, outs, scratch=(), in_specs=None, out_specs=None):
    return pl.pallas_call(
        kernel,
        out_shape=[jax.ShapeDtypeStruct(s, d) for s, d in outs],
        in_specs=in_specs or [VMEM] * len(args),
        out_specs=out_specs or [VMEM] * len(outs),
        scratch_shapes=list(scratch),
        compiler_params=PARAMS,
    )(*args)


def along(block, axis, step):
    size = lax.axis_size(axis)
    return lax.ppermute(block, axis, [(i, i + step) for i in range(size) if 0 <= i + step < size])


def both(lo, hi, axis, step=1):
    return along(lo, axis, step), along(hi, axis, -step)


def list_scratch():
    return [
        pltpu.VMEM((E, 128), jnp.int32),
        pltpu.SMEM((E, 128), jnp.int32),
        pltpu.SMEM((64,), jnp.int32),
        pltpu.SMEM((64,), jnp.int32),
        pltpu.SemaphoreType.DMA,
        pltpu.SemaphoreType.DMA,
        pltpu.SemaphoreType.DMA,
    ]


def forward_call(*args):
    return call(
        forward_kernel,
        args,
        [
            ((BX, A, C), F32),
            ((BX, 4 * A, C), BF16),
            ((EX, A, C), BF16),
            ((EX, A, C), F32),
            ((EX, A, C), BF16),
            ((E, K * A, C), BF16),
            ((E, K * A, C), BF16),
        ],
        [
            pltpu.VMEM((E + 8, 8, A), F32),
            pltpu.VMEM((E + 1, 3, A, 128), F32),
            pltpu.VMEM((E, A, C), BF16),
            pltpu.VMEM((E + 1, K * A, C), BF16),
            pltpu.VMEM((E + 1, K * A, C), BF16),
            pltpu.VMEM((BX, 4 * A, C), F32),
            pltpu.VMEM((4 * A, K * A), BF16),
            pltpu.VMEM((4 * A, K * A), BF16),
            pltpu.VMEM((A, 4 * K * A), BF16),
            pltpu.VMEM((A, 4 * K * A), BF16),
            pltpu.VMEM((BX, 4 * K * A, C), BF16),
            pltpu.VMEM((E + 1, A, C), F32),
            *list_scratch(),
        ],
        out_specs=[VMEM] * 5 + [ANY] * 2,
    )


def backward_call(*args):
    return call(
        backward_kernel,
        args,
        [((EX, 3, A), F32)] * 3,
        [
            pltpu.VMEM((E + 8, 8, A), F32),
            pltpu.VMEM((BX, 3, A, 128), F32),
            pltpu.VMEM((E + 1, K * A, C), BF16),
            pltpu.VMEM((E + 1, K * A, C), BF16),
            pltpu.VMEM((E + 1, K * A, C), BF16),
            pltpu.VMEM((E + 1, K * A, C), BF16),
            pltpu.VMEM((BX, 4 * A, C), F32),
            pltpu.VMEM((4 * A, K * A), BF16),
            pltpu.VMEM((4 * A, K * A), BF16),
            pltpu.VMEM((4 * A, K * A), F32),
            pltpu.VMEM((4 * A, K * A), F32),
            pltpu.VMEM((BX, 4 * A, C), BF16),
            pltpu.VMEM((E + 1, 3, 8, A), F32),
            pltpu.VMEM((BX, 3, A, 128), F32),
            *list_scratch(),
        ],
        in_specs=[VMEM] * 8 + [ANY] * 2 + [VMEM] * 5,
    )


def local(
    positions, species, pair_codes, pair_count, embed_table, ws1, wv1, ws2, wv2, ms, mv, m2, readout
):
    first, own, last = call(
        pack_kernel,
        (positions, species, pair_codes, pair_count),
        [((1, 8, A), F32), ((BX, 8, A), F32), ((1, 8, A), F32)],
        in_specs=[VMEM, VMEM, SMEM, SMEM],
    )
    left, right = both(last, first, "gx")
    mid = jnp.concatenate([left, own, right], axis=0)
    ext = both(mid, mid, "gy")
    ext = (ext[0], mid, ext[1])
    table = jnp.pad(embed_table, ((0, 128 - embed_table.shape[0]), (0, 0)))
    readout = readout.reshape(1, C)
    pre, feat, lo, mid, hi, keep_s, keep_v = forward_call(
        *ext, table, ws1, wv1, ws2, wv2, ms, mv
    )
    below, above = both(hi, lo, "gy")
    edge = lambda x: (mid[x : x + 2] + below[x : x + 2] + above[x : x + 2]).astype(BF16)
    left, right = both(edge(EX - 2), edge(0), "gx")
    energy, inner, inner_own = call(
        middle_kernel,
        (mid, below, above, left, right, feat, m2, readout),
        [((BX, 1, A), F32), ((EX, A, C), BF16), ((EX, A, C), F32)],
    )
    inner = both(inner, inner, "gy")
    lo, mid, hi = backward_call(
        *ext, inner[0], inner_own, inner[1], feat, pre, keep_s, keep_v, ws2, wv2, ms, mv, readout
    )
    below, above = both(hi, lo, "gy")
    edge = lambda x: mid[x : x + 1] + below[x : x + 1] + above[x : x + 1]
    left, right = both(edge(EX - 1), edge(0), "gx")
    (forces,) = call(final_kernel, (mid, below, above, left, right), [((BX, 1, 3, A), F32)])
    return energy, forces


def solution(mesh):
    in_specs = (
        P("gx", "gy", None, None),
        P("gx", "gy", None),
        P("gx", "gy", None),
        P("gx", "gy"),
        *[P()] * 9,
    )
    out_specs = (P("gx", "gy", None), P("gx", "gy", None, None))
    return jax.shard_map(local, mesh=mesh, in_specs=in_specs, out_specs=out_specs, check_vma=False)
```

time: 190 us -> 171 us (0.900)
  the two profiles are of different devices: /device:TPU:18 before, /device:TPU:20 now
where the time goes in v2:
time: 171 us; the launch traced here: 169 us
  Pallas kernels  65.1 us (38%)
  starting transfers between devices  57.9 us (34%)
  waiting for transfers between devices  34.9 us (20%)
  local copies, waits for them, and re-layouts  7.27 us (4%)
  other arithmetic  1.8 us (1%)
    pallas_call x5, Pallas kernels, call(): pl.pallas_call(kernel, out_shape=[jax.ShapeDtypeStruct(s, d) for s, d in...  65.1 us
    ppermute x14, starting transfers between devices, along(): lax.ppermute(block, axis, [(i, i + step) for i in range(size) if 0 <= i +...  57.9 us
    ppermute x14, waiting for transfers between devices, along(): lax.ppermute(block, axis, [(i, i + step) for i in range(size) if 0 <= i +...  34.9 us
    unnamed x30, local copies, waits for them, and re-layouts  5.91 us
  transfers between devices with their start and end apart: 14, of which 10 were waited for; matrix products, arithmetic and copies ran while one was open for 1% of the time, Pallas kernels for 0%

profile of v2, /device:TPU:20, one launch (start us, length us, event | category | flops | bytes accessed | tf_op | source)
XLA Modules:
  0.0 168.5 jit_solution(695883099826668358)
XLA Ops:
  1.3 1.3 copy.15.pos_ref
  2.6 1.5 shard_map.140
  4.1 9.1 %collective-permute-start = (f32[1,8,128]{2,1,0:T(8,128)}, f32[1,8,128]{2,1,0:T(8,128)S(1)}, u32[]{:S(2)}, u32[]{:S(2)}) collective-permute-start(f32[1,8,128]{2,1,0:T(8,128)} %get-tuple-element.18), channel_id=1, source_target_pairs={{0,32},{32,64},{64,96},{96,128},{128,160},{160,192},{192,224},{1,3... | collective-permute-start | bytes 12296 | tf_op jit(solution)/shard_map/ppermute | solution.py:476
  13.1 1.9 %collective-permute-start.1 = (f32[1,8,128]{2,1,0:T(8,128)}, f32[1,8,128]{2,1,0:T(8,128)S(1)}, u32[]{:S(2)}, u32[]{:S(2)}) collective-permute-start(f32[1,8,128]{2,1,0:T(8,128)} %get-tuple-element.20), channel_id=1, source_target_pairs={{32,0},{64,32},{96,64},{128,96},{160,128},{192,160},{224,192},{33,... | collective-permute-start | bytes 12296 | tf_op jit(solution)/shard_map/ppermute | solution.py:476
  15.1 0.0 collective-permute-done
  15.1 0.7 constant_dynamic-update-slice_fusion.1
  15.8 7.0 %collective-permute-done.1 = f32[1,8,128]{2,1,0:T(8,128)S(1)} collective-permute-done((f32[1,8,128]{2,1,0:T(8,128)}, f32[1,8,128]{2,1,0:T(8,128)S(1)}, u32[]{:S(2)}, u32[]{:S(2)}) %collective-permute-start.1) | collective-permute-done | bytes 4128 | tf_op jit(solution)/shard_map/ppermute | solution.py:476
  22.8 1.9 %collective-permute-start.3 = (f32[8,8,128]{2,1,0:T(8,128)S(1)}, f32[8,8,128]{2,1,0:T(8,128)S(1)}, u32[]{:S(2)}, u32[]{:S(2)}) collective-permute-start(f32[8,8,128]{2,1,0:T(8,128)S(1)} %constant_dynamic-update-slice_fusion.mid_ref), channel_id=1, source_target_pairs={{1,0},{2,1},{3,2},{4,3},{5,4},{6,5},{7,6},{8,7},{9,8},{10,9},{11,1... | collective-permute-start | bytes 98312 | tf_op jit(solution)/shard_map/ppermute | solution.py:476
  24.7 2.4 %collective-permute-start.2 = (f32[8,8,128]{2,1,0:T(8,128)S(1)}, f32[8,8,128]{2,1,0:T(8,128)S(1)}, u32[]{:S(2)}, u32[]{:S(2)}) collective-permute-start(f32[8,8,128]{2,1,0:T(8,128)S(1)} %constant_dynamic-update-slice_fusion.mid_ref), channel_id=1, source_target_pairs={{0,1},{1,2},{2,3},{3,4},{4,5},{5,6},{6,7},{7,8},{8,9},{9,10},{10,1... | collective-permute-start | bytes 98312 | tf_op jit(solution)/shard_map/ppermute | solution.py:476
  27.1 1.4 pad.4.table_ref
  28.5 0.0 collective-permute-done.3.hi_ref
  28.5 4.2 %collective-permute-done.2.lo_ref = f32[8,8,128]{2,1,0:T(8,128)S(1)} collective-permute-done((f32[8,8,128]{2,1,0:T(8,128)S(1)}, f32[8,8,128]{2,1,0:T(8,128)S(1)}, u32[]{:S(2)}, u32[]{:S(2)}) %collective-permute-start.2) | collective-permute-done | bytes 32800 | tf_op jit(solution)/shard_map/ppermute | solution.py:476
  32.6 0.0 copy-done.4
  32.6 0.0 copy-done.5
  32.7 0.6 copy-done.6
  33.3 25.9 %shard_map.141 = (f32[6,128,128]{2,1,0:T(8,128)}, bf16[6,512,128]{2,1,0:T(8,128)(2,1)}, bf16[8,128,128]{2,1,0:T(8,128)(2,1)}, f32[8,128,128]{2,1,0:T(8,128)}, bf...) custom-call(f32[8,8,128]{2,1,0:T(8,128)} %copy-done.6, ...), custom_call_target="tpu_custom_call" | custom-call | tf_op jit(solution)/shard_map/pallas_call | solution.py:464
  59.1 1.9 %collective-permute-start.4 = (bf16[8,128,128]{2,1,0:T(8,128)(2,1)}, bf16[8,128,128]{2,1,0:T(8,128)(2,1)S(1)}, u32[]{:S(2)}, u32[]{:S(2)}) collective-permute-start(bf16[8,128,128]{2,1,0:T(8,128)(2,1)} %get-tuple-element.22), channel_id=1, source_target_pairs={{0,1},{1,2},{2,3},{3,4},{4,5},{5,6},{6,7},{7,8},{8,9},{9,10},{10,1... | collective-permute-start | bytes 786440 | tf_op jit(solution)/shard_map/ppermute | solution.py:476
  61.1 6.3 %collective-permute-start.5 = (bf16[8,128,128]{2,1,0:T(8,128)(2,1)}, bf16[8,128,128]{2,1,0:T(8,128)(2,1)S(1)}, u32[]{:S(2)}, u32[]{:S(2)}) collective-permute-start(bf16[8,128,128]{2,1,0:T(8,128)(2,1)} %get-tuple-element.23), channel_id=1, source_target_pairs={{1,0},{2,1},{3,2},{4,3},{5,4},{6,5},{7,6},{8,7},{9,8},{10,9},{11,1... | collective-permute-start | bytes 786440 | tf_op jit(solution)/shard_map/ppermute | solution.py:476
  67.4 2.4 %collective-permute-done.4.below_ref = bf16[8,128,128]{2,1,0:T(8,128)(2,1)S(1)} collective-permute-done((bf16[8,128,128]{2,1,0:T(8,128)(2,1)}, bf16[8,128,128]{2,1,0:T(8,128)(2,1)S(1)}, u32[]{:S(2)}, u32[]{:S(2)}) %collective-permute-start.4) | collective-permute-done | bytes 262176 | tf_op jit(solution)/shard_map/ppermute | solution.py:476
  69.8 3.9 %collective-permute-done.5.above_ref = bf16[8,128,128]{2,1,0:T(8,128)(2,1)S(1)} collective-permute-done((bf16[8,128,128]{2,1,0:T(8,128)(2,1)}, bf16[8,128,128]{2,1,0:T(8,128)(2,1)S(1)}, u32[]{:S(2)}, u32[]{:S(2)}) %collective-permute-start.5) | collective-permute-done | bytes 262176 | tf_op jit(solution)/shard_map/ppermute | solution.py:476
  73.7 1.1 add_convert_fusion
  74.8 2.7 %collective-permute-start.7 = (bf16[2,128,128]{2,1,0:T(8,128)(2,1)S(1)}, bf16[2,128,128]{2,1,0:T(8,128)(2,1)S(1)}, u32[]{:S(2)}, u32[]{:S(2)}) collective-permute-start(bf16[2,128,128]{2,1,0:T(8,128)(2,1)S(1)} %get-tuple-element.36), channel_id=1, source_target_pairs={{32,0},{64,32},{96,64},{128,96},{160,128},{192,160},{224,192},{33,... | collective-permute-start | bytes 196616 | tf_op jit(solution)/shard_map/ppermute | solution.py:476
  77.6 7.0 %collective-permute-start.6 = (bf16[2,128,128]{2,1,0:T(8,128)(2,1)S(1)}, bf16[2,128,128]{2,1,0:T(8,128)(2,1)S(1)}, u32[]{:S(2)}, u32[]{:S(2)}) collective-permute-start(bf16[2,128,128]{2,1,0:T(8,128)(2,1)S(1)} %get-tuple-element.37), channel_id=1, source_target_pairs={{0,32},{32,64},{64,96},{96,128},{128,160},{160,192},{192,224},{1,3... | collective-permute-start | bytes 196616 | tf_op jit(solution)/shard_map/ppermute | solution.py:476
  84.6 0.3 collective-permute-done.7.right_ref
  84.9 3.7 %collective-permute-done.6.left_ref = bf16[2,128,128]{2,1,0:T(8,128)(2,1)S(1)} collective-permute-done((bf16[2,128,128]{2,1,0:T(8,128)(2,1)S(1)}, bf16[2,128,128]{2,1,0:T(8,128)(2,1)S(1)}, u32[]{:S(2)}, u32[]{:S(2)}) %collective-permute-start.6) | collective-permute-done | bytes 65568 | tf_op jit(solution)/shard_map/ppermute | solution.py:476
  88.6 0.0 copy-done
  88.6 0.0 copy-done.1
  88.6 0.6 copy-done.8
  89.2 3.2 %shard_map.142 = (f32[6,1,128]{2,1,0:T(1,128)}, bf16[8,128,128]{2,1,0:T(8,128)(2,1)}, f32[8,128,128]{2,1,0:T(8,128)}) custom-call(f32[8,128,128]{2,1,0:T(8,128)} %get-tuple-element.21.mid_ref, bf16[8,128,128]{2,1,0:T(8,128)(2,1)} %copy-done, bf16[8,128,128]{2,1,0:T(8,128)(2,1)} %copy-done.1, bf16[2,128,128]{2,1,0:T(8,128)(2,1)} %copy-done.8, ...), custom_call_target="tpu_custom_call" | custom-call | tf_op jit(solution)/shard_map/pallas_call | solution.py:464
  92.4 4.7 %collective-permute-start.9 = (bf16[8,128,128]{2,1,0:T(8,128)(2,1)}, bf16[8,128,128]{2,1,0:T(8,128)(2,1)S(1)}, u32[]{:S(2)}, u32[]{:S(2)}) collective-permute-start(bf16[8,128,128]{2,1,0:T(8,128)(2,1)} %get-tuple-element.26), channel_id=1, source_target_pairs={{1,0},{2,1},{3,2},{4,3},{5,4},{6,5},{7,6},{8,7},{9,8},{10,9},{11,1... | collective-permute-start | bytes 786440 | tf_op jit(solution)/shard_map/ppermute | solution.py:476
  97.1 1.9 %collective-permute-start.8 = (bf16[8,128,128]{2,1,0:T(8,128)(2,1)}, bf16[8,128,128]{2,1,0:T(8,128)(2,1)S(1)}, u32[]{:S(2)}, u32[]{:S(2)}) collective-permute-start(bf16[8,128,128]{2,1,0:T(8,128)(2,1)} %get-tuple-element.26), channel_id=1, source_target_pairs={{0,1},{1,2},{2,3},{3,4},{4,5},{5,6},{6,7},{7,8},{8,9},{9,10},{10,1... | collective-permute-start | bytes 786440 | tf_op jit(solution)/shard_map/ppermute | solution.py:476
  99.0 4.1 %collective-permute-done.9.in_hi_ref = bf16[8,128,128]{2,1,0:T(8,128)(2,1)S(1)} collective-permute-done((bf16[8,128,128]{2,1,0:T(8,128)(2,1)}, bf16[8,128,128]{2,1,0:T(8,128)(2,1)S(1)}, u32[]{:S(2)}, u32[]{:S(2)}) %collective-permute-start.9) | collective-permute-done | bytes 262176 | tf_op jit(solution)/shard_map/ppermute | solution.py:476
  103.1 4.6 %collective-permute-done.8.in_lo_ref = bf16[8,128,128]{2,1,0:T(8,128)(2,1)S(1)} collective-permute-done((bf16[8,128,128]{2,1,0:T(8,128)(2,1)}, bf16[8,128,128]{2,1,0:T(8,128)(2,1)S(1)}, u32[]{:S(2)}, u32[]{:S(2)}) %collective-permute-start.8) | collective-permute-done | bytes 262176 | tf_op jit(solution)/shard_map/ppermute | solution.py:476
  107.7 0.7 copy-done.3
  108.4 33.2 %shard_map.143 = (f32[8,3,128]{2,1,0:T(4,128)}, f32[8,3,128]{2,1,0:T(4,128)}, f32[8,3,128]{2,1,0:T(4,128)}) custom-call(f32[8,8,128]{2,1,0:T(8,128)} %copy-done.6, f32[8,8,128]{2,1,0:T(8,128)} %copy-done.4, f32[8,8,128]{2,1,0:T(8,128)} %copy-done.5, bf16[8,128,128]{2,1,0:T(8,128)(2,1)} %copy-done.3, f32[8,128,128]{2,1,0:T(8,128)} %get-tuple-element.27.in_mid_ref, ...), custom_call_target="tpu_custom_call" | custom-call | tf_op jit(solution)/shard_map/pallas_call | solution.py:464
  141.6 1.9 %collective-permute-start.10 = (f32[8,3,128]{2,1,0:T(4,128)}, f32[8,3,128]{2,1,0:T(4,128)S(1)}, u32[]{:S(2)}, u32[]{:S(2)}) collective-permute-start(f32[8,3,128]{2,1,0:T(4,128)} %get-tuple-element.32), channel_id=1, source_target_pairs={{0,1},{1,2},{2,3},{3,4},{4,5},{5,6},{6,7},{7,8},{8,9},{9,10},{10,1... | collective-permute-start | bytes 36872 | tf_op jit(solution)/shard_map/ppermute | solution.py:476
  143.5 6.3 %collective-permute-start.11 = (f32[8,3,128]{2,1,0:T(4,128)}, f32[8,3,128]{2,1,0:T(4,128)S(1)}, u32[]{:S(2)}, u32[]{:S(2)}) collective-permute-start(f32[8,3,128]{2,1,0:T(4,128)} %get-tuple-element.33), channel_id=1, source_target_pairs={{1,0},{2,1},{3,2},{4,3},{5,4},{6,5},{7,6},{8,7},{9,8},{10,9},{11,1... | collective-permute-start | bytes 36872 | tf_op jit(solution)/shard_map/ppermute | solution.py:476
  149.9 0.0 collective-permute-done.10.below_ref
  149.9 1.6 collective-permute-done.11.above_ref
  151.5 0.7 slice_add_fusion
  152.2 2.7 %collective-permute-start.13 = (f32[1,3,128]{2,1,0:T(4,128)S(1)}, f32[1,3,128]{2,1,0:T(4,128)S(1)}, u32[]{:S(2)}, u32[]{:S(2)}) collective-permute-start(f32[1,3,128]{2,1,0:T(4,128)S(1)} %get-tuple-element.38), channel_id=1, source_target_pairs={{32,0},{64,32},{96,64},{128,96},{160,128},{192,160},{224,192},{33,... | collective-permute-start | bytes 4616 | tf_op jit(solution)/shard_map/ppermute | solution.py:476
  155.0 7.0 %collective-permute-start.12 = (f32[1,3,128]{2,1,0:T(4,128)S(1)}, f32[1,3,128]{2,1,0:T(4,128)S(1)}, u32[]{:S(2)}, u32[]{:S(2)}) collective-permute-start(f32[1,3,128]{2,1,0:T(4,128)S(1)} %get-tuple-element.39), channel_id=1, source_target_pairs={{0,32},{32,64},{64,96},{96,128},{128,160},{160,192},{192,224},{1,3... | collective-permute-start | bytes 4616 | tf_op jit(solution)/shard_map/ppermute | solution.py:476
  162.0 0.0 collective-permute-done.13.right_ref
  162.0 3.3 %collective-permute-done.12.left_ref = f32[1,3,128]{2,1,0:T(4,128)S(1)} collective-permute-done((f32[1,3,128]{2,1,0:T(4,128)S(1)}, f32[1,3,128]{2,1,0:T(4,128)S(1)}, u32[]{:S(2)}, u32[]{:S(2)}) %collective-permute-start.12) | collective-permute-done | bytes 1568 | tf_op jit(solution)/shard_map/ppermute | solution.py:476
  165.3 0.0 copy-start.12
  165.3 0.6 copy-done.12
  165.8 1.4 shard_map.144
  167.2 1.3 copy.16
  (19 shorter events, 0.0 us)
Async XLA Ops:
  4.1 11.0 %collective-permute-start = (f32[1,8,128]{2,1,0:T(8,128)}, f32[1,8,128]{2,1,0:T(8,128)S(1)}, u32[]{:S(2)}, u32[]{:S(2)}) collective-permute-start(f32[1,8,128]{2,1,0:T(8,128)} %get-tuple-element.18), channel_id=1, source_target_pairs={{0,32},{32,64},{64,96},{96,128},{128,160},{160,192},{192,224},{1,3... | collective-permute-start | bytes 12296 | tf_op jit(solution)/shard_map/ppermute | solution.py:476
  13.1 9.7 %collective-permute-start.1 = (f32[1,8,128]{2,1,0:T(8,128)}, f32[1,8,128]{2,1,0:T(8,128)S(1)}, u32[]{:S(2)}, u32[]{:S(2)}) collective-permute-start(f32[1,8,128]{2,1,0:T(8,128)} %get-tuple-element.20), channel_id=1, source_target_pairs={{32,0},{64,32},{96,64},{128,96},{160,128},{192,160},{224,192},{33,... | collective-permute-start | bytes 12296 | tf_op jit(solution)/shard_map/ppermute | solution.py:476
  22.8 9.9 %copy-start.4 = (f32[8,8,128]{2,1,0:T(8,128)}, f32[8,8,128]{2,1,0:T(8,128)S(1)}, u32[]{:S(2)}) copy-start(f32[8,8,128]{2,1,0:T(8,128)S(1)} %constant_dynamic-update-slice_fusion.mid_ref) | copy-start | bytes 98308
  22.8 5.7 %collective-permute-start.3 = (f32[8,8,128]{2,1,0:T(8,128)S(1)}, f32[8,8,128]{2,1,0:T(8,128)S(1)}, u32[]{:S(2)}, u32[]{:S(2)}) collective-permute-start(f32[8,8,128]{2,1,0:T(8,128)S(1)} %constant_dynamic-update-slice_fusion.mid_ref), channel_id=1, source_target_pairs={{1,0},{2,1},{3,2},{4,3},{5,4},{6,5},{7,6},{8,7},{9,8},{10,9},{11,1... | collective-permute-start | bytes 98312 | tf_op jit(solution)/shard_map/ppermute | solution.py:476
  24.7 7.9 %collective-permute-start.2 = (f32[8,8,128]{2,1,0:T(8,128)S(1)}, f32[8,8,128]{2,1,0:T(8,128)S(1)}, u32[]{:S(2)}, u32[]{:S(2)}) collective-permute-start(f32[8,8,128]{2,1,0:T(8,128)S(1)} %constant_dynamic-update-slice_fusion.mid_ref), channel_id=1, source_target_pairs={{0,1},{1,2},{2,3},{3,4},{4,5},{5,6},{6,7},{7,8},{8,9},{9,10},{10,1... | collective-permute-start | bytes 98312 | tf_op jit(solution)/shard_map/ppermute | solution.py:476
  28.5 4.2 %copy-start.5 = (f32[8,8,128]{2,1,0:T(8,128)}, f32[8,8,128]{2,1,0:T(8,128)S(1)}, u32[]{:S(2)}) copy-start(f32[8,8,128]{2,1,0:T(8,128)S(1)} %collective-permute-done.3.hi_ref) | copy-start | bytes 98308
  32.7 0.6 copy-start.6
  59.1 10.7 %collective-permute-start.4 = (bf16[8,128,128]{2,1,0:T(8,128)(2,1)}, bf16[8,128,128]{2,1,0:T(8,128)(2,1)S(1)}, u32[]{:S(2)}, u32[]{:S(2)}) collective-permute-start(bf16[8,128,128]{2,1,0:T(8,128)(2,1)} %get-tuple-element.22), channel_id=1, source_target_pairs={{0,1},{1,2},{2,3},{3,4},{4,5},{5,6},{6,7},{7,8},{8,9},{9,10},{10,1... | collective-permute-start | bytes 786440 | tf_op jit(solution)/shard_map/ppermute | solution.py:476
  61.1 12.7 %collective-permute-start.5 = (bf16[8,128,128]{2,1,0:T(8,128)(2,1)}, bf16[8,128,128]{2,1,0:T(8,128)(2,1)S(1)}, u32[]{:S(2)}, u32[]{:S(2)}) collective-permute-start(bf16[8,128,128]{2,1,0:T(8,128)(2,1)} %get-tuple-element.23), channel_id=1, source_target_pairs={{1,0},{2,1},{3,2},{4,3},{5,4},{6,5},{7,6},{8,7},{9,8},{10,9},{11,1... | collective-permute-start | bytes 786440 | tf_op jit(solution)/shard_map/ppermute | solution.py:476
  69.8 18.7 %copy-start = (bf16[8,128,128]{2,1,0:T(8,128)(2,1)}, bf16[8,128,128]{2,1,0:T(8,128)(2,1)S(1)}, u32[]{:S(2)}) copy-start(bf16[8,128,128]{2,1,0:T(8,128)(2,1)S(1)} %collective-permute-done.4.below_ref) | copy-start | bytes 786436
  73.7 14.9 %copy-start.1 = (bf16[8,128,128]{2,1,0:T(8,128)(2,1)}, bf16[8,128,128]{2,1,0:T(8,128)(2,1)S(1)}, u32[]{:S(2)}) copy-start(bf16[8,128,128]{2,1,0:T(8,128)(2,1)S(1)} %collective-permute-done.5.above_ref) | copy-start | bytes 786436
  74.8 10.1 %collective-permute-start.7 = (bf16[2,128,128]{2,1,0:T(8,128)(2,1)S(1)}, bf16[2,128,128]{2,1,0:T(8,128)(2,1)S(1)}, u32[]{:S(2)}, u32[]{:S(2)}) collective-permute-start(bf16[2,128,128]{2,1,0:T(8,128)(2,1)S(1)} %get-tuple-element.36), channel_id=1, source_target_pairs={{32,0},{64,32},{96,64},{128,96},{160,128},{192,160},{224,192},{33,... | collective-permute-start | bytes 196616 | tf_op jit(solution)/shard_map/ppermute | solution.py:476
  77.6 11.0 %collective-permute-start.6 = (bf16[2,128,128]{2,1,0:T(8,128)(2,1)S(1)}, bf16[2,128,128]{2,1,0:T(8,128)(2,1)S(1)}, u32[]{:S(2)}, u32[]{:S(2)}) collective-permute-start(bf16[2,128,128]{2,1,0:T(8,128)(2,1)S(1)} %get-tuple-element.37), channel_id=1, source_target_pairs={{0,32},{32,64},{64,96},{96,128},{128,160},{160,192},{192,224},{1,3... | collective-permute-start | bytes 196616 | tf_op jit(solution)/shard_map/ppermute | solution.py:476
  84.9 3.7 %copy-start.7 = (bf16[2,128,128]{2,1,0:T(8,128)(2,1)}, bf16[2,128,128]{2,1,0:T(8,128)(2,1)S(1)}, u32[]{:S(2)}) copy-start(bf16[2,128,128]{2,1,0:T(8,128)(2,1)S(1)} %collective-permute-done.7.right_ref) | copy-start | bytes 196612
  88.6 0.6 copy-start.8
  92.4 10.6 %collective-permute-start.9 = (bf16[8,128,128]{2,1,0:T(8,128)(2,1)}, bf16[8,128,128]{2,1,0:T(8,128)(2,1)S(1)}, u32[]{:S(2)}, u32[]{:S(2)}) collective-permute-start(bf16[8,128,128]{2,1,0:T(8,128)(2,1)} %get-tuple-element.26), channel_id=1, source_target_pairs={{1,0},{2,1},{3,2},{4,3},{5,4},{6,5},{7,6},{8,7},{9,8},{10,9},{11,1... | collective-permute-start | bytes 786440 | tf_op jit(solution)/shard_map/ppermute | solution.py:476
  97.1 10.6 %collective-permute-start.8 = (bf16[8,128,128]{2,1,0:T(8,128)(2,1)}, bf16[8,128,128]{2,1,0:T(8,128)(2,1)S(1)}, u32[]{:S(2)}, u32[]{:S(2)}) collective-permute-start(bf16[8,128,128]{2,1,0:T(8,128)(2,1)} %get-tuple-element.26), channel_id=1, source_target_pairs={{0,1},{1,2},{2,3},{3,4},{4,5},{5,6},{6,7},{7,8},{8,9},{9,10},{10,1... | collective-permute-start | bytes 786440 | tf_op jit(solution)/shard_map/ppermute | solution.py:476
  103.1 4.6 %copy-start.2 = (bf16[8,128,128]{2,1,0:T(8,128)(2,1)}, bf16[8,128,128]{2,1,0:T(8,128)(2,1)S(1)}, u32[]{:S(2)}) copy-start(bf16[8,128,128]{2,1,0:T(8,128)(2,1)S(1)} %collective-permute-done.9.in_hi_ref) | copy-start | bytes 786436
  107.7 0.7 copy-start.3
  141.6 8.3 %collective-permute-start.10 = (f32[8,3,128]{2,1,0:T(4,128)}, f32[8,3,128]{2,1,0:T(4,128)S(1)}, u32[]{:S(2)}, u32[]{:S(2)}) collective-permute-start(f32[8,3,128]{2,1,0:T(4,128)} %get-tuple-element.32), channel_id=1, source_target_pairs={{0,1},{1,2},{2,3},{3,4},{4,5},{5,6},{6,7},{7,8},{8,9},{9,10},{10,1... | collective-permute-start | bytes 36872 | tf_op jit(solution)/shard_map/ppermute | solution.py:476
  143.5 8.0 %collective-permute-start.11 = (f32[8,3,128]{2,1,0:T(4,128)}, f32[8,3,128]{2,1,0:T(4,128)S(1)}, u32[]{:S(2)}, u32[]{:S(2)}) collective-permute-start(f32[8,3,128]{2,1,0:T(4,128)} %get-tuple-element.33), channel_id=1, source_target_pairs={{1,0},{2,1},{3,2},{4,3},{5,4},{6,5},{7,6},{8,7},{9,8},{10,9},{11,1... | collective-permute-start | bytes 36872 | tf_op jit(solution)/shard_map/ppermute | solution.py:476
  149.9 15.3 %copy-start.9 = (f32[8,3,128]{2,1,0:T(4,128)}, f32[8,3,128]{2,1,0:T(4,128)S(1)}, u32[]{:S(2)}) copy-start(f32[8,3,128]{2,1,0:T(4,128)S(1)} %collective-permute-done.10.below_ref) | copy-start | bytes 36868
  151.5 13.7 %copy-start.10 = (f32[8,3,128]{2,1,0:T(4,128)}, f32[8,3,128]{2,1,0:T(4,128)S(1)}, u32[]{:S(2)}) copy-start(f32[8,3,128]{2,1,0:T(4,128)S(1)} %collective-permute-done.11.above_ref) | copy-start | bytes 36868
  152.2 9.8 %collective-permute-start.13 = (f32[1,3,128]{2,1,0:T(4,128)S(1)}, f32[1,3,128]{2,1,0:T(4,128)S(1)}, u32[]{:S(2)}, u32[]{:S(2)}) collective-permute-start(f32[1,3,128]{2,1,0:T(4,128)S(1)} %get-tuple-element.38), channel_id=1, source_target_pairs={{32,0},{64,32},{96,64},{128,96},{160,128},{192,160},{224,192},{33,... | collective-permute-start | bytes 4616 | tf_op jit(solution)/shard_map/ppermute | solution.py:476
  155.0 10.3 %collective-permute-start.12 = (f32[1,3,128]{2,1,0:T(4,128)S(1)}, f32[1,3,128]{2,1,0:T(4,128)S(1)}, u32[]{:S(2)}, u32[]{:S(2)}) collective-permute-start(f32[1,3,128]{2,1,0:T(4,128)S(1)} %get-tuple-element.39), channel_id=1, source_target_pairs={{0,32},{32,64},{64,96},{96,128},{128,160},{160,192},{192,224},{1,3... | collective-permute-start | bytes 4616 | tf_op jit(solution)/shard_map/ppermute | solution.py:476
  162.0 3.3 %copy-start.11 = (f32[1,3,128]{2,1,0:T(4,128)}, f32[1,3,128]{2,1,0:T(4,128)S(1)}, u32[]{:S(2)}) copy-start(f32[1,3,128]{2,1,0:T(4,128)S(1)} %collective-permute-done.13.right_ref) | copy-start | bytes 4612
  165.3 0.6 copy-start.12

commit v3 on v2

v3 whole, which is shorter than its diff:
```python
import jax
import jax.numpy as jnp
from jax import lax
from jax.experimental import pallas as pl
from jax.experimental.pallas import tpu as pltpu
from jax.sharding import PartitionSpec as P

BX = 6
EX = 8
A = 128
C = 128
K = 4
ROWS = 16
F32 = jnp.float32
BF16 = jnp.bfloat16
SIGMA = 1.5
NT = (((1,), (1,)), ((), ()))
E = 3 * EX

HOME_PAIRS = [
    [(h, (o % 3) * EX + h + o // 3, EX + 1 + h, o) for h in range(BX) for o in range(9) if (o % 3 == 1) == inner]
    for inner in (False, True)
]
FAR_PAIRS = [
    [
        (f, (2 - o % 3) * EX + f + 2 - o // 3, (2 - o % 3) * EX + f + 2 - o // 3, o)
        for f in range(BX)
        for o in range(9)
        if (o % 3 == 1) == inner
    ]
    for inner in (False, True)
]
MIDDLE, END = 62, 63


def dot(a, b):
    return jnp.dot(a, b, preferred_element_type=F32)


def dot_nt(a, b):
    return lax.dot_general(a, b, NT, preferred_element_type=F32)


def pack_kernel(pos_ref, species_ref, codes_ref, count_ref, first_ref, out_ref, last_ref):
    block_id = lax.broadcasted_iota(jnp.int32, (8, 128), 0)
    mask = jnp.zeros((8, 128), jnp.int32)
    for p in range(codes_ref.shape[2]):
        code = codes_ref[0, 0, p]
        block = lax.shift_right_logical(code * 57, 9)
        bit = jnp.where(p < count_ref[0, 0], lax.shift_left(1, code - 9 * block), 0)
        mask = mask + jnp.where(block_id == block, bit, 0)
    mask = mask.astype(F32)
    for h in range(BX):
        places = [(out_ref, h)]
        if h == 0:
            places.append((first_ref, 0))
        if h == BX - 1:
            places.append((last_ref, 0))
        for ref, i in places:
            for d in range(3):
                ref[i, d : d + 1, :] = pos_ref[h, d]
            ref[i, 3:4, :] = species_ref[h].astype(F32)
            ref[i, 4:5, :] = mask[h : h + 1, :]
            ref[i, 5:8, :] = jnp.zeros((3, 128), F32)


def gather_ext(lo_ref, mid_ref, hi_ref, ext_ref):
    for row, ref in enumerate((lo_ref, mid_ref, hi_ref)):
        for x in range(EX):
            ext_ref[row * EX + x] = ref[x]
    ext_ref[E : E + 8] = jnp.full((8, 8, A), 1.0e4, F32)


def send_masks(ext_ref, maskv_ref, masks_ref, sem):
    for e in range(E):
        maskv_ref[e : e + 1, :] = ext_ref[e, 4:5, :].astype(jnp.int32)
    copy = pltpu.make_async_copy(maskv_ref, masks_ref, sem)
    copy.start()
    return copy


def make_list(parts, masks_ref, list_ref):
    n = jnp.int32(0)
    for pairs, place in zip(parts, (MIDDLE, END)):
        held = None
        for own, other, lister, o in sorted(pairs, key=lambda pair: pair[2]):
            if lister != held:
                held, mask = lister, masks_ref[lister, 0]
            list_ref[n] = own + other * 8 + (256 if o == 4 else 0)
            n = n + (lax.shift_right_logical(mask, o) & 1)
        for i in range(3):
            list_ref[n + i] = E * 8
        n = n + (n & 1)
        list_ref[place] = n


def entry(list_ref, p):
    code = list_ref[p]
    own = code & 7
    other = lax.shift_right_logical(code, 3) & 31
    bias = jnp.where(code >= 256, 0, 1024)
    return own, other, bias


def turned_blocks(ext_ref):
    return [ext_ref[0:16].reshape(128, A).T, ext_ref[16:32].reshape(128, A).T]


def spread_lane(turned, e, d):
    lane = 8 * (e % 16) + d
    return jnp.broadcast_to(turned[e // 16][:, lane : lane + 1], (A, 128))


def geometry(col_ref, i, row, r, sign, bias, rows=ROWS):
    off = [sign * (row[d] - col_ref[i, d, pl.ds(r, rows), :]) for d in range(3)]
    squared = off[0] * off[0] + off[1] * off[1] + off[2] * off[2]
    soft = squared + 0.25
    inv = lax.rsqrt(soft)
    s = soft * inv
    taper = jnp.maximum(1.0 - squared * (1.0 / 36.0), 0.0)
    at = lax.broadcasted_iota(jnp.int32, (rows, 128), 0) + (r + bias)
    lane = lax.broadcasted_iota(jnp.int32, (rows, 128), 1)
    taper = jnp.where(at == lane, 0.0, taper)
    u = jnp.minimum(s, 6.25) * (1.0 / SIGMA) - 0.5
    base = taper * jnp.exp(-u * u)
    step = jnp.exp(2.0 * u - 1.0)
    q = [base]
    for k in range(1, K):
        q.append(q[-1] * (step * EXPS[k]))
    return off, inv, taper, u, q


EXPS = [1.0, 1.0, 0.1353352832366127, 0.01831563888873418]


def store_tiles(put, off, inv, taper, q):
    direction = [o * inv for o in off]
    for k in range(K):
        radial = taper * q[k]
        put(0, k, radial.astype(BF16))
        for d in range(3):
            put(1 + d, k, (radial * direction[d]).astype(BF16))


def pull_back(grads, off, inv, taper, u, q):
    direction = [o * inv for o in off]
    s0 = s1 = None
    dg = [None] * 3
    for k in reversed(range(K)):
        tilted = [grads(1 + d, k) for d in range(3)]
        along = tilted[0] * direction[0] + tilted[1] * direction[1] + tilted[2] * direction[2]
        p = (grads(0, k) + along) * q[k]
        s0 = p if s0 is None else s0 + p
        if k:
            s1 = s0 if s1 is None else s1 + s0
        for d in range(3):
            v = tilted[d] * q[k]
            dg[d] = v if dg[d] is None else dg[d] + v
    turn = dg[0] * direction[0] + dg[1] * direction[1] + dg[2] * direction[2]
    bend = (2.0 / SIGMA) * (u * s0 - s1) + turn * inv
    pull = taper * inv
    weight = s0 * (1.0 / 9.0) + pull * bend
    return [dg[d] * pull - weight * off[d] for d in range(3)]


def rows_of(ext_ref, e):
    return [ext_ref[e, d : d + 1, :] for d in range(3)]


def scaled(feature, weights_ref, k):
    return (feature.astype(F32) * weights_ref[k : k + 1, :]).astype(BF16)


def forward_kernel(
    lo_ref, mid_ref, hi_ref, radial_ref, square_ref,
    pre_ref, feat_ref, out_lo_ref, out_hi_ref, scaled_s_ref, scaled_v_ref, ready_ref, keep_col_ref,
    list1_ref, list2_ref,
    ext_ref, col_ref, init_ref, acc_ref, tile_a_ref, tile_b_ref, wide_a_ref, wide_b_ref, total_ref,
    maskv_ref, masks_ref, sem,
):
    ws1_ref, wv1_ref, ws2_ref, wv2_ref, _ = radial_parts(radial_ref)
    ms_ref, mv_ref, _, table_ref = square_parts(square_ref)
    gather_ext(lo_ref, mid_ref, hi_ref, ext_ref)
    copy = send_masks(ext_ref, maskv_ref, masks_ref, sem)
    turned = turned_blocks(ext_ref)
    lanes = lax.broadcasted_iota(jnp.int32, (A, 128), 1).astype(F32)
    for e in range(E):
        if e == 8:
            copy.wait()
            make_list(HOME_PAIRS, masks_ref, list1_ref)
            make_list(FAR_PAIRS, masks_ref, list2_ref)
        for d in range(3):
            column = spread_lane(turned, e, d)
            col_ref[e, d] = column
            if EX <= e < 2 * EX:
                keep_col_ref[e - EX, d] = column
        hot = (spread_lane(turned, e, 3) == lanes).astype(BF16)
        init_ref[e] = dot(hot, table_ref[...]).astype(BF16)
    col_ref[E] = jnp.full((3, A, 128), 1.0e4, F32)
    keep_col_ref[EX] = jnp.full((3, A, 128), 1.0e4, F32)

    def scale_block(e, carry):
        for k in range(K):
            scaled_s_ref[e, pl.ds(k * A, A), :] = scaled(init_ref[e], ws1_ref, k)
            scaled_v_ref[e, pl.ds(k * A, A), :] = scaled(init_ref[e], wv1_ref, k)
        return carry

    lax.fori_loop(0, E, scale_block, 0)
    scaled_s_ref[E] = jnp.zeros((K * A, C), BF16)
    scaled_v_ref[E] = jnp.zeros((K * A, C), BF16)
    acc_ref[...] = jnp.zeros_like(acc_ref)
    total_ref[...] = jnp.zeros_like(total_ref)

    def first_tiles(p, tile_ref, r):
        own, other, bias = entry(list1_ref, p)
        row = rows_of(ext_ref, other)
        off, inv, taper, u, q = geometry(col_ref, own + EX + 1, row, r, 1.0, bias)

        def put(g, k, tile):
            tile_ref[pl.ds(g * A + r, ROWS), pl.ds(k * A, A)] = tile

        store_tiles(put, off, inv, taper, q)

    def first_sum(p, tile_ref, g):
        own, other, _ = entry(list1_ref, p)
        part = pl.ds(g * A, A)
        acc_ref[own, part, :] += dot(tile_ref[part, :], (scaled_v_ref if g else scaled_s_ref)[other])

    def first_half(p, this_ref, next_ref):
        for g in range(4):
            first_sum(p, this_ref, g)
            for r in range(g * 32, g * 32 + 32, ROWS):
                first_tiles(p + 1, next_ref, r)

    def first(i, carry):
        first_half(2 * i, tile_a_ref, tile_b_ref)
        first_half(2 * i + 1, tile_b_ref, tile_a_ref)
        return carry

    for r in range(0, A, ROWS):
        first_tiles(0, tile_a_ref, r)
    lax.fori_loop(0, half(list1_ref[END]), first, 0)

    for h in range(BX):
        pre = dot((acc_ref[h, 0:A, :] * 0.125).astype(BF16), ms_ref[...])
        pre_ref[h] = pre
        scalar = (init_ref[h + EX + 1].astype(F32) + pre * jax.nn.sigmoid(pre)).astype(BF16)
        vector = dot((acc_ref[h, A : 4 * A, :] * 0.125).astype(BF16), mv_ref[...]).astype(BF16)
        feat_ref[h, 0:A, :] = scalar
        feat_ref[h, A : 4 * A, :] = vector
        for k in range(K):
            ready_ref[h, pl.ds(k * A, A), :] = scaled(scalar, ws2_ref, k)
            for d in range(3):
                ready_ref[h, pl.ds(((1 + d) * K + k) * A, A), :] = scaled(
                    vector[d * A : (d + 1) * A, :], wv2_ref, k
                )
    second_sums(
        0, list2_ref[MIDDLE], list2_ref, col_ref, 0, lambda own: rows_of(ext_ref, own + EX + 1),
        ready_ref, total_ref, wide_a_ref, wide_b_ref,
    )
    for x in range(EX):
        out_lo_ref[x] = total_ref[x].astype(BF16)
        out_hi_ref[x] = total_ref[2 * EX + x].astype(BF16)


def place(other, shift):
    return jnp.minimum(other - shift, EX) if shift else other


def second_sums(
    start, end, list_ref, col_ref, shift, rows, ready_ref, total_ref, wide_a_ref, wide_b_ref
):
    def second_tiles(p, wide_ref, r):
        own, other, bias = entry(list_ref, p)
        row = rows(own)
        off, inv, taper, u, q = geometry(col_ref, place(other, shift), row, r, 1.0, bias)

        def put(g, k, tile):
            wide_ref[pl.ds(r, ROWS), pl.ds((g * K + k) * A, A)] = tile

        store_tiles(put, off, inv, taper, q)

    def second_half(p, this_ref, next_ref):
        own, other, _ = entry(list_ref, p)
        for g in range(4):
            part = pl.ds(g * K * A, K * A)
            total_ref[place(other, shift)] += dot(this_ref[:, part], ready_ref[own, part, :])
            for r in range(g * 32, g * 32 + 32, ROWS):
                second_tiles(p + 1, next_ref, r)

    def second(i, carry):
        second_half(2 * i, wide_a_ref, wide_b_ref)
        second_half(2 * i + 1, wide_b_ref, wide_a_ref)
        return carry

    for r in range(0, A, ROWS):
        second_tiles(start, wide_a_ref, r)
    lax.fori_loop(half(start), half(end), second, 0)


def forward_inner_kernel(
    mid_ref, list2_ref, ready_ref, col_ref, out_ref, wide_a_ref, wide_b_ref, total_ref
):
    total_ref[...] = jnp.zeros_like(total_ref)
    second_sums(
        list2_ref[MIDDLE], list2_ref[END], list2_ref, col_ref, EX,
        lambda own: rows_of(mid_ref, own + 1), ready_ref, total_ref, wide_a_ref, wide_b_ref,
    )
    out_ref[...] = total_ref[0:EX]


def radial_parts(ref):
    return [ref.at[pl.ds(K * i, K if i < 4 else 1), :] for i in range(5)]


def square_parts(ref):
    return [ref.at[pl.ds(C * i, C), :] for i in range(4)]


def half(n):
    return lax.shift_right_logical(n, 1)


def slope_of(value):
    sigma = jax.nn.sigmoid(value)
    return sigma * (1.0 + value * (1.0 - sigma))


def middle_kernel(
    mid_ref, below_ref, above_ref, left_ref, right_ref, feat_ref, radial_ref, square_ref,
    energy_ref, second_in_ref, second_own_ref,
):
    readout_ref = radial_parts(radial_ref)[4]
    mix_ref = square_parts(square_ref)[2]
    for x in range(EX):
        msg = mid_ref[x] + below_ref[x].astype(F32) + above_ref[x].astype(F32)
        if x < 2:
            msg = msg + left_ref[x].astype(F32)
        if x >= EX - 2:
            msg = msg + right_ref[x - EX + 2].astype(F32)
        pre = dot((msg * 0.125).astype(BF16), mix_ref[...])
        sigma = jax.nn.sigmoid(pre)
        if 1 <= x <= BX:
            part = (feat_ref[x - 1, 0:A, :].astype(F32) + pre * sigma) * readout_ref[...]
            energy_ref[x - 1] = jnp.sum(part.T, axis=0, keepdims=True)
        grad = (readout_ref[...] * (sigma * (1.0 + pre * (1.0 - sigma)))).astype(BF16)
        second = dot_nt(grad, mix_ref[...]) * 0.125
        second_own_ref[x] = second
        second_in_ref[x] = second.astype(BF16)


def move(across_ref, own, r, near, own_sign, grad_ref):
    def grads(g, k):
        return grad_ref[pl.ds(g * A + r, ROWS), pl.ds(k * A, A)]

    parts = []
    for d, moved in enumerate(pull_back(grads, *near)):
        if own_sign > 0:
            across_ref[own, d, pl.ds(r, ROWS), :] += moved
        else:
            across_ref[own, d, pl.ds(r, ROWS), :] -= moved
        part = moved[0:8]
        for i in range(8, ROWS, 8):
            part = part + moved[i : i + 8]
        parts.append(part)
    return parts


def add_down(down_ref, other, own_sign, sums):
    for d in range(3):
        down_ref[other, d] -= own_sign * sums[d]


def plus(sums, parts):
    return parts if sums is None else [a + b for a, b in zip(sums, parts)]


def first_moves(
    start, end, list_ref, col_ref, shift, rows, inward_ref, scaled_s_ref, scaled_v_ref, across_ref,
    down_ref, grad_a_ref, grad_b_ref,
):
    def first_grads(p, grad_ref):
        own, other, _ = entry(list_ref, p)
        grad_ref[0:A, :] = dot_nt(inward_ref[own, 0:A, :], scaled_s_ref[other])
        grad_ref[A : 4 * A, :] = dot_nt(inward_ref[own, A : 4 * A, :], scaled_v_ref[other])

    def first_move(p, grad_ref):
        own, other, bias = entry(list_ref, p)
        row = rows(place(other, shift))
        sums = None
        for r in range(0, A, ROWS):
            near = geometry(col_ref, own + 1, row, r, 1.0, bias)
            sums = plus(sums, move(across_ref, own, r, near, -1.0, grad_ref))
        add_down(down_ref, place(other, shift), -1.0, sums)

    def first_back(i, carry):
        p = 2 * i
        first_grads(p + 1, grad_b_ref)
        first_move(p, grad_a_ref)
        first_grads(p + 2, grad_a_ref)
        first_move(p + 1, grad_b_ref)
        return carry

    first_grads(start, grad_a_ref)
    lax.fori_loop(half(start), half(end), first_back, 0)


def line_of(down_ref, across_ref, e, x, d):
    line = jnp.sum(down_ref[e, d], axis=0, keepdims=True)
    if x is not None and 1 <= x <= BX:
        line = line + jnp.sum(across_ref[x - 1, d].T, axis=0, keepdims=True)
    return line


def second_moves(
    start, end, list_ref, col_ref, shift, rows, feat_ref, cot_s_ref, cot_v_ref, acc_ref, across_ref,
    down_ref, tile_a_ref, tile_b_ref, grad_a_ref, grad_b_ref,
):
    def second_grads(p, grad_ref):
        own, other, _ = entry(list_ref, p)
        source = place(other, shift)
        grad_ref[0:A, :] = dot_nt(feat_ref[own, 0:A, :], cot_s_ref[source])
        grad_ref[A : 4 * A, :] = dot_nt(feat_ref[own, A : 4 * A, :], cot_v_ref[source])

    def second_move(p, grad_ref, tile_ref):
        own, other, bias = entry(list_ref, p)
        source = place(other, shift)
        row = rows(source)
        sums = None
        for r in range(0, A, ROWS):
            near = geometry(col_ref, own + 1, row, r, -1.0, bias)
            off, inv, taper, u, q = near

            def put(g, k, tile):
                tile_ref[pl.ds(g * A + r, ROWS), pl.ds(k * A, A)] = tile

            store_tiles(put, off, inv, taper, q)
            sums = plus(sums, move(across_ref, own, r, near, 1.0, grad_ref))
        add_down(down_ref, source, 1.0, sums)

    def second_sum(own, source, tile_ref):
        acc_ref[own, 0:A, :] += dot(tile_ref[0:A, :], cot_s_ref[source])
        acc_ref[own, A : 4 * A, :] += dot(tile_ref[A : 4 * A, :], cot_v_ref[source])

    def second_back(i, carry):
        p = 2 * i
        own, other, _ = entry(list_ref, p)
        second_sum(*carry, tile_b_ref)
        second_grads(p + 1, grad_b_ref)
        second_move(p, grad_a_ref, tile_a_ref)
        second_sum(own, place(other, shift), tile_a_ref)
        second_grads(p + 2, grad_a_ref)
        second_move(p + 1, grad_b_ref, tile_b_ref)
        own, other, _ = entry(list_ref, p + 1)
        return own, place(other, shift)

    empty = EX if shift else E
    for ref in (cot_s_ref, cot_v_ref):
        ref[empty] = jnp.zeros((K * A, C), BF16)
    tile_b_ref[...] = jnp.zeros_like(tile_b_ref)
    second_grads(start, grad_a_ref)
    last = lax.fori_loop(half(start), half(end), second_back, (jnp.int32(0), jnp.int32(empty)))
    second_sum(*last, tile_b_ref)


def cotangents(ref, cot_s_ref, cot_v_ref, first, ws2_ref, wv2_ref):
    def cot_block(x, carry):
        for k in range(K):
            cot_s_ref[first + x, pl.ds(k * A, A), :] = scaled(ref[x], ws2_ref, k)
            cot_v_ref[first + x, pl.ds(k * A, A), :] = scaled(ref[x], wv2_ref, k)
        return carry

    lax.fori_loop(0, EX, cot_block, 0)


def backward_inner_two_kernel(
    mid_ref, list2_ref, in_mid_ref, feat_ref, col_ref, radial_ref,
    acc_ref, across_ref, down_ref,
    ext_ref, cot_s_ref, cot_v_ref, tile_a_ref, tile_b_ref, grad_a_ref, grad_b_ref,
):
    _, _, ws2_ref, wv2_ref, _ = radial_parts(radial_ref)
    for x in range(EX):
        ext_ref[x] = mid_ref[x]
    ext_ref[EX] = jnp.full((8, A), 1.0e4, F32)
    acc_ref[...] = jnp.zeros_like(acc_ref)
    down_ref[...] = jnp.zeros_like(down_ref)
    across_ref[...] = jnp.zeros_like(across_ref)
    cotangents(in_mid_ref, cot_s_ref, cot_v_ref, 0, ws2_ref, wv2_ref)
    second_moves(
        list2_ref[MIDDLE], list2_ref[END], list2_ref, col_ref, EX, lambda e: rows_of(ext_ref, e),
        feat_ref, cot_s_ref, cot_v_ref, acc_ref, across_ref, down_ref, tile_a_ref, tile_b_ref,
        grad_a_ref, grad_b_ref,
    )


def backward_kernel(
    lo_ref, mid_ref, hi_ref, list1_ref, list2_ref, acc_in_ref, across_in_ref, down_in_ref, feat_ref,
    pre_ref, in_lo_ref, in_hi_ref, scaled_s_ref, scaled_v_ref, col_ref, radial_ref, square_ref,
    out_lo_ref, out_mid_ref, out_hi_ref, inward_ref,
    ext_ref, cot_s_ref, cot_v_ref, acc_ref, tile_a_ref, tile_b_ref, grad_a_ref, grad_b_ref,
    down_ref, across_ref,
):
    _, _, ws2_ref, wv2_ref, readout_ref = radial_parts(radial_ref)
    ms_ref, mv_ref, _, _ = square_parts(square_ref)
    gather_ext(lo_ref, mid_ref, hi_ref, ext_ref)
    acc_ref[...] = acc_in_ref[...]
    across_ref[...] = across_in_ref[...]
    down_ref[0:EX] = jnp.zeros((EX, 3, 8, A), F32)
    down_ref[EX : 2 * EX] = down_in_ref[0:EX]
    down_ref[2 * EX : E + 1] = jnp.zeros((EX + 1, 3, 8, A), F32)
    cotangents(in_lo_ref, cot_s_ref, cot_v_ref, 0, ws2_ref, wv2_ref)
    cotangents(in_hi_ref, cot_s_ref, cot_v_ref, 2 * EX, ws2_ref, wv2_ref)
    second_moves(
        0, list2_ref[MIDDLE], list2_ref, col_ref, 0, lambda e: rows_of(ext_ref, e), feat_ref,
        cot_s_ref, cot_v_ref, acc_ref, across_ref, down_ref, tile_a_ref, tile_b_ref, grad_a_ref,
        grad_b_ref,
    )
    for h in range(BX):
        slope = (readout_ref[...] + acc_ref[h, 0:A, :]) * slope_of(pre_ref[h])
        inward_ref[h, 0:A, :] = (dot_nt(slope.astype(BF16), ms_ref[...]) * 0.125).astype(BF16)
        inward_ref[h, A : 4 * A, :] = (
            dot_nt(acc_ref[h, A : 4 * A, :].astype(BF16), mv_ref[...]) * 0.125
        ).astype(BF16)
    first_moves(
        0, list1_ref[MIDDLE], list1_ref, col_ref, 0, lambda e: rows_of(ext_ref, e), inward_ref,
        scaled_s_ref, scaled_v_ref, across_ref, down_ref, grad_a_ref, grad_b_ref,
    )
    for row, ref in enumerate((out_lo_ref, out_mid_ref, out_hi_ref)):
        for x in range(EX):
            for d in range(3):
                line = line_of(down_ref, across_ref, row * EX + x, x if row == 1 else None, d)
                ref[x, d : d + 1, :] = line


def backward_inner_kernel(
    mid_ref, list1_ref, scaled_s_ref, scaled_v_ref, col_ref, inward_ref, out_ref,
    ext_ref, grad_a_ref, grad_b_ref, down_ref, across_ref,
):
    for x in range(EX):
        ext_ref[x] = mid_ref[x]
    ext_ref[EX] = jnp.full((8, A), 1.0e4, F32)
    down_ref[...] = jnp.zeros_like(down_ref)
    across_ref[...] = jnp.zeros_like(across_ref)
    first_moves(
        list1_ref[MIDDLE], list1_ref[END], list1_ref, col_ref, EX, lambda e: rows_of(ext_ref, e),
        inward_ref, scaled_s_ref, scaled_v_ref, across_ref, down_ref, grad_a_ref, grad_b_ref,
    )
    for x in range(EX):
        for d in range(3):
            out_ref[x, d : d + 1, :] = line_of(down_ref, across_ref, x, x, d)


ANY = pl.BlockSpec(memory_space=pl.ANY)
VMEM = pl.BlockSpec(memory_space=pltpu.VMEM)
SMEM = pl.BlockSpec(memory_space=pltpu.SMEM)
PARAMS = pltpu.CompilerParams(vmem_limit_bytes=24 * 1024 * 1024)


SEM = pltpu.SemaphoreType.DMA


def forward_call(*args):
    return call(
        forward_kernel,
        args,
        [
            ((BX, A, C), F32),
            ((BX, 4 * A, C), BF16),
            ((EX, A, C), BF16),
            ((EX, A, C), BF16),
            ((E + 1, K * A, C), BF16),
            ((E + 1, K * A, C), BF16),
            ((BX, 4 * K * A, C), BF16),
            ((EX + 1, 3, A, 128), F32),
            ((64,), jnp.int32),
            ((64,), jnp.int32),
        ],
        [
            pltpu.VMEM((E + 8, 8, A), F32),
            pltpu.VMEM((E + 1, 3, A, 128), F32),
            pltpu.VMEM((E, A, C), BF16),
            pltpu.VMEM((BX, 4 * A, C), F32),
            pltpu.VMEM((4 * A, K * A), BF16),
            pltpu.VMEM((4 * A, K * A), BF16),
            pltpu.VMEM((A, 4 * K * A), BF16),
            pltpu.VMEM((A, 4 * K * A), BF16),
            pltpu.VMEM((E + 1, A, C), F32),
            pltpu.VMEM((E, 128), jnp.int32),
            pltpu.SMEM((E, 128), jnp.int32),
            SEM,
        ],
        out_specs=[VMEM] * 8 + [SMEM] * 2,
    )


def forward_inner_call(*args):
    return call(
        forward_inner_kernel,
        args,
        [((EX, A, C), F32)],
        [
            pltpu.VMEM((A, 4 * K * A), BF16),
            pltpu.VMEM((A, 4 * K * A), BF16),
            pltpu.VMEM((EX + 1, A, C), F32),
        ],
        in_specs=[VMEM, SMEM, VMEM, VMEM],
        cost=pl.CostEstimate(flops=4 * 10**9, bytes_accessed=10**6, transcendentals=0),
    )


def backward_inner_two_call(*args):
    return call(
        backward_inner_two_kernel,
        args,
        [((BX, 4 * A, C), F32), ((BX, 3, A, 128), F32), ((EX + 1, 3, 8, A), F32)],
        [
            pltpu.VMEM((EX + 1, 8, A), F32),
            pltpu.VMEM((EX + 1, K * A, C), BF16),
            pltpu.VMEM((EX + 1, K * A, C), BF16),
            pltpu.VMEM((4 * A, K * A), BF16),
            pltpu.VMEM((4 * A, K * A), BF16),
            pltpu.VMEM((4 * A, K * A), F32),
            pltpu.VMEM((4 * A, K * A), F32),
        ],
        in_specs=[VMEM, SMEM, VMEM, VMEM, VMEM, VMEM],
        cost=pl.CostEstimate(flops=4 * 10**9, bytes_accessed=10**6, transcendentals=0),
    )


def backward_call(*args):
    return call(
        backward_kernel,
        args,
        [*[((EX, 3, A), F32)] * 3, ((BX, 4 * A, C), BF16)],
        [
            pltpu.VMEM((E + 8, 8, A), F32),
            pltpu.VMEM((E + 1, K * A, C), BF16),
            pltpu.VMEM((E + 1, K * A, C), BF16),
            pltpu.VMEM((BX, 4 * A, C), F32),
            pltpu.VMEM((4 * A, K * A), BF16),
            pltpu.VMEM((4 * A, K * A), BF16),
            pltpu.VMEM((4 * A, K * A), F32),
            pltpu.VMEM((4 * A, K * A), F32),
            pltpu.VMEM((E + 1, 3, 8, A), F32),
            pltpu.VMEM((BX, 3, A, 128), F32),
        ],
        in_specs=[VMEM] * 3 + [SMEM] * 2 + [VMEM] * 12,
    )


def backward_inner_call(*args):
    return call(
        backward_inner_kernel,
        args,
        [((EX, 3, A), F32)],
        [
            pltpu.VMEM((EX + 1, 8, A), F32),
            pltpu.VMEM((4 * A, K * A), F32),
            pltpu.VMEM((4 * A, K * A), F32),
            pltpu.VMEM((EX + 1, 3, 8, A), F32),
            pltpu.VMEM((BX, 3, A, 128), F32),
        ],
        in_specs=[VMEM, SMEM, VMEM, VMEM, VMEM, VMEM],
        cost=pl.CostEstimate(flops=4 * 10**9, bytes_accessed=10**6, transcendentals=0),
    )


def call(kernel, args, outs, scratch=(), in_specs=None, out_specs=None, cost=None, params=PARAMS):
    return pl.pallas_call(
        kernel,
        out_shape=[jax.ShapeDtypeStruct(s, d) for s, d in outs],
        in_specs=in_specs or [VMEM] * len(args),
        out_specs=out_specs or [VMEM] * len(outs),
        scratch_shapes=list(scratch),
        compiler_params=params,
        cost_estimate=cost,
    )(*args)


def along(block, axis, step):
    size = lax.axis_size(axis)
    return lax.ppermute(block, axis, [(i, i + step) for i in range(size) if 0 <= i + step < size])


def both(lo, hi, axis, step=1):
    return along(lo, axis, step), along(hi, axis, -step)


def local(
    positions, species, pair_codes, pair_count, embed_table, ws1, wv1, ws2, wv2, ms, mv, m2, readout
):
    first, own, last = call(
        pack_kernel,
        (positions.transpose(0, 2, 1, 3), species, pair_codes, pair_count),
        [((1, 8, A), F32), ((BX, 8, A), F32), ((1, 8, A), F32)],
        in_specs=[VMEM, VMEM, SMEM, SMEM],
        params=pltpu.CompilerParams(vmem_limit_bytes=60 * 1024 * 1024),
    )
    left, right = both(last, first, "gx")
    ext_mid = jnp.concatenate([left, own, right], axis=0)
    ext_lo, ext_hi = both(ext_mid, ext_mid, "gy")
    ext = (ext_lo, ext_mid, ext_hi)
    table = jnp.pad(embed_table, ((0, 128 - embed_table.shape[0]), (0, 0)))
    square = jnp.concatenate([ms, mv, m2, table], axis=0)
    radial = jnp.concatenate([ws1, wv1, ws2, wv2, readout.reshape(1, C), jnp.zeros((7, C), F32)], axis=0)
    pre, feat, lo, hi, keep_s, keep_v, keep_ready, keep_col, list1, list2 = forward_call(
        *ext, radial, square
    )
    below, above = both(hi, lo, "gy")
    (mid,) = forward_inner_call(ext_mid, list2, keep_ready, keep_col)
    edge = lambda x: (mid[x : x + 2] + below[x : x + 2] + above[x : x + 2]).astype(BF16)
    left, right = both(edge(EX - 2), edge(0), "gx")
    energy, inner, inner_own = call(
        middle_kernel,
        (mid, below, above, left, right, feat, radial, square),
        [((BX, 1, A), F32), ((EX, A, C), BF16), ((EX, A, C), F32)],
    )
    in_lo, in_hi = both(inner, inner, "gy")
    held = backward_inner_two_call(ext_mid, list2, inner_own, feat, keep_col, radial)
    lo, mid, hi, keep_inward = backward_call(
        *ext, list1, list2, *held, feat, pre, in_lo, in_hi, keep_s, keep_v, keep_col, radial, square
    )
    below, above = both(hi, lo, "gy")
    (more,) = backward_inner_call(ext_mid, list1, keep_s, keep_v, keep_col, keep_inward)
    total = mid + more + below + above
    left, right = both(total[EX - 1 :], total[:1], "gx")
    total = total[1 : BX + 1] + jnp.concatenate(
        [left, jnp.zeros((BX - 2, 3, A), F32), right], axis=0
    )
    return energy, -total.reshape(BX, 1, 3, A)


def solution(mesh):
    in_specs = (
        P("gx", "gy", None, None),
        P("gx", "gy", None),
        P("gx", "gy", None),
        P("gx", "gy"),
        *[P()] * 9,
    )
    out_specs = (P("gx", "gy", None), P("gx", "gy", None, None))
    return jax.shard_map(local, mesh=mesh, in_specs=in_specs, out_specs=out_specs, check_vma=False)
```

time: 171 us -> 148 us (0.87)
  the two profiles are of different devices: /device:TPU:20 before, /device:TPU:18 now
where the time goes in v3:
time: 148 us; the launch traced here: 146 us
  starting transfers between devices  64.9 us (44%)
  Pallas kernels  56.3 us (38%)
  waiting for transfers between devices  18.8 us (13%)
  local copies, waits for them, and re-layouts  3.54 us (2%)
  between operations  1.51 us (1%)
    ppermute x14, starting transfers between devices, along(): lax.ppermute(block, axis, [(i, i + step) for i in range(size) if 0 <= i +...  64.9 us
    pallas_call x7, Pallas kernels, call(): pl.pallas_call(kernel, out_shape=[jax.ShapeDtypeStruct(s, d) for s, d in...  56.3 us
    ppermute x14, waiting for transfers between devices, along(): lax.ppermute(block, axis, [(i, i + step) for i in range(size) if 0 <= i +...  18.8 us
  transfers between devices with their start and end apart: 14, of which 6 were waited for; matrix products, arithmetic and copies ran while one was open for 3% of the time, Pallas kernels for 11%

profile of v3, /device:TPU:18, one launch (start us, length us, event | category | flops | bytes accessed | tf_op | source)
XLA Modules:
  0.0 146.0 jit_solution(16445606561078083755)
XLA Ops:
  1.3 1.5 %shard_map.140 = (f32[1,8,128]{2,1,0:T(8,128)}, f32[6,8,128]{2,1,0:T(8,128)}, f32[1,8,128]{2,1,0:T(8,128)}) custom-call(f32[6,3,1,128]{3,2,1,0:T(1,128)} %bitcast.4, s32[6,1,128]{2,1,0:T(1,128)} %species_ref.1, s32[1,1,26]{2,1,0:T(1,128)} %codes_ref.1, s32[1,1]{1,0:T(1,128)S(6)} %copy.18.count_ref), custom_call_target="tpu_custom_call" | custom-call | tf_op jit(solution)/shard_map/pallas_call | solution.py:669
  2.8 9.1 %collective-permute-start = (f32[1,8,128]{2,1,0:T(8,128)}, f32[1,8,128]{2,1,0:T(8,128)S(1)}, u32[]{:S(2)}, u32[]{:S(2)}) collective-permute-start(f32[1,8,128]{2,1,0:T(8,128)} %get-tuple-element.25), channel_id=1, source_target_pairs={{0,32},{32,64},{64,96},{96,128},{128,160},{160,192},{192,224},{1,3... | collective-permute-start | bytes 12296 | tf_op jit(solution)/shard_map/ppermute | solution.py:682
  11.8 1.9 %collective-permute-start.1 = (f32[1,8,128]{2,1,0:T(8,128)}, f32[1,8,128]{2,1,0:T(8,128)S(1)}, u32[]{:S(2)}, u32[]{:S(2)}) collective-permute-start(f32[1,8,128]{2,1,0:T(8,128)} %get-tuple-element.27), channel_id=1, source_target_pairs={{32,0},{64,32},{96,64},{128,96},{160,128},{192,160},{224,192},{33,... | collective-permute-start | bytes 12296 | tf_op jit(solution)/shard_map/ppermute | solution.py:682
  13.8 0.0 collective-permute-done
  13.8 0.7 constant_dynamic-update-slice_fusion.1
  14.5 7.0 %collective-permute-done.1 = f32[1,8,128]{2,1,0:T(8,128)S(1)} collective-permute-done((f32[1,8,128]{2,1,0:T(8,128)}, f32[1,8,128]{2,1,0:T(8,128)S(1)}, u32[]{:S(2)}, u32[]{:S(2)}) %collective-permute-start.1) | collective-permute-done | bytes 4128 | tf_op jit(solution)/shard_map/ppermute | solution.py:682
  21.5 1.9 %collective-permute-start.2 = (f32[8,8,128]{2,1,0:T(8,128)S(1)}, f32[8,8,128]{2,1,0:T(8,128)S(1)}, u32[]{:S(2)}, u32[]{:S(2)}) collective-permute-start(f32[8,8,128]{2,1,0:T(8,128)S(1)} %constant_dynamic-update-slice_fusion.mid_ref), channel_id=1, source_target_pairs={{0,1},{1,2},{2,3},{3,4},{4,5},{5,6},{6,7},{7,8},{8,9},{9,10},{10,1... | collective-permute-start | bytes 98312 | tf_op jit(solution)/shard_map/ppermute | solution.py:682
  23.4 6.3 %collective-permute-start.3 = (f32[8,8,128]{2,1,0:T(8,128)S(1)}, f32[8,8,128]{2,1,0:T(8,128)S(1)}, u32[]{:S(2)}, u32[]{:S(2)}) collective-permute-start(f32[8,8,128]{2,1,0:T(8,128)S(1)} %constant_dynamic-update-slice_fusion.mid_ref), channel_id=1, source_target_pairs={{1,0},{2,1},{3,2},{4,3},{5,4},{6,5},{7,6},{8,7},{9,8},{10,9},{11,1... | collective-permute-start | bytes 98312 | tf_op jit(solution)/shard_map/ppermute | solution.py:682
  29.8 0.8 fusion.1.square_ref
  30.6 2.1 %concatenate.13.radial_ref = f32[24,128]{1,0:T(8,128)S(1)} concatenate(f32[4,128]{1,0:T(4,128)} %param.18, f32[4,128]{1,0:T(4,128)} %param.19, f32[4,128]{1,0:T(4,128)} %param.20, f32[4,128]{1,0:T(4,128)} %param.21, f32[1,128]{1,0:T(1,128)} %bitcast.5, f32[7,128]{1,0:T(8,128)S(1)} %broadcast_in_dim.6), dimensions={0} | concatenate | bytes 24576 | tf_op jit(solution)/shard_map/concatenate | solution.py:705
  32.7 0.0 collective-permute-done.2.lo_ref
  32.7 0.0 collective-permute-done.3.hi_ref
  32.7 19.5 %shard_map.141 = (f32[6,128,128]{2,1,0:T(8,128)S(1)}, bf16[6,512,128]{2,1,0:T(8,128)(2,1)S(1)}, bf16[8,128,128]{2,1,0:T(8,128)(2,1)S(1)}, bf16[8,128,128]{2,1,0:...) custom-call(f32[8,8,128]{2,1,0:T(8,128)S(1)} %collective-permute-don, ...), custom_call_target="tpu_custom_call" | custom-call | tf_op jit(solution)/shard_map/pallas_call | solution.py:669
  52.2 1.9 %collective-permute-start.4 = (bf16[8,128,128]{2,1,0:T(8,128)(2,1)S(1)}, bf16[8,128,128]{2,1,0:T(8,128)(2,1)S(1)}, u32[]{:S(2)}, u32[]{:S(2)}) collective-permute-start(bf16[8,128,128]{2,1,0:T(8,128)(2,1)S(1)} %get-tuple-element.31), channel_id=1, source_target_pairs={{0,1},{1,2},{2,3},{3,4},{4,5},{5,6},{6,7},{7,8},{8,9},{9,10},{10,1... | collective-permute-start | bytes 786440 | tf_op jit(solution)/shard_map/ppermute | solution.py:682
  54.2 6.3 %collective-permute-start.5 = (bf16[8,128,128]{2,1,0:T(8,128)(2,1)S(1)}, bf16[8,128,128]{2,1,0:T(8,128)(2,1)S(1)}, u32[]{:S(2)}, u32[]{:S(2)}) collective-permute-start(bf16[8,128,128]{2,1,0:T(8,128)(2,1)S(1)} %get-tuple-element.32), channel_id=1, source_target_pairs={{1,0},{2,1},{3,2},{4,3},{5,4},{6,5},{7,6},{8,7},{9,8},{10,9},{11,1... | collective-permute-start | bytes 786440 | tf_op jit(solution)/shard_map/ppermute | solution.py:682
  60.5 4.3 %shard_map.142.mid_ref = f32[8,128,128]{2,1,0:T(8,128)S(1)} custom-call(f32[8,8,128]{2,1,0:T(8,128)S(1)} %constant_dynamic-update-slice_fusion.mid_ref, s32[64]{0:T(128)S(1)} %get-tuple-element.28.list2_ref, bf16[6,2048,128]{2,1,0:T(8,128)(2,1)S(1)} %get-tuple-element.29.ready_ref, f32[9,3,128,128]{3,2,1,0:T(8,128)S(1)} %get-tuple-element.30.col_ref), custom_call_target="tpu_custom_call" | custom-call | flops 4000000000 | bytes 1000000 | tf_op jit(solution)/shard_map/pallas_call | solution.py:669
  64.8 0.0 collective-permute-done.4.below_ref
  64.8 0.8 collective-permute-done.5.above_ref
  65.5 0.1 fusion.3
  65.6 2.5 %collective-permute-start.6 = (bf16[2,128,128]{2,1,0:T(8,128)(2,1)S(1)}, bf16[2,128,128]{2,1,0:T(8,128)(2,1)S(1)}, u32[]{:S(2)}, u32[]{:S(2)}) collective-permute-start(bf16[2,128,128]{2,1,0:T(8,128)(2,1)S(1)} %get-tuple-element.51), channel_id=1, source_target_pairs={{0,32},{32,64},{64,96},{96,128},{128,160},{160,192},{192,224},{1,3... | collective-permute-start | bytes 196616 | tf_op jit(solution)/shard_map/ppermute | solution.py:682
  68.1 8.2 %collective-permute-start.7 = (bf16[2,128,128]{2,1,0:T(8,128)(2,1)S(1)}, bf16[2,128,128]{2,1,0:T(8,128)(2,1)S(1)}, u32[]{:S(2)}, u32[]{:S(2)}) collective-permute-start(bf16[2,128,128]{2,1,0:T(8,128)(2,1)S(1)} %get-tuple-element.50), channel_id=1, source_target_pairs={{32,0},{64,32},{96,64},{128,96},{160,128},{192,160},{224,192},{33,... | collective-permute-start | bytes 196616 | tf_op jit(solution)/shard_map/ppermute | solution.py:682
  76.3 0.3 collective-permute-done.6.left_ref
  76.6 3.5 %collective-permute-done.7.right_ref = bf16[2,128,128]{2,1,0:T(8,128)(2,1)S(1)} collective-permute-done((bf16[2,128,128]{2,1,0:T(8,128)(2,1)S(1)}, bf16[2,128,128]{2,1,0:T(8,128)(2,1)S(1)}, u32[]{:S(2)}, u32[]{:S(2)}) %collective-permute-start.7) | collective-permute-done | bytes 65568 | tf_op jit(solution)/shard_map/ppermute | solution.py:682
  80.1 1.4 shard_map.143
  81.5 1.9 %collective-permute-start.8 = (bf16[8,128,128]{2,1,0:T(8,128)(2,1)S(1)}, bf16[8,128,128]{2,1,0:T(8,128)(2,1)S(1)}, u32[]{:S(2)}, u32[]{:S(2)}) collective-permute-start(bf16[8,128,128]{2,1,0:T(8,128)(2,1)S(1)} %get-tuple-element.41), channel_id=1, source_target_pairs={{0,1},{1,2},{2,3},{3,4},{4,5},{5,6},{6,7},{7,8},{8,9},{9,10},{10,1... | collective-permute-start | bytes 786440 | tf_op jit(solution)/shard_map/ppermute | solution.py:682
  83.4 6.3 %collective-permute-start.9 = (bf16[8,128,128]{2,1,0:T(8,128)(2,1)S(1)}, bf16[8,128,128]{2,1,0:T(8,128)(2,1)S(1)}, u32[]{:S(2)}, u32[]{:S(2)}) collective-permute-start(bf16[8,128,128]{2,1,0:T(8,128)(2,1)S(1)} %get-tuple-element.41), channel_id=1, source_target_pairs={{1,0},{2,1},{3,2},{4,3},{5,4},{6,5},{7,6},{8,7},{9,8},{10,9},{11,1... | collective-permute-start | bytes 786440 | tf_op jit(solution)/shard_map/ppermute | solution.py:682
  89.8 7.0 %shard_map.144 = (f32[6,512,128]{2,1,0:T(8,128)S(1)}, f32[6,3,128,128]{3,2,1,0:T(8,128)S(1)}, f32[9,3,8,128]{3,2,1,0:T(8,128)S(1)}) custom-call(f32[8,8,128]{2,1,0:T(8,128)S(1)} %constant_dynamic-update-slice_fusion.mid_ref, s32[64]{0:T(128)S(1)} %get-tuple-element.28.list2_ref, f32[8,128,128]{2,1,0:T(8,128)S(1)} %get-tuple-element.36.in_mid_ref, ...), custom_call_target="tpu_custom_call" | custom-call | flops 4000000000 | bytes 1000000 | tf_op jit(solution)/shard_map/pallas_call | solution.py:669
  96.8 0.0 collective-permute-done.8.in_lo_ref
  96.8 0.0 collective-permute-done.9.in_hi_ref
  96.8 17.8 %shard_map.145 = (f32[8,3,128]{2,1,0:T(4,128)S(1)}, f32[8,3,128]{2,1,0:T(4,128)S(1)}, f32[8,3,128]{2,1,0:T(4,128)S(1)}, bf16[6,512,128]{2,1,0:T(8,128)(2,1)S(1)}) custom-call(f32[8,8,128]{2,1,0:T(8,128)S(1)} %collective-permute-done.2.lo_ref, f32[8,8,128]{2,1,0:T(8,128)S(1)} %constant_dynamic-update-slice_fusion.mid_ref, ...), custom_call_target="tpu_custom_call" | custom-call | tf_op jit(solution)/shard_map/pallas_call | solution.py:669
  114.6 4.3 %collective-permute-start.11 = (f32[8,3,128]{2,1,0:T(4,128)S(1)}, f32[8,3,128]{2,1,0:T(4,128)S(1)}, u32[]{:S(2)}, u32[]{:S(2)}) collective-permute-start(f32[8,3,128]{2,1,0:T(4,128)S(1)} %get-tuple-element.47), channel_id=1, source_target_pairs={{1,0},{2,1},{3,2},{4,3},{5,4},{6,5},{7,6},{8,7},{9,8},{10,9},{11,1... | collective-permute-start | bytes 36872 | tf_op jit(solution)/shard_map/ppermute | solution.py:682
  118.9 1.9 %collective-permute-start.10 = (f32[8,3,128]{2,1,0:T(4,128)S(1)}, f32[8,3,128]{2,1,0:T(4,128)S(1)}, u32[]{:S(2)}, u32[]{:S(2)}) collective-permute-start(f32[8,3,128]{2,1,0:T(4,128)S(1)} %get-tuple-element.46), channel_id=1, source_target_pairs={{0,1},{1,2},{2,3},{3,4},{4,5},{5,6},{6,7},{7,8},{8,9},{9,10},{10,1... | collective-permute-start | bytes 36872 | tf_op jit(solution)/shard_map/ppermute | solution.py:682
  120.9 4.8 %shard_map.146 = f32[8,3,128]{2,1,0:T(4,128)S(1)} custom-call(f32[8,8,128]{2,1,0:T(8,128)S(1)} %constant_dynamic-update-slice_fusion.mid_ref, s32[64]{0:T(128)S(1)} %get-tuple-element.35.list1_ref, bf16[25,512,128]{2,1,0:T(8,128)(2,1)S(1)} %get-tuple-element.42.scaled_s_ref, bf16[25,512,128]{2,1,0:T(8,128)(2,1)S(1)} %get-tuple-element.43.scaled_v_ref, ...), custom_call_target="tpu_custom_call" | custom-call | flops 4000000000 | bytes 1000000 | tf_op jit(solution)/shard_map/pallas_call | solution.py:669
  125.7 0.0 collective-permute-done.11
  125.7 1.0 collective-permute-done.10
  126.7 8.3 %collective-permute-start.13 = (f32[1,3,128]{2,1,0:T(4,128)S(1)}, f32[1,3,128]{2,1,0:T(4,128)S(1)}, u32[]{:S(2)}, u32[]{:S(2)}) collective-permute-start(f32[1,3,128]{2,1,0:T(4,128)S(1)} %get-tuple-element.53), channel_id=1, source_target_pairs={{32,0},{64,32},{96,64},{128,96},{160,128},{192,160},{224,192},{33,... | collective-permute-start | bytes 4616 | tf_op jit(solution)/shard_map/ppermute | solution.py:682
  135.1 4.0 %collective-permute-start.12 = (f32[1,3,128]{2,1,0:T(4,128)S(1)}, f32[1,3,128]{2,1,0:T(4,128)S(1)}, u32[]{:S(2)}, u32[]{:S(2)}) collective-permute-start(f32[1,3,128]{2,1,0:T(4,128)S(1)} %get-tuple-element.52), channel_id=1, source_target_pairs={{0,32},{32,64},{64,96},{96,128},{128,160},{160,192},{192,224},{1,3... | collective-permute-start | bytes 4616 | tf_op jit(solution)/shard_map/ppermute | solution.py:682
  139.1 0.1 pad.6.clone
  139.1 0.0 collective-permute-done.13
  139.1 6.2 %collective-permute-done.12 = f32[1,3,128]{2,1,0:T(4,128)S(1)} collective-permute-done((f32[1,3,128]{2,1,0:T(4,128)S(1)}, f32[1,3,128]{2,1,0:T(4,128)S(1)}, u32[]{:S(2)}, u32[]{:S(2)}) %collective-permute-start.12) | collective-permute-done | bytes 1568 | tf_op jit(solution)/shard_map/ppermute | solution.py:682
  145.3 0.1 fusion.7
  145.4 0.6 copy.15
  (6 shorter events, 0.0 us)
Async XLA Ops:
  2.8 11.0 %collective-permute-start = (f32[1,8,128]{2,1,0:T(8,128)}, f32[1,8,128]{2,1,0:T(8,128)S(1)}, u32[]{:S(2)}, u32[]{:S(2)}) collective-permute-start(f32[1,8,128]{2,1,0:T(8,128)} %get-tuple-element.25), channel_id=1, source_target_pairs={{0,32},{32,64},{64,96},{96,128},{128,160},{160,192},{192,224},{1,3... | collective-permute-start | bytes 12296 | tf_op jit(solution)/shard_map/ppermute | solution.py:682
  11.8 9.7 %collective-permute-start.1 = (f32[1,8,128]{2,1,0:T(8,128)}, f32[1,8,128]{2,1,0:T(8,128)S(1)}, u32[]{:S(2)}, u32[]{:S(2)}) collective-permute-start(f32[1,8,128]{2,1,0:T(8,128)} %get-tuple-element.27), channel_id=1, source_target_pairs={{32,0},{64,32},{96,64},{128,96},{160,128},{192,160},{224,192},{33,... | collective-permute-start | bytes 12296 | tf_op jit(solution)/shard_map/ppermute | solution.py:682
  21.5 11.2 %collective-permute-start.2 = (f32[8,8,128]{2,1,0:T(8,128)S(1)}, f32[8,8,128]{2,1,0:T(8,128)S(1)}, u32[]{:S(2)}, u32[]{:S(2)}) collective-permute-start(f32[8,8,128]{2,1,0:T(8,128)S(1)} %constant_dynamic-update-slice_fusion.mid_ref), channel_id=1, source_target_pairs={{0,1},{1,2},{2,3},{3,4},{4,5},{5,6},{6,7},{7,8},{8,9},{9,10},{10,1... | collective-permute-start | bytes 98312 | tf_op jit(solution)/shard_map/ppermute | solution.py:682
  23.4 9.3 %collective-permute-start.3 = (f32[8,8,128]{2,1,0:T(8,128)S(1)}, f32[8,8,128]{2,1,0:T(8,128)S(1)}, u32[]{:S(2)}, u32[]{:S(2)}) collective-permute-start(f32[8,8,128]{2,1,0:T(8,128)S(1)} %constant_dynamic-update-slice_fusion.mid_ref), channel_id=1, source_target_pairs={{1,0},{2,1},{3,2},{4,3},{5,4},{6,5},{7,6},{8,7},{9,8},{10,9},{11,1... | collective-permute-start | bytes 98312 | tf_op jit(solution)/shard_map/ppermute | solution.py:682
  52.2 12.5 %collective-permute-start.4 = (bf16[8,128,128]{2,1,0:T(8,128)(2,1)S(1)}, bf16[8,128,128]{2,1,0:T(8,128)(2,1)S(1)}, u32[]{:S(2)}, u32[]{:S(2)}) collective-permute-start(bf16[8,128,128]{2,1,0:T(8,128)(2,1)S(1)} %get-tuple-element.31), channel_id=1, source_target_pairs={{0,1},{1,2},{2,3},{3,4},{4,5},{5,6},{6,7},{7,8},{8,9},{9,10},{10,1... | collective-permute-start | bytes 786440 | tf_op jit(solution)/shard_map/ppermute | solution.py:682
  54.2 11.4 %collective-permute-start.5 = (bf16[8,128,128]{2,1,0:T(8,128)(2,1)S(1)}, bf16[8,128,128]{2,1,0:T(8,128)(2,1)S(1)}, u32[]{:S(2)}, u32[]{:S(2)}) collective-permute-start(bf16[8,128,128]{2,1,0:T(8,128)(2,1)S(1)} %get-tuple-element.32), channel_id=1, source_target_pairs={{1,0},{2,1},{3,2},{4,3},{5,4},{6,5},{7,6},{8,7},{9,8},{10,9},{11,1... | collective-permute-start | bytes 786440 | tf_op jit(solution)/shard_map/ppermute | solution.py:682
  65.6 11.0 %collective-permute-start.6 = (bf16[2,128,128]{2,1,0:T(8,128)(2,1)S(1)}, bf16[2,128,128]{2,1,0:T(8,128)(2,1)S(1)}, u32[]{:S(2)}, u32[]{:S(2)}) collective-permute-start(bf16[2,128,128]{2,1,0:T(8,128)(2,1)S(1)} %get-tuple-element.51), channel_id=1, source_target_pairs={{0,32},{32,64},{64,96},{96,128},{128,160},{160,192},{192,224},{1,3... | collective-permute-start | bytes 196616 | tf_op jit(solution)/shard_map/ppermute | solution.py:682
  68.1 12.0 %collective-permute-start.7 = (bf16[2,128,128]{2,1,0:T(8,128)(2,1)S(1)}, bf16[2,128,128]{2,1,0:T(8,128)(2,1)S(1)}, u32[]{:S(2)}, u32[]{:S(2)}) collective-permute-start(bf16[2,128,128]{2,1,0:T(8,128)(2,1)S(1)} %get-tuple-element.50), channel_id=1, source_target_pairs={{32,0},{64,32},{96,64},{128,96},{160,128},{192,160},{224,192},{33,... | collective-permute-start | bytes 196616 | tf_op jit(solution)/shard_map/ppermute | solution.py:682
  81.5 15.3 %collective-permute-start.8 = (bf16[8,128,128]{2,1,0:T(8,128)(2,1)S(1)}, bf16[8,128,128]{2,1,0:T(8,128)(2,1)S(1)}, u32[]{:S(2)}, u32[]{:S(2)}) collective-permute-start(bf16[8,128,128]{2,1,0:T(8,128)(2,1)S(1)} %get-tuple-element.41), channel_id=1, source_target_pairs={{0,1},{1,2},{2,3},{3,4},{4,5},{5,6},{6,7},{7,8},{8,9},{9,10},{10,1... | collective-permute-start | bytes 786440 | tf_op jit(solution)/shard_map/ppermute | solution.py:682
  83.4 13.4 %collective-permute-start.9 = (bf16[8,128,128]{2,1,0:T(8,128)(2,1)S(1)}, bf16[8,128,128]{2,1,0:T(8,128)(2,1)S(1)}, u32[]{:S(2)}, u32[]{:S(2)}) collective-permute-start(bf16[8,128,128]{2,1,0:T(8,128)(2,1)S(1)} %get-tuple-element.41), channel_id=1, source_target_pairs={{1,0},{2,1},{3,2},{4,3},{5,4},{6,5},{7,6},{8,7},{9,8},{10,9},{11,1... | collective-permute-start | bytes 786440 | tf_op jit(solution)/shard_map/ppermute | solution.py:682
  114.6 11.1 %collective-permute-start.11 = (f32[8,3,128]{2,1,0:T(4,128)S(1)}, f32[8,3,128]{2,1,0:T(4,128)S(1)}, u32[]{:S(2)}, u32[]{:S(2)}) collective-permute-start(f32[8,3,128]{2,1,0:T(4,128)S(1)} %get-tuple-element.47), channel_id=1, source_target_pairs={{1,0},{2,1},{3,2},{4,3},{5,4},{6,5},{7,6},{8,7},{9,8},{10,9},{11,1... | collective-permute-start | bytes 36872 | tf_op jit(solution)/shard_map/ppermute | solution.py:682
  118.9 7.8 %collective-permute-start.10 = (f32[8,3,128]{2,1,0:T(4,128)S(1)}, f32[8,3,128]{2,1,0:T(4,128)S(1)}, u32[]{:S(2)}, u32[]{:S(2)}) collective-permute-start(f32[8,3,128]{2,1,0:T(4,128)S(1)} %get-tuple-element.46), channel_id=1, source_target_pairs={{0,1},{1,2},{2,3},{3,4},{4,5},{5,6},{6,7},{7,8},{8,9},{9,10},{10,1... | collective-permute-start | bytes 36872 | tf_op jit(solution)/shard_map/ppermute | solution.py:682
  126.7 12.4 %collective-permute-start.13 = (f32[1,3,128]{2,1,0:T(4,128)S(1)}, f32[1,3,128]{2,1,0:T(4,128)S(1)}, u32[]{:S(2)}, u32[]{:S(2)}) collective-permute-start(f32[1,3,128]{2,1,0:T(4,128)S(1)} %get-tuple-element.53), channel_id=1, source_target_pairs={{32,0},{64,32},{96,64},{128,96},{160,128},{192,160},{224,192},{33,... | collective-permute-start | bytes 4616 | tf_op jit(solution)/shard_map/ppermute | solution.py:682
  135.1 10.3 %collective-permute-start.12 = (f32[1,3,128]{2,1,0:T(4,128)S(1)}, f32[1,3,128]{2,1,0:T(4,128)S(1)}, u32[]{:S(2)}, u32[]{:S(2)}) collective-permute-start(f32[1,3,128]{2,1,0:T(4,128)S(1)} %get-tuple-element.52), channel_id=1, source_target_pairs={{0,32},{32,64},{64,96},{96,128},{128,160},{160,192},{192,224},{1,3... | collective-permute-start | bytes 4616 | tf_op jit(solution)/shard_map/ppermute | solution.py:682

commit v4 on v3

--- a/solution.py
+++ b/solution.py
@@ -18,19 +18,32 @@
 E = 3 * EX
 
 HOME_PAIRS = [
-    [(h, (o % 3) * EX + h + o // 3, EX + 1 + h, o) for h in range(BX) for o in range(9) if (o % 3 == 1) == inner]
+    [
+        (h, (o % 3) * EX + h + o // 3, EX + 1 + h, o)
+        for h in range(BX)
+        for o in range(9)
+        if (o % 3 == 1 and 0 <= h + o // 3 - 1 < BX) == inner
+    ]
     for inner in (False, True)
 ]
+
+
+def far_part(e):
+    return 0 if e // EX != 1 else 1 if 2 <= e % EX < EX - 2 else 2
+
+
 FAR_PAIRS = [
     [
         (f, (2 - o % 3) * EX + f + 2 - o // 3, (2 - o % 3) * EX + f + 2 - o // 3, o)
         for f in range(BX)
         for o in range(9)
-        if (o % 3 == 1) == inner
+        if far_part((2 - o % 3) * EX + f + 2 - o // 3) == part
     ]
-    for inner in (False, True)
+    for part in range(3)
 ]
-MIDDLE, END = 62, 63
+MIDDLE, THIRD, END = 62, 61, 63
+INNER = range(2, EX - 2)
+OUTER = [0, 1, EX - 2, EX - 1]
 
 
 def dot(a, b):
@@ -41,14 +54,37 @@
     return lax.dot_general(a, b, NT, preferred_element_type=F32)
 
 
-def pack_kernel(pos_ref, species_ref, codes_ref, count_ref, first_ref, out_ref, last_ref):
+def pack_kernel(
+    pos_ref, species_ref, codes_ref, count_ref, table_ref, ws1_ref, wv1_ref, ws2_ref, wv2_ref, ms_ref,
+    mv_ref, m2_ref, readout_ref,
+    first_ref, out_ref, last_ref, list_ref, radial_ref, square_ref,
+    wide_ref,
+):
+    for i, ref in enumerate((ws1_ref, wv1_ref, ws2_ref, wv2_ref)):
+        radial_ref[K * i : K * i + K, :] = ref[...]
+    radial_ref[4 * K : 4 * K + 1, :] = readout_ref[...]
+    for i, ref in enumerate((ms_ref, mv_ref, m2_ref)):
+        square_ref[C * i : C * i + C, :] = ref[...]
+    wide_ref[...] = jnp.zeros_like(wide_ref)
+    wide_ref[0 : table_ref.shape[0], :] = table_ref[...].astype(F32)
+    square_ref[3 * C : 4 * C, :] = wide_ref[...].astype(BF16)
+    n = jnp.int32(0)
     block_id = lax.broadcasted_iota(jnp.int32, (8, 128), 0)
     mask = jnp.zeros((8, 128), jnp.int32)
     for p in range(codes_ref.shape[2]):
         code = codes_ref[0, 0, p]
         block = lax.shift_right_logical(code * 57, 9)
-        bit = jnp.where(p < count_ref[0, 0], lax.shift_left(1, code - 9 * block), 0)
+        offset = code - 9 * block
+        bit = jnp.where(p < count_ref[0, 0], lax.shift_left(1, offset), 0)
         mask = mask + jnp.where(block_id == block, bit, 0)
+        over = lax.shift_right_logical(offset * 11, 5)
+        far = block + over - 1
+        inside = (bit > 0) & (offset - 3 * over == 1) & (far >= 0) & (far < BX)
+        list_ref[n] = block + (far + EX + 1) * 8 + jnp.where(offset == 4, 256, 0)
+        n = n + jnp.where(inside, 1, 0)
+    for i in range(3):
+        list_ref[n + i] = E * 8
+    list_ref[END] = n + (n & 1)
     mask = mask.astype(F32)
     for h in range(BX):
         places = [(out_ref, h)]
@@ -81,7 +117,8 @@
 
 def make_list(parts, masks_ref, list_ref):
     n = jnp.int32(0)
-    for pairs, place in zip(parts, (MIDDLE, END)):
+    places = (MIDDLE, END) if len(parts) == 2 else (MIDDLE, THIRD, END)
+    for pairs, place in zip(parts, places):
         held = None
         for own, other, lister, o in sorted(pairs, key=lambda pair: pair[2]):
             if lister != held:
@@ -171,8 +208,75 @@
     return (feature.astype(F32) * weights_ref[k : k + 1, :]).astype(BF16)
 
 
+def first_sums(
+    end, list_ref, col_ref, near, rows, where, scaled_s_ref, scaled_v_ref, acc_ref, tile_a_ref,
+    tile_b_ref,
+):
+    def first_tiles(p, tile_ref, r):
+        own, other, bias = entry(list_ref, p)
+        row = rows(where(other))
+        off, inv, taper, u, q = geometry(col_ref, own + near, row, r, 1.0, bias)
+
+        def put(g, k, tile):
+            tile_ref[pl.ds(g * A + r, ROWS), pl.ds(k * A, A)] = tile
+
+        store_tiles(put, off, inv, taper, q)
+
+    def first_sum(p, tile_ref, g):
+        own, other, _ = entry(list_ref, p)
+        part = pl.ds(g * A, A)
+        acc_ref[own, part, :] += dot(tile_ref[part, :], (scaled_v_ref if g else scaled_s_ref)[where(other)])
+
+    def first_half(p, this_ref, next_ref):
+        for g in range(4):
+            first_sum(p, this_ref, g)
+            for r in range(g * 32, g * 32 + 32, ROWS):
+                first_tiles(p + 1, next_ref, r)
+
+    def first(i, carry):
+        first_half(2 * i, tile_a_ref, tile_b_ref)
+        first_half(2 * i + 1, tile_b_ref, tile_a_ref)
+        return carry
+
+    for r in range(0, A, ROWS):
+        first_tiles(0, tile_a_ref, r)
+    lax.fori_loop(0, half(end), first, 0)
+
+
+def own_kernel(
+    own_ref, list_ref, radial_ref, square_ref,
+    acc_ref,
+    ext_ref, col_ref, scaled_s_ref, scaled_v_ref, tile_a_ref, tile_b_ref,
+):
+    ws1_ref, wv1_ref, _, _, _ = radial_parts(radial_ref)
+    table = square_parts(square_ref)[3][...]
+    for h in range(BX):
+        ext_ref[h] = own_ref[h]
+    ext_ref[BX] = jnp.full((8, A), 1.0e4, F32)
+    for h in range(BX + 1, 16):
+        ext_ref[h] = jnp.zeros((8, A), F32)
+    turned = [ext_ref[0:16].reshape(128, A).T]
+    lanes = lax.broadcasted_iota(jnp.int32, (A, 128), 1).astype(F32)
+    acc_ref[...] = jnp.zeros_like(acc_ref)
+    for h in range(BX):
+        for d in range(3):
+            col_ref[h, d] = spread_lane(turned, h, d)
+        hot = (spread_lane(turned, h, 3) == lanes).astype(BF16)
+        initial = dot(hot, table).astype(BF16)
+        for k in range(K):
+            scaled_s_ref[h, pl.ds(k * A, A), :] = scaled(initial, ws1_ref, k)
+            scaled_v_ref[h, pl.ds(k * A, A), :] = scaled(initial, wv1_ref, k)
+    scaled_s_ref[BX] = jnp.zeros((K * A, C), BF16)
+    scaled_v_ref[BX] = jnp.zeros((K * A, C), BF16)
+    first_sums(
+        list_ref[END], list_ref, col_ref, 0, lambda e: rows_of(ext_ref, e),
+        lambda e: jnp.minimum(e - EX - 1, BX), scaled_s_ref, scaled_v_ref, acc_ref, tile_a_ref,
+        tile_b_ref,
+    )
+
+
 def forward_kernel(
-    lo_ref, mid_ref, hi_ref, radial_ref, square_ref,
+    lo_ref, mid_ref, hi_ref, acc_own_ref, radial_ref, square_ref,
     pre_ref, feat_ref, out_lo_ref, out_hi_ref, scaled_s_ref, scaled_v_ref, ready_ref, keep_col_ref,
     list1_ref, list2_ref,
     ext_ref, col_ref, init_ref, acc_ref, tile_a_ref, tile_b_ref, wide_a_ref, wide_b_ref, total_ref,
@@ -208,39 +312,12 @@
     lax.fori_loop(0, E, scale_block, 0)
     scaled_s_ref[E] = jnp.zeros((K * A, C), BF16)
     scaled_v_ref[E] = jnp.zeros((K * A, C), BF16)
-    acc_ref[...] = jnp.zeros_like(acc_ref)
+    acc_ref[...] = acc_own_ref[...]
     total_ref[...] = jnp.zeros_like(total_ref)
-
-    def first_tiles(p, tile_ref, r):
-        own, other, bias = entry(list1_ref, p)
-        row = rows_of(ext_ref, other)
-        off, inv, taper, u, q = geometry(col_ref, own + EX + 1, row, r, 1.0, bias)
-
-        def put(g, k, tile):
-            tile_ref[pl.ds(g * A + r, ROWS), pl.ds(k * A, A)] = tile
-
-        store_tiles(put, off, inv, taper, q)
-
-    def first_sum(p, tile_ref, g):
-        own, other, _ = entry(list1_ref, p)
-        part = pl.ds(g * A, A)
-        acc_ref[own, part, :] += dot(tile_ref[part, :], (scaled_v_ref if g else scaled_s_ref)[other])
-
-    def first_half(p, this_ref, next_ref):
-        for g in range(4):
-            first_sum(p, this_ref, g)
-            for r in range(g * 32, g * 32 + 32, ROWS):
-                first_tiles(p + 1, next_ref, r)
-
-    def first(i, carry):
-        first_half(2 * i, tile_a_ref, tile_b_ref)
-        first_half(2 * i + 1, tile_b_ref, tile_a_ref)
-        return carry
-
-    for r in range(0, A, ROWS):
-        first_tiles(0, tile_a_ref, r)
-    lax.fori_loop(0, half(list1_ref[END]), first, 0)
-
+    first_sums(
+        list1_ref[MIDDLE], list1_ref, col_ref, EX + 1, lambda e: rows_of(ext_ref, e), lambda e: e,
+        scaled_s_ref, scaled_v_ref, acc_ref, tile_a_ref, tile_b_ref,
+    )
     for h in range(BX):
         pre = dot((acc_ref[h, 0:A, :] * 0.125).astype(BF16), ms_ref[...])
         pre_ref[h] = pre
@@ -326,27 +403,66 @@
     return sigma * (1.0 + value * (1.0 - sigma))
 
 
+def middle(msg, x, feat_ref, radial_ref, square_ref, energy_ref):
+    readout = radial_parts(radial_ref)[4][...]
+    mix_ref = square_parts(square_ref)[2]
+    pre = dot((msg * 0.125).astype(BF16), mix_ref[...])
+    sigma = jax.nn.sigmoid(pre)
+    if 1 <= x <= BX:
+        part = (feat_ref[x - 1, 0:A, :].astype(F32) + pre * sigma) * readout
+        energy_ref[x - 1] = jnp.sum(part.T, axis=0, keepdims=True)
+    grad = (readout * (sigma * (1.0 + pre * (1.0 - sigma)))).astype(BF16)
+    return dot_nt(grad, mix_ref[...]) * 0.125
+
+
+def message(mid_ref, below_ref, above_ref, x):
+    return mid_ref[x] + below_ref[x].astype(F32) + above_ref[x].astype(F32)
+
+
+def middle_inner_kernel(
+    mid_ref, below_ref, above_ref, ext_mid_ref, list2_ref, feat_ref, col_ref, radial_ref, square_ref,
+    energy_ref, second_in_ref, acc_ref, across_ref, down_ref,
+    ext_ref, second_ref, cot_s_ref, cot_v_ref, tile_a_ref, tile_b_ref, grad_a_ref, grad_b_ref,
+):
+    _, _, ws2_ref, wv2_ref, _ = radial_parts(radial_ref)
+    for x in range(EX):
+        ext_ref[x] = ext_mid_ref[x]
+    ext_ref[EX] = jnp.full((8, A), 1.0e4, F32)
+    for x in INNER:
+        second = middle(
+            message(mid_ref, below_ref, above_ref, x), x, feat_ref, radial_ref, square_ref, energy_ref
+        )
+        second_ref[x] = second
+        second_in_ref[x] = second.astype(BF16)
+    acc_ref[...] = jnp.zeros_like(acc_ref)
+    down_ref[...] = jnp.zeros_like(down_ref)
+    across_ref[...] = jnp.zeros_like(across_ref)
+    cotangents(second_ref, cot_s_ref, cot_v_ref, 0, ws2_ref, wv2_ref, INNER)
+    second_moves(
+        list2_ref[MIDDLE], list2_ref[THIRD], list2_ref, col_ref, EX, lambda e: rows_of(ext_ref, e),
+        feat_ref, cot_s_ref, cot_v_ref, acc_ref, across_ref, down_ref, tile_a_ref, tile_b_ref,
+        grad_a_ref, grad_b_ref,
+    )
+
+
 def middle_kernel(
     mid_ref, below_ref, above_ref, left_ref, right_ref, feat_ref, radial_ref, square_ref,
+    energy_part_ref, second_part_ref,
     energy_ref, second_in_ref, second_own_ref,
 ):
-    readout_ref = radial_parts(radial_ref)[4]
-    mix_ref = square_parts(square_ref)[2]
-    for x in range(EX):
-        msg = mid_ref[x] + below_ref[x].astype(F32) + above_ref[x].astype(F32)
+    for x in OUTER:
+        msg = message(mid_ref, below_ref, above_ref, x)
         if x < 2:
             msg = msg + left_ref[x].astype(F32)
-        if x >= EX - 2:
+        else:
             msg = msg + right_ref[x - EX + 2].astype(F32)
-        pre = dot((msg * 0.125).astype(BF16), mix_ref[...])
-        sigma = jax.nn.sigmoid(pre)
-        if 1 <= x <= BX:
-            part = (feat_ref[x - 1, 0:A, :].astype(F32) + pre * sigma) * readout_ref[...]
-            energy_ref[x - 1] = jnp.sum(part.T, axis=0, keepdims=True)
-        grad = (readout_ref[...] * (sigma * (1.0 + pre * (1.0 - sigma)))).astype(BF16)
-        second = dot_nt(grad, mix_ref[...]) * 0.125
+        second = middle(msg, x, feat_ref, radial_ref, square_ref, energy_ref)
         second_own_ref[x] = second
         second_in_ref[x] = second.astype(BF16)
+    for x in INNER:
+        energy_ref[x - 1] = energy_part_ref[x - 1]
+        second_in_ref[x] = second_part_ref[x]
+        second_own_ref[x] = jnp.zeros((A, C), F32)
 
 
 def move(across_ref, own, r, near, own_sign, grad_ref):
@@ -463,18 +579,16 @@
     second_sum(*last, tile_b_ref)
 
 
-def cotangents(ref, cot_s_ref, cot_v_ref, first, ws2_ref, wv2_ref):
-    def cot_block(x, carry):
+def cotangents(ref, cot_s_ref, cot_v_ref, first, ws2_ref, wv2_ref, blocks=range(EX)):
+    for x in blocks:
         for k in range(K):
             cot_s_ref[first + x, pl.ds(k * A, A), :] = scaled(ref[x], ws2_ref, k)
             cot_v_ref[first + x, pl.ds(k * A, A), :] = scaled(ref[x], wv2_ref, k)
-        return carry
-
-    lax.fori_loop(0, EX, cot_block, 0)
-
-
-def backward_inner_two_kernel(
-    mid_ref, list2_ref, in_mid_ref, feat_ref, col_ref, radial_ref,
+
+
+def backward_outer_two_kernel(
+    mid_ref, list2_ref, in_mid_ref, feat_ref, col_ref, radial_ref, acc_in_ref, across_in_ref,
+    down_in_ref,
     acc_ref, across_ref, down_ref,
     ext_ref, cot_s_ref, cot_v_ref, tile_a_ref, tile_b_ref, grad_a_ref, grad_b_ref,
 ):
@@ -482,12 +596,12 @@
     for x in range(EX):
         ext_ref[x] = mid_ref[x]
     ext_ref[EX] = jnp.full((8, A), 1.0e4, F32)
-    acc_ref[...] = jnp.zeros_like(acc_ref)
-    down_ref[...] = jnp.zeros_like(down_ref)
-    across_ref[...] = jnp.zeros_like(across_ref)
-    cotangents(in_mid_ref, cot_s_ref, cot_v_ref, 0, ws2_ref, wv2_ref)
+    acc_ref[...] = acc_in_ref[...]
+    down_ref[...] = down_in_ref[...]
+    across_ref[...] = across_in_ref[...]
+    cotangents(in_mid_ref, cot_s_ref, cot_v_ref, 0, ws2_ref, wv2_ref, OUTER)
     second_moves(
-        list2_ref[MIDDLE], list2_ref[END], list2_ref, col_ref, EX, lambda e: rows_of(ext_ref, e),
+        list2_ref[THIRD], list2_ref[END], list2_ref, col_ref, EX, lambda e: rows_of(ext_ref, e),
         feat_ref, cot_s_ref, cot_v_ref, acc_ref, across_ref, down_ref, tile_a_ref, tile_b_ref,
         grad_a_ref, grad_b_ref,
     )
@@ -550,7 +664,6 @@
             out_ref[x, d : d + 1, :] = line_of(down_ref, across_ref, x, x, d)
 
 
-ANY = pl.BlockSpec(memory_space=pl.ANY)
 VMEM = pl.BlockSpec(memory_space=pltpu.VMEM)
 SMEM = pl.BlockSpec(memory_space=pltpu.SMEM)
 PARAMS = pltpu.CompilerParams(vmem_limit_bytes=24 * 1024 * 1024)
@@ -608,22 +721,55 @@
     )
 
 
-def backward_inner_two_call(*args):
+LONG = pl.CostEstimate(flops=4 * 10**9, bytes_accessed=10**6, transcendentals=0)
+HELD = [((BX, 4 * A, C), F32), ((BX, 3, A, 128), F32), ((EX + 1, 3, 8, A), F32)]
+ROW_SCRATCH = [
+    pltpu.VMEM((EX + 1, K * A, C), BF16),
+    pltpu.VMEM((EX + 1, K * A, C), BF16),
+    pltpu.VMEM((4 * A, K * A), BF16),
+    pltpu.VMEM((4 * A, K * A), BF16),
+    pltpu.VMEM((4 * A, K * A), F32),
+    pltpu.VMEM((4 * A, K * A), F32),
+]
+
+
+def own_call(*args):
     return call(
-        backward_inner_two_kernel,
+        own_kernel,
         args,
-        [((BX, 4 * A, C), F32), ((BX, 3, A, 128), F32), ((EX + 1, 3, 8, A), F32)],
+        [((BX, 4 * A, C), F32)],
         [
-            pltpu.VMEM((EX + 1, 8, A), F32),
-            pltpu.VMEM((EX + 1, K * A, C), BF16),
-            pltpu.VMEM((EX + 1, K * A, C), BF16),
+            pltpu.VMEM((16, 8, A), F32),
+            pltpu.VMEM((BX, 3, A, 128), F32),
+            pltpu.VMEM((BX + 1, K * A, C), BF16),
+            pltpu.VMEM((BX + 1, K * A, C), BF16),
             pltpu.VMEM((4 * A, K * A), BF16),
             pltpu.VMEM((4 * A, K * A), BF16),
-            pltpu.VMEM((4 * A, K * A), F32),
-            pltpu.VMEM((4 * A, K * A), F32),
         ],
-        in_specs=[VMEM, SMEM, VMEM, VMEM, VMEM, VMEM],
-        cost=pl.CostEstimate(flops=4 * 10**9, bytes_accessed=10**6, transcendentals=0),
+        in_specs=[VMEM, SMEM, VMEM, VMEM],
+        cost=LONG,
+    )
+
+
+def middle_inner_call(*args):
+    return call(
+        middle_inner_kernel,
+        args,
+        [((BX, 1, A), F32), ((EX, A, C), BF16), *HELD],
+        [pltpu.VMEM((EX + 1, 8, A), F32), pltpu.VMEM((EX, A, C), F32), *ROW_SCRATCH],
+        in_specs=[VMEM] * 4 + [SMEM] + [VMEM] * 4,
+        cost=LONG,
+    )
+
+
+def backward_outer_two_call(*args):
+    return call(
+        backward_outer_two_kernel,
+        args,
+        HELD,
+        [pltpu.VMEM((EX + 1, 8, A), F32), *ROW_SCRATCH],
+        in_specs=[VMEM, SMEM] + [VMEM] * 7,
+        cost=LONG,
     )
 
 
@@ -689,44 +835,57 @@
 def local(
     positions, species, pair_codes, pair_count, embed_table, ws1, wv1, ws2, wv2, ms, mv, m2, readout
 ):
-    first, own, last = call(
+    first, own, last, own_list, radial, square = call(
         pack_kernel,
-        (positions.transpose(0, 2, 1, 3), species, pair_codes, pair_count),
-        [((1, 8, A), F32), ((BX, 8, A), F32), ((1, 8, A), F32)],
-        in_specs=[VMEM, VMEM, SMEM, SMEM],
+        (
+            positions.transpose(0, 2, 1, 3), species, pair_codes, pair_count, embed_table, ws1, wv1,
+            ws2, wv2, ms, mv, m2, readout.reshape(1, C),
+        ),
+        [
+            ((1, 8, A), F32),
+            ((BX, 8, A), F32),
+            ((1, 8, A), F32),
+            ((64,), jnp.int32),
+            ((24, C), F32),
+            ((4 * C, C), BF16),
+        ],
+        [pltpu.VMEM((C, C), F32)],
+        in_specs=[VMEM] * 2 + [SMEM] * 2 + [VMEM] * 9,
+        out_specs=[VMEM] * 3 + [SMEM] + [VMEM] * 2,
         params=pltpu.CompilerParams(vmem_limit_bytes=60 * 1024 * 1024),
     )
     left, right = both(last, first, "gx")
+    (acc,) = own_call(own, own_list, radial, square)
+    own, acc = lax.optimization_barrier((own, acc))
     ext_mid = jnp.concatenate([left, own, right], axis=0)
     ext_lo, ext_hi = both(ext_mid, ext_mid, "gy")
     ext = (ext_lo, ext_mid, ext_hi)
-    table = jnp.pad(embed_table, ((0, 128 - embed_table.shape[0]), (0, 0)))
-    square = jnp.concatenate([ms, mv, m2, table], axis=0)
-    radial = jnp.concatenate([ws1, wv1, ws2, wv2, readout.reshape(1, C), jnp.zeros((7, C), F32)], axis=0)
-    pre, feat, lo, hi, keep_s, keep_v, keep_ready, keep_col, list1, list2 = forward_call(
-        *ext, radial, square
+    pre, feat, lo, hi, scaled_s, scaled_v, ready, col, list1, list2 = forward_call(
+        *ext, acc, radial, square
     )
     below, above = both(hi, lo, "gy")
-    (mid,) = forward_inner_call(ext_mid, list2, keep_ready, keep_col)
+    (mid,) = forward_inner_call(ext_mid, list2, ready, col)
     edge = lambda x: (mid[x : x + 2] + below[x : x + 2] + above[x : x + 2]).astype(BF16)
     left, right = both(edge(EX - 2), edge(0), "gx")
+    energy, inner, *held = middle_inner_call(
+        mid, below, above, ext_mid, list2, feat, col, radial, square
+    )
     energy, inner, inner_own = call(
         middle_kernel,
-        (mid, below, above, left, right, feat, radial, square),
+        (mid, below, above, left, right, feat, radial, square, energy, inner),
         [((BX, 1, A), F32), ((EX, A, C), BF16), ((EX, A, C), F32)],
     )
     in_lo, in_hi = both(inner, inner, "gy")
-    held = backward_inner_two_call(ext_mid, list2, inner_own, feat, keep_col, radial)
-    lo, mid, hi, keep_inward = backward_call(
-        *ext, list1, list2, *held, feat, pre, in_lo, in_hi, keep_s, keep_v, keep_col, radial, square
+    held = backward_outer_two_call(ext_mid, list2, inner_own, feat, col, radial, *held)
+    lo, mid, hi, inward = backward_call(
+        *ext, list1, list2, *held, feat, pre, in_lo, in_hi, scaled_s, scaled_v, col, radial, square
     )
     below, above = both(hi, lo, "gy")
-    (more,) = backward_inner_call(ext_mid, list1, keep_s, keep_v, keep_col, keep_inward)
-    total = mid + more + below + above
+    (more,) = backward_inner_call(ext_mid, list1, scaled_s, scaled_v, col, inward)
+    total = mid + below + above
     left, right = both(total[EX - 1 :], total[:1], "gx")
-    total = total[1 : BX + 1] + jnp.concatenate(
-        [left, jnp.zeros((BX - 2, 3, A), F32), right], axis=0
-    )
+    total = total[1 : BX + 1] + more[1 : BX + 1]
+    total = total + jnp.concatenate([left, jnp.zeros((BX - 2, 3, A), F32), right], axis=0)
     return energy, -total.reshape(BX, 1, 3, A)
 
 

time: 148 us -> 143 us (0.966)
  waiting for transfers between devices: 18.8 us -> 11.3 us
  starting transfers between devices: 64.9 us -> 68.5 us
    ppermute x14, waiting for transfers between devices: 18.8 us -> 11.3 us  [along(): lax.ppermute(block, axis, [(i, i + step) for i in range(size) if 0 <= i +...]
    ppermute x14, starting transfers between devices: 64.9 us -> 68.5 us  [along(): lax.ppermute(block, axis, [(i, i + step) for i in range(size) if 0 <= i +...]
    unnamed x3 -> x15, local copies, waits for them, and re-layouts: 1.36 us -> 3.62 us
    concatenate x1 -> x0, local copies, waits for them, and re-layouts: 2.1 us -> none  [local(): jnp.concatenate([ws1, wv1, ws2, wv2, readout.reshape(1, C), jnp.zeros((7,...]
    pallas_call x7 -> x9, Pallas kernels: 56.3 us -> 57.3 us  [call(): pl.pallas_call(kernel, out_shape=[jax.ShapeDtypeStruct(s, d) for s, d in...]
  transfers between devices with their start and end apart: 14 -> 14, of which waited for: 6 -> 8; matrix products, arithmetic and copies ran while one was open for 3% -> 0% of each run, Pallas kernels for 11% -> 13%
where the time goes in v4:
time: 143 us; the launch traced here: 142 us
  starting transfers between devices  68.5 us (48%)
  Pallas kernels  57.3 us (40%)
  waiting for transfers between devices  11.3 us (8%)
  local copies, waits for them, and re-layouts  3.71 us (3%)
  between operations  1.57 us (1%)
    ppermute x14, starting transfers between devices, along(): lax.ppermute(block, axis, [(i, i + step) for i in range(size) if 0 <= i +...  68.5 us
    pallas_call x9, Pallas kernels, call(): pl.pallas_call(kernel, out_shape=[jax.ShapeDtypeStruct(s, d) for s, d in...  57.3 us
    ppermute x14, waiting for transfers between devices, along(): lax.ppermute(block, axis, [(i, i + step) for i in range(size) if 0 <= i +...  11.3 us
    unnamed x15, local copies, waits for them, and re-layouts  3.62 us
  transfers between devices with their start and end apart: 14, of which 8 were waited for; matrix products, arithmetic and copies ran while one was open for 0% of the time, Pallas kernels for 13%

profile of v4, /device:TPU:18, one launch (start us, length us, event | category | flops | bytes accessed | tf_op | source)
XLA Modules:
  0.0 142.5 jit_solution(1803739496847216460)
XLA Ops:
  1.3 1.9 %shard_map.140 = (f32[1,8,128]{2,1,0:T(8,128)}, f32[6,8,128]{2,1,0:T(8,128)}, f32[1,8,128]{2,1,0:T(8,128)}, s32[64]{0:T(128)}, f32[24,128]{1,0:T(8,128)}, /*index=5*/bf16[512,128]{1,0:T(8,128)(2,1)}) custom-call(f32[6,3,1,128]{3,2,1,0:T(1,128)} %bitcast.4, s32[6,1,128]{2,1,0:T(1,128)} %species_ref.1, s32[1,1,26]{2,1,0:T(1,128)} %codes_ref.1, ...), custom_call_target="tpu_custom_call" | custom-call | tf_op jit(solution)/shard_map/pallas_call | solution.py:815
  3.1 9.1 %collective-permute-start = (f32[1,8,128]{2,1,0:T(8,128)}, f32[1,8,128]{2,1,0:T(8,128)S(1)}, u32[]{:S(2)}, u32[]{:S(2)}) collective-permute-start(f32[1,8,128]{2,1,0:T(8,128)} %get-tuple-element.35), channel_id=1, source_target_pairs={{0,32},{32,64},{64,96},{96,128},{128,160},{160,192},{192,224},{1,3... | collective-permute-start | bytes 12296 | tf_op jit(solution)/shard_map/ppermute | solution.py:828
  12.3 1.9 %collective-permute-start.1 = (f32[1,8,128]{2,1,0:T(8,128)}, f32[1,8,128]{2,1,0:T(8,128)S(1)}, u32[]{:S(2)}, u32[]{:S(2)}) collective-permute-start(f32[1,8,128]{2,1,0:T(8,128)} %get-tuple-element.41), channel_id=1, source_target_pairs={{32,0},{64,32},{96,64},{128,96},{160,128},{192,160},{224,192},{33,... | collective-permute-start | bytes 12296 | tf_op jit(solution)/shard_map/ppermute | solution.py:828
  14.2 0.0 copy-start
  14.2 0.9 copy-done
  15.1 0.7 copy-done.2
  15.8 0.7 copy-done.4
  16.5 0.7 copy-done.5
  17.2 3.4 %shard_map.141.acc_own_ref = f32[6,512,128]{2,1,0:T(8,128)S(1)} custom-call(f32[6,8,128]{2,1,0:T(8,128)S(1)} %copy-done.4, s32[64]{0:T(128)S(1)} %copy-done.5, f32[24,128]{1,0:T(8,128)S(1)} %copy-done.2, bf16[512,128]{1,0:T(8,128)(2,1)S(1)} %copy-done), custom_call_target="tpu_custom_call" | custom-call | flops 4000000000 | bytes 1000000 | tf_op jit(solution)/shard_map/pallas_call | solution.py:815
  20.6 0.0 collective-permute-done
  20.6 1.3 collective-permute-done.1
  21.9 1.9 %collective-permute-start.2 = (f32[8,8,128]{2,1,0:T(8,128)S(1)}, f32[8,8,128]{2,1,0:T(8,128)S(1)}, u32[]{:S(2)}, u32[]{:S(2)}) collective-permute-start(f32[8,8,128]{2,1,0:T(8,128)S(1)} %constant_dynamic-update-slice_fusion.mid_ref.ext_mid_ref), channel_id=1, source_target_pairs={{0,1},{1,2},{2,3},{3,4},{4,5},{5,6},{6,7},{7,8},{8,9},{9,10},{10,1... | collective-permute-start | bytes 98312 | tf_op jit(solution)/shard_map/ppermute | solution.py:828
  23.8 6.3 %collective-permute-start.3 = (f32[8,8,128]{2,1,0:T(8,128)S(1)}, f32[8,8,128]{2,1,0:T(8,128)S(1)}, u32[]{:S(2)}, u32[]{:S(2)}) collective-permute-start(f32[8,8,128]{2,1,0:T(8,128)S(1)} %constant_dynamic-update-slice_fusion.mid_ref.ext_mid_ref), channel_id=1, source_target_pairs={{1,0},{2,1},{3,2},{4,3},{5,4},{6,5},{7,6},{8,7},{9,8},{10,9},{11,1... | collective-permute-start | bytes 98312 | tf_op jit(solution)/shard_map/ppermute | solution.py:828
  30.2 0.0 collective-permute-done.2.lo_ref
  30.2 1.6 %collective-permute-done.3.hi_ref = f32[8,8,128]{2,1,0:T(8,128)S(1)} collective-permute-done((f32[8,8,128]{2,1,0:T(8,128)S(1)}, f32[8,8,128]{2,1,0:T(8,128)S(1)}, u32[]{:S(2)}, u32[]{:S(2)}) %collective-permute-start.3) | collective-permute-done | bytes 32800 | tf_op jit(solution)/shard_map/ppermute | solution.py:828
  31.7 17.3 %shard_map.142 = (f32[6,128,128]{2,1,0:T(8,128)S(1)}, bf16[6,512,128]{2,1,0:T(8,128)(2,1)S(1)}, bf16[8,128,128]{2,1,0:T(8,128)(2,1)S(1)}, bf16[8,128,128]{2,1,0:...) custom-call(f32[8,8,128]{2,1,0:T(8,128)S(1)} %collective-permute-don, ...), custom_call_target="tpu_custom_call" | custom-call | tf_op jit(solution)/shard_map/pallas_call | solution.py:815
  49.1 1.9 %collective-permute-start.4 = (bf16[8,128,128]{2,1,0:T(8,128)(2,1)S(1)}, bf16[8,128,128]{2,1,0:T(8,128)(2,1)S(1)}, u32[]{:S(2)}, u32[]{:S(2)}) collective-permute-start(bf16[8,128,128]{2,1,0:T(8,128)(2,1)S(1)} %get-tuple-element.46), channel_id=1, source_target_pairs={{0,1},{1,2},{2,3},{3,4},{4,5},{5,6},{6,7},{7,8},{8,9},{9,10},{10,1... | collective-permute-start | bytes 786440 | tf_op jit(solution)/shard_map/ppermute | solution.py:828
  51.0 6.4 %collective-permute-start.5 = (bf16[8,128,128]{2,1,0:T(8,128)(2,1)S(1)}, bf16[8,128,128]{2,1,0:T(8,128)(2,1)S(1)}, u32[]{:S(2)}, u32[]{:S(2)}) collective-permute-start(bf16[8,128,128]{2,1,0:T(8,128)(2,1)S(1)} %get-tuple-element.47), channel_id=1, source_target_pairs={{1,0},{2,1},{3,2},{4,3},{5,4},{6,5},{7,6},{8,7},{9,8},{10,9},{11,1... | collective-permute-start | bytes 786440 | tf_op jit(solution)/shard_map/ppermute | solution.py:828
  57.4 0.0 copy-start.1
  57.4 0.0 copy-start.3
  57.4 3.6 %shard_map.143.mid_ref = f32[8,128,128]{2,1,0:T(8,128)S(1)} custom-call(f32[8,8,128]{2,1,0:T(8,128)S(1)} %constant_dynamic-update-slice_fusion.mid_ref.ext_mid_ref, s32[64]{0:T(128)S(1)} %get-tuple-element.43.list2_ref, bf16[6,2048,128]{2,1,0:T(8,128)(2,1)S(1)} %get-tuple-element.44.ready_ref, f32[9,3,128,128]{3,2,1,0:T(8,128)S(1)} %get-tuple-element.45.col_ref), custom_call_target="tpu_custom_call" | custom-call | flops 4000000000 | bytes 1000000 | tf_op jit(solution)/shard_map/pallas_call | solution.py:815
  61.0 0.0 collective-permute-done.4.below_ref
  61.0 1.0 collective-permute-done.5.above_ref
  62.0 11.3 %collective-permute-start.6 = (bf16[2,128,128]{2,1,0:T(8,128)(2,1)S(1)}, bf16[2,128,128]{2,1,0:T(8,128)(2,1)S(1)}, u32[]{:S(2)}, u32[]{:S(2)}) collective-permute-start(bf16[2,128,128]{2,1,0:T(8,128)(2,1)S(1)} %get-tuple-element.71), channel_id=1, source_target_pairs={{0,32},{32,64},{64,96},{96,128},{128,160},{160,192},{192,224},{1,3... | collective-permute-start | bytes 196616 | tf_op jit(solution)/shard_map/ppermute | solution.py:828
  73.3 1.9 %collective-permute-start.7 = (bf16[2,128,128]{2,1,0:T(8,128)(2,1)S(1)}, bf16[2,128,128]{2,1,0:T(8,128)(2,1)S(1)}, u32[]{:S(2)}, u32[]{:S(2)}) collective-permute-start(bf16[2,128,128]{2,1,0:T(8,128)(2,1)S(1)} %get-tuple-element.70), channel_id=1, source_target_pairs={{32,0},{64,32},{96,64},{128,96},{160,128},{192,160},{224,192},{33,... | collective-permute-start | bytes 196616 | tf_op jit(solution)/shard_map/ppermute | solution.py:828
  75.3 0.0 copy-done.1
  75.3 5.2 %shard_map.144 = (f32[6,1,128]{2,1,0:T(1,128)S(1)}, bf16[8,128,128]{2,1,0:T(8,128)(2,1)S(1)}, f32[6,512,128]{2,1,0:T(8,128)S(1)}, f32[6,3,128,128]{3,2,1,0:T(8,128)S(1)}, f32[9,3,8,128]{3,2,1,0:T(8,128)S(1)}) custom-call(f32[8,128,128]{2,1,0:T(8,128)S(1)} %shard_map.143.mid_ref, bf16[8,128,128]{2,1,0:T(8,128)(2,1)S(1)} %collective-permute-done.4.below_ref, ...), custom_call_target="tpu_custom_call" | custom-call | flops 4000000000 | bytes 1000000 | tf_op jit(solution)/shard_map/pallas_call | solution.py:815
  80.5 0.0 collective-permute-done.6.left_ref
  80.5 2.9 %collective-permute-done.7.right_ref = bf16[2,128,128]{2,1,0:T(8,128)(2,1)S(1)} collective-permute-done((bf16[2,128,128]{2,1,0:T(8,128)(2,1)S(1)}, bf16[2,128,128]{2,1,0:T(8,128)(2,1)S(1)}, u32[]{:S(2)}, u32[]{:S(2)}) %collective-permute-start.7) | collective-permute-done | bytes 65568 | tf_op jit(solution)/shard_map/ppermute | solution.py:828
  83.4 1.0 shard_map.145
  84.5 1.9 %collective-permute-start.8 = (bf16[8,128,128]{2,1,0:T(8,128)(2,1)S(1)}, bf16[8,128,128]{2,1,0:T(8,128)(2,1)S(1)}, u32[]{:S(2)}, u32[]{:S(2)}) collective-permute-start(bf16[8,128,128]{2,1,0:T(8,128)(2,1)S(1)} %get-tuple-element.61), channel_id=1, source_target_pairs={{0,1},{1,2},{2,3},{3,4},{4,5},{5,6},{6,7},{7,8},{8,9},{9,10},{10,1... | collective-permute-start | bytes 786440 | tf_op jit(solution)/shard_map/ppermute | solution.py:828
  86.4 6.3 %collective-permute-start.9 = (bf16[8,128,128]{2,1,0:T(8,128)(2,1)S(1)}, bf16[8,128,128]{2,1,0:T(8,128)(2,1)S(1)}, u32[]{:S(2)}, u32[]{:S(2)}) collective-permute-start(bf16[8,128,128]{2,1,0:T(8,128)(2,1)S(1)} %get-tuple-element.61), channel_id=1, source_target_pairs={{1,0},{2,1},{3,2},{4,3},{5,4},{6,5},{7,6},{8,7},{9,8},{10,9},{11,1... | collective-permute-start | bytes 786440 | tf_op jit(solution)/shard_map/ppermute | solution.py:828
  92.7 2.8 %shard_map.146 = (f32[6,512,128]{2,1,0:T(8,128)S(1)}, f32[6,3,128,128]{3,2,1,0:T(8,128)S(1)}, f32[9,3,8,128]{3,2,1,0:T(8,128)S(1)}) custom-call(f32[8,8,128]{2,1,0:T(8,128)S(1)} %constant_dynamic-update-slice_fusion.mid_ref.ext_mid_ref, s32[64]{0:T(128)S(1)} %get-tuple-element.43.list2_ref, f32[8,128,128]{2,1,0:T(8,128)S(1)} %get-tuple-element.53.in_mid_ref, ...), custom_call_target="tpu_custom_call" | custom-call | flops 4000000000 | bytes 1000000 | tf_op jit(solution)/shard_map/pallas_call | solution.py:815
  95.5 0.6 collective-permute-done.8.in_lo_ref
  96.2 0.4 collective-permute-done.9.in_hi_ref
  96.6 18.6 %shard_map.147 = (f32[8,3,128]{2,1,0:T(4,128)S(1)}, f32[8,3,128]{2,1,0:T(4,128)S(1)}, f32[8,3,128]{2,1,0:T(4,128)S(1)}, bf16[6,512,128]{2,1,0:T(8,128)(2,1)S(1)}) custom-call(f32[8,8,128]{2,1,0:T(8,128)S(1)} %collective-permute-done.2.lo_ref, f32[8,8,128]{2,1,0:T(8,128)S(1)} %constant_dynamic-update-slice_fusion.mid_ref.ext_mid_ref, ...), custom_call_target="tpu_custom_call" | custom-call | tf_op jit(solution)/shard_map/pallas_call | solution.py:815
  115.2 1.9 %collective-permute-start.10 = (f32[8,3,128]{2,1,0:T(4,128)S(1)}, f32[8,3,128]{2,1,0:T(4,128)S(1)}, u32[]{:S(2)}, u32[]{:S(2)}) collective-permute-start(f32[8,3,128]{2,1,0:T(4,128)S(1)} %get-tuple-element.65), channel_id=1, source_target_pairs={{0,1},{1,2},{2,3},{3,4},{4,5},{5,6},{6,7},{7,8},{8,9},{9,10},{10,1... | collective-permute-start | bytes 36872 | tf_op jit(solution)/shard_map/ppermute | solution.py:828
  117.2 6.9 %collective-permute-start.11 = (f32[8,3,128]{2,1,0:T(4,128)S(1)}, f32[8,3,128]{2,1,0:T(4,128)S(1)}, u32[]{:S(2)}, u32[]{:S(2)}) collective-permute-start(f32[8,3,128]{2,1,0:T(4,128)S(1)} %get-tuple-element.66), channel_id=1, source_target_pairs={{1,0},{2,1},{3,2},{4,3},{5,4},{6,5},{7,6},{8,7},{9,8},{10,9},{11,1... | collective-permute-start | bytes 36872 | tf_op jit(solution)/shard_map/ppermute | solution.py:828
  124.1 0.1 pad.1.clone
  124.2 0.0 collective-permute-done.10
  124.2 1.3 collective-permute-done.11
  125.5 6.9 %collective-permute-start.12 = (f32[1,3,128]{2,1,0:T(4,128)S(1)}, f32[1,3,128]{2,1,0:T(4,128)S(1)}, u32[]{:S(2)}, u32[]{:S(2)}) collective-permute-start(f32[1,3,128]{2,1,0:T(4,128)S(1)} %get-tuple-element.72), channel_id=1, source_target_pairs={{0,32},{32,64},{64,96},{96,128},{128,160},{160,192},{192,224},{1,3... | collective-permute-start | bytes 4616 | tf_op jit(solution)/shard_map/ppermute | solution.py:828
  132.4 3.7 %collective-permute-start.13 = (f32[1,3,128]{2,1,0:T(4,128)S(1)}, f32[1,3,128]{2,1,0:T(4,128)S(1)}, u32[]{:S(2)}, u32[]{:S(2)}) collective-permute-start(f32[1,3,128]{2,1,0:T(4,128)S(1)} %get-tuple-element.73), channel_id=1, source_target_pairs={{32,0},{64,32},{96,64},{128,96},{160,128},{192,160},{224,192},{33,... | collective-permute-start | bytes 4616 | tf_op jit(solution)/shard_map/ppermute | solution.py:828
  136.2 3.4 %shard_map.148 = f32[8,3,128]{2,1,0:T(4,128)S(1)} custom-call(f32[8,8,128]{2,1,0:T(8,128)S(1)} %constant_dynamic-update-slice_fusion.mid_ref.ext_mid_ref, s32[64]{0:T(128)S(1)} %get-tuple-element.52.list1_ref, bf16[25,512,128]{2,1,0:T(8,128)(2,1)S(1)} %get-tuple-element.62.scaled_s_ref, bf16[25,512,128]{2,1,0:T(8,128)(2,1)S(1)} %get-tuple-element.63.scaled_v_ref, ...), custom_call_target="tpu_custom_call" | custom-call | flops 4000000000 | bytes 1000000 | tf_op jit(solution)/shard_map/pallas_call | solution.py:815
  139.6 0.0 collective-permute-done.12
  139.6 2.2 %collective-permute-done.13 = f32[1,3,128]{2,1,0:T(4,128)S(1)} collective-permute-done((f32[1,3,128]{2,1,0:T(4,128)S(1)}, f32[1,3,128]{2,1,0:T(4,128)S(1)}, u32[]{:S(2)}, u32[]{:S(2)}) %collective-permute-start.13) | collective-permute-done | bytes 1568 | tf_op jit(solution)/shard_map/ppermute | solution.py:828
  141.8 0.1 fusion.6
  141.9 0.6 copy.15
  (11 shorter events, 0.1 us)
Async XLA Ops:
  3.1 17.4 %collective-permute-start = (f32[1,8,128]{2,1,0:T(8,128)}, f32[1,8,128]{2,1,0:T(8,128)S(1)}, u32[]{:S(2)}, u32[]{:S(2)}) collective-permute-start(f32[1,8,128]{2,1,0:T(8,128)} %get-tuple-element.35), channel_id=1, source_target_pairs={{0,32},{32,64},{64,96},{96,128},{128,160},{160,192},{192,224},{1,3... | collective-permute-start | bytes 12296 | tf_op jit(solution)/shard_map/ppermute | solution.py:828
  12.3 9.7 %collective-permute-start.1 = (f32[1,8,128]{2,1,0:T(8,128)}, f32[1,8,128]{2,1,0:T(8,128)S(1)}, u32[]{:S(2)}, u32[]{:S(2)}) collective-permute-start(f32[1,8,128]{2,1,0:T(8,128)} %get-tuple-element.41), channel_id=1, source_target_pairs={{32,0},{64,32},{96,64},{128,96},{160,128},{192,160},{224,192},{33,... | collective-permute-start | bytes 12296 | tf_op jit(solution)/shard_map/ppermute | solution.py:828
  14.2 0.9 copy-start
  15.1 0.7 copy-start.2
  15.8 0.7 copy-start.4
  16.5 0.7 copy-start.5
  21.9 8.3 %collective-permute-start.2 = (f32[8,8,128]{2,1,0:T(8,128)S(1)}, f32[8,8,128]{2,1,0:T(8,128)S(1)}, u32[]{:S(2)}, u32[]{:S(2)}) collective-permute-start(f32[8,8,128]{2,1,0:T(8,128)S(1)} %constant_dynamic-update-slice_fusion.mid_ref.ext_mid_ref), channel_id=1, source_target_pairs={{0,1},{1,2},{2,3},{3,4},{4,5},{5,6},{6,7},{7,8},{8,9},{9,10},{10,1... | collective-permute-start | bytes 98312 | tf_op jit(solution)/shard_map/ppermute | solution.py:828
  23.8 7.9 %collective-permute-start.3 = (f32[8,8,128]{2,1,0:T(8,128)S(1)}, f32[8,8,128]{2,1,0:T(8,128)S(1)}, u32[]{:S(2)}, u32[]{:S(2)}) collective-permute-start(f32[8,8,128]{2,1,0:T(8,128)S(1)} %constant_dynamic-update-slice_fusion.mid_ref.ext_mid_ref), channel_id=1, source_target_pairs={{1,0},{2,1},{3,2},{4,3},{5,4},{6,5},{7,6},{8,7},{9,8},{10,9},{11,1... | collective-permute-start | bytes 98312 | tf_op jit(solution)/shard_map/ppermute | solution.py:828
  49.1 11.9 %collective-permute-start.4 = (bf16[8,128,128]{2,1,0:T(8,128)(2,1)S(1)}, bf16[8,128,128]{2,1,0:T(8,128)(2,1)S(1)}, u32[]{:S(2)}, u32[]{:S(2)}) collective-permute-start(bf16[8,128,128]{2,1,0:T(8,128)(2,1)S(1)} %get-tuple-element.46), channel_id=1, source_target_pairs={{0,1},{1,2},{2,3},{3,4},{4,5},{5,6},{6,7},{7,8},{8,9},{9,10},{10,1... | collective-permute-start | bytes 786440 | tf_op jit(solution)/shard_map/ppermute | solution.py:828
  51.0 11.0 %collective-permute-start.5 = (bf16[8,128,128]{2,1,0:T(8,128)(2,1)S(1)}, bf16[8,128,128]{2,1,0:T(8,128)(2,1)S(1)}, u32[]{:S(2)}, u32[]{:S(2)}) collective-permute-start(bf16[8,128,128]{2,1,0:T(8,128)(2,1)S(1)} %get-tuple-element.47), channel_id=1, source_target_pairs={{1,0},{2,1},{3,2},{4,3},{5,4},{6,5},{7,6},{8,7},{9,8},{10,9},{11,1... | collective-permute-start | bytes 786440 | tf_op jit(solution)/shard_map/ppermute | solution.py:828
  57.4 17.9 %copy-start.1 = (bf16[512,128]{1,0:T(8,128)(2,1)S(1)}, bf16[512,128]{1,0:T(8,128)(2,1)}, u32[]{:S(2)}) copy-start(bf16[512,128]{1,0:T(8,128)(2,1)} %get-tuple-element.39.square_ref) | copy-start | bytes 393220
  57.4 17.9 %copy-start.3 = (f32[24,128]{1,0:T(8,128)S(1)}, f32[24,128]{1,0:T(8,128)}, u32[]{:S(2)}) copy-start(f32[24,128]{1,0:T(8,128)} %get-tuple-element.38.radial_ref) | copy-start | bytes 36868
  62.0 18.5 %collective-permute-start.6 = (bf16[2,128,128]{2,1,0:T(8,128)(2,1)S(1)}, bf16[2,128,128]{2,1,0:T(8,128)(2,1)S(1)}, u32[]{:S(2)}, u32[]{:S(2)}) collective-permute-start(bf16[2,128,128]{2,1,0:T(8,128)(2,1)S(1)} %get-tuple-element.71), channel_id=1, source_target_pairs={{0,32},{32,64},{64,96},{96,128},{128,160},{160,192},{192,224},{1,3... | collective-permute-start | bytes 196616 | tf_op jit(solution)/shard_map/ppermute | solution.py:828
  73.3 10.1 %collective-permute-start.7 = (bf16[2,128,128]{2,1,0:T(8,128)(2,1)S(1)}, bf16[2,128,128]{2,1,0:T(8,128)(2,1)S(1)}, u32[]{:S(2)}, u32[]{:S(2)}) collective-permute-start(bf16[2,128,128]{2,1,0:T(8,128)(2,1)S(1)} %get-tuple-element.70), channel_id=1, source_target_pairs={{32,0},{64,32},{96,64},{128,96},{160,128},{192,160},{224,192},{33,... | collective-permute-start | bytes 196616 | tf_op jit(solution)/shard_map/ppermute | solution.py:828
  84.5 11.7 %collective-permute-start.8 = (bf16[8,128,128]{2,1,0:T(8,128)(2,1)S(1)}, bf16[8,128,128]{2,1,0:T(8,128)(2,1)S(1)}, u32[]{:S(2)}, u32[]{:S(2)}) collective-permute-start(bf16[8,128,128]{2,1,0:T(8,128)(2,1)S(1)} %get-tuple-element.61), channel_id=1, source_target_pairs={{0,1},{1,2},{2,3},{3,4},{4,5},{5,6},{6,7},{7,8},{8,9},{9,10},{10,1... | collective-permute-start | bytes 786440 | tf_op jit(solution)/shard_map/ppermute | solution.py:828
  86.4 10.2 %collective-permute-start.9 = (bf16[8,128,128]{2,1,0:T(8,128)(2,1)S(1)}, bf16[8,128,128]{2,1,0:T(8,128)(2,1)S(1)}, u32[]{:S(2)}, u32[]{:S(2)}) collective-permute-start(bf16[8,128,128]{2,1,0:T(8,128)(2,1)S(1)} %get-tuple-element.61), channel_id=1, source_target_pairs={{1,0},{2,1},{3,2},{4,3},{5,4},{6,5},{7,6},{8,7},{9,8},{10,9},{11,1... | collective-permute-start | bytes 786440 | tf_op jit(solution)/shard_map/ppermute | solution.py:828
  115.2 8.9 %collective-permute-start.10 = (f32[8,3,128]{2,1,0:T(4,128)S(1)}, f32[8,3,128]{2,1,0:T(4,128)S(1)}, u32[]{:S(2)}, u32[]{:S(2)}) collective-permute-start(f32[8,3,128]{2,1,0:T(4,128)S(1)} %get-tuple-element.65), channel_id=1, source_target_pairs={{0,1},{1,2},{2,3},{3,4},{4,5},{5,6},{6,7},{7,8},{8,9},{9,10},{10,1... | collective-permute-start | bytes 36872 | tf_op jit(solution)/shard_map/ppermute | solution.py:828
  117.2 8.3 %collective-permute-start.11 = (f32[8,3,128]{2,1,0:T(4,128)S(1)}, f32[8,3,128]{2,1,0:T(4,128)S(1)}, u32[]{:S(2)}, u32[]{:S(2)}) collective-permute-start(f32[8,3,128]{2,1,0:T(4,128)S(1)} %get-tuple-element.66), channel_id=1, source_target_pairs={{1,0},{2,1},{3,2},{4,3},{5,4},{6,5},{7,6},{8,7},{9,8},{10,9},{11,1... | collective-permute-start | bytes 36872 | tf_op jit(solution)/shard_map/ppermute | solution.py:828
  125.5 14.1 %collective-permute-start.12 = (f32[1,3,128]{2,1,0:T(4,128)S(1)}, f32[1,3,128]{2,1,0:T(4,128)S(1)}, u32[]{:S(2)}, u32[]{:S(2)}) collective-permute-start(f32[1,3,128]{2,1,0:T(4,128)S(1)} %get-tuple-element.72), channel_id=1, source_target_pairs={{0,32},{32,64},{64,96},{96,128},{128,160},{160,192},{192,224},{1,3... | collective-permute-start | bytes 4616 | tf_op jit(solution)/shard_map/ppermute | solution.py:828
  132.4 9.4 %collective-permute-start.13 = (f32[1,3,128]{2,1,0:T(4,128)S(1)}, f32[1,3,128]{2,1,0:T(4,128)S(1)}, u32[]{:S(2)}, u32[]{:S(2)}) collective-permute-start(f32[1,3,128]{2,1,0:T(4,128)S(1)} %get-tuple-element.73), channel_id=1, source_target_pairs={{32,0},{64,32},{96,64},{128,96},{160,128},{192,160},{224,192},{33,... | collective-permute-start | bytes 4616 | tf_op jit(solution)/shard_map/ppermute | solution.py:828

commit v5 on v4

--- a/solution.py
+++ b/solution.py
@@ -17,14 +17,18 @@
 NT = (((1,), (1,)), ((), ()))
 E = 3 * EX
 
+def home_part(e):
+    return 0 if e % EX in (0, EX - 1) else 1 if e // EX != 1 else 2
+
+
 HOME_PAIRS = [
     [
         (h, (o % 3) * EX + h + o // 3, EX + 1 + h, o)
         for h in range(BX)
         for o in range(9)
-        if (o % 3 == 1 and 0 <= h + o // 3 - 1 < BX) == inner
+        if home_part((o % 3) * EX + h + o // 3) == part
     ]
-    for inner in (False, True)
+    for part in range(3)
 ]
 
 
@@ -57,12 +61,12 @@
 def pack_kernel(
     pos_ref, species_ref, codes_ref, count_ref, table_ref, ws1_ref, wv1_ref, ws2_ref, wv2_ref, ms_ref,
     mv_ref, m2_ref, readout_ref,
-    first_ref, out_ref, last_ref, list_ref, radial_ref, square_ref,
+    first_ref, out_ref, last_ref, list_ref, square_ref,
     wide_ref,
 ):
     for i, ref in enumerate((ws1_ref, wv1_ref, ws2_ref, wv2_ref)):
-        radial_ref[K * i : K * i + K, :] = ref[...]
-    radial_ref[4 * K : 4 * K + 1, :] = readout_ref[...]
+        out_ref[BX + i // 2, K * (i % 2) : K * (i % 2) + K, :] = ref[...]
+    out_ref[BX + 2] = jnp.broadcast_to(readout_ref[...], (8, C))
     for i, ref in enumerate((ms_ref, mv_ref, m2_ref)):
         square_ref[C * i : C * i + C, :] = ref[...]
     wide_ref[...] = jnp.zeros_like(wide_ref)
@@ -117,8 +121,7 @@
 
 def make_list(parts, masks_ref, list_ref):
     n = jnp.int32(0)
-    places = (MIDDLE, END) if len(parts) == 2 else (MIDDLE, THIRD, END)
-    for pairs, place in zip(parts, places):
+    for pairs, place in zip(parts, (MIDDLE, THIRD, END)):
         held = None
         for own, other, lister, o in sorted(pairs, key=lambda pair: pair[2]):
             if lister != held:
@@ -244,11 +247,11 @@
 
 
 def own_kernel(
-    own_ref, list_ref, radial_ref, square_ref,
+    own_ref, list_ref, square_ref,
     acc_ref,
     ext_ref, col_ref, scaled_s_ref, scaled_v_ref, tile_a_ref, tile_b_ref,
 ):
-    ws1_ref, wv1_ref, _, _, _ = radial_parts(radial_ref)
+    ws1_ref, wv1_ref, _, _, _ = radial_parts(own_ref)
     table = square_parts(square_ref)[3][...]
     for h in range(BX):
         ext_ref[h] = own_ref[h]
@@ -315,7 +318,7 @@
     acc_ref[...] = acc_own_ref[...]
     total_ref[...] = jnp.zeros_like(total_ref)
     first_sums(
-        list1_ref[MIDDLE], list1_ref, col_ref, EX + 1, lambda e: rows_of(ext_ref, e), lambda e: e,
+        list1_ref[THIRD], list1_ref, col_ref, EX + 1, lambda e: rows_of(ext_ref, e), lambda e: e,
         scaled_s_ref, scaled_v_ref, acc_ref, tile_a_ref, tile_b_ref,
     )
     for h in range(BX):
@@ -387,7 +390,7 @@
 
 
 def radial_parts(ref):
-    return [ref.at[pl.ds(K * i, K if i < 4 else 1), :] for i in range(5)]
+    return [ref.at[BX + i // 2, pl.ds(K * (i % 2), K if i < 4 else 1), :] for i in range(5)]
 
 
 def square_parts(ref):
@@ -610,9 +613,8 @@
 def backward_kernel(
     lo_ref, mid_ref, hi_ref, list1_ref, list2_ref, acc_in_ref, across_in_ref, down_in_ref, feat_ref,
     pre_ref, in_lo_ref, in_hi_ref, scaled_s_ref, scaled_v_ref, col_ref, radial_ref, square_ref,
-    out_lo_ref, out_mid_ref, out_hi_ref, inward_ref,
+    out_left_ref, out_right_ref, inward_ref, down_ref, across_ref,
     ext_ref, cot_s_ref, cot_v_ref, acc_ref, tile_a_ref, tile_b_ref, grad_a_ref, grad_b_ref,
-    down_ref, across_ref,
 ):
     _, _, ws2_ref, wv2_ref, readout_ref = radial_parts(radial_ref)
     ms_ref, mv_ref, _, _ = square_parts(square_ref)
@@ -639,11 +641,30 @@
         0, list1_ref[MIDDLE], list1_ref, col_ref, 0, lambda e: rows_of(ext_ref, e), inward_ref,
         scaled_s_ref, scaled_v_ref, across_ref, down_ref, grad_a_ref, grad_b_ref,
     )
+    for row in range(3):
+        for d in range(3):
+            out_left_ref[row, d : d + 1, :] = line_of(down_ref, None, row * EX, None, d)
+            out_right_ref[row, d : d + 1, :] = line_of(down_ref, None, row * EX + EX - 1, None, d)
+
+
+def backward_rows_kernel(
+    lo_ref, mid_ref, hi_ref, list1_ref, scaled_s_ref, scaled_v_ref, col_ref, inward_ref, down_in_ref,
+    across_in_ref,
+    out_lo_ref, out_mid_ref, out_hi_ref,
+    ext_ref, grad_a_ref, grad_b_ref, down_ref, across_ref,
+):
+    gather_ext(lo_ref, mid_ref, hi_ref, ext_ref)
+    down_ref[...] = down_in_ref[...]
+    across_ref[...] = across_in_ref[...]
+    first_moves(
+        list1_ref[MIDDLE], list1_ref[THIRD], list1_ref, col_ref, 0, lambda e: rows_of(ext_ref, e),
+        inward_ref, scaled_s_ref, scaled_v_ref, across_ref, down_ref, grad_a_ref, grad_b_ref,
+    )
     for row, ref in enumerate((out_lo_ref, out_mid_ref, out_hi_ref)):
-        for x in range(EX):
+        for h in range(BX):
             for d in range(3):
-                line = line_of(down_ref, across_ref, row * EX + x, x if row == 1 else None, d)
-                ref[x, d : d + 1, :] = line
+                line = line_of(down_ref, across_ref, row * EX + h + 1, h + 1 if row == 1 else None, d)
+                ref[h, d : d + 1, :] = line
 
 
 def backward_inner_kernel(
@@ -656,7 +677,7 @@
     down_ref[...] = jnp.zeros_like(down_ref)
     across_ref[...] = jnp.zeros_like(across_ref)
     first_moves(
-        list1_ref[MIDDLE], list1_ref[END], list1_ref, col_ref, EX, lambda e: rows_of(ext_ref, e),
+        list1_ref[THIRD], list1_ref[END], list1_ref, col_ref, EX, lambda e: rows_of(ext_ref, e),
         inward_ref, scaled_s_ref, scaled_v_ref, across_ref, down_ref, grad_a_ref, grad_b_ref,
     )
     for x in range(EX):
@@ -746,7 +767,7 @@
             pltpu.VMEM((4 * A, K * A), BF16),
             pltpu.VMEM((4 * A, K * A), BF16),
         ],
-        in_specs=[VMEM, SMEM, VMEM, VMEM],
+        in_specs=[VMEM, SMEM, VMEM],
         cost=LONG,
     )
 
@@ -777,7 +798,13 @@
     return call(
         backward_kernel,
         args,
-        [*[((EX, 3, A), F32)] * 3, ((BX, 4 * A, C), BF16)],
+        [
+            ((3, 3, A), F32),
+            ((3, 3, A), F32),
+            ((BX, 4 * A, C), BF16),
+            ((E + 1, 3, 8, A), F32),
+            ((BX, 3, A, 128), F32),
+        ],
         [
             pltpu.VMEM((E + 8, 8, A), F32),
             pltpu.VMEM((E + 1, K * A, C), BF16),
@@ -787,10 +814,25 @@
             pltpu.VMEM((4 * A, K * A), BF16),
             pltpu.VMEM((4 * A, K * A), F32),
             pltpu.VMEM((4 * A, K * A), F32),
+        ],
+        in_specs=[VMEM] * 3 + [SMEM] * 2 + [VMEM] * 12,
+    )
+
+
+def backward_rows_call(*args):
+    return call(
+        backward_rows_kernel,
+        args,
+        [((BX, 3, A), F32)] * 3,
+        [
+            pltpu.VMEM((E + 8, 8, A), F32),
+            pltpu.VMEM((4 * A, K * A), F32),
+            pltpu.VMEM((4 * A, K * A), F32),
             pltpu.VMEM((E + 1, 3, 8, A), F32),
             pltpu.VMEM((BX, 3, A, 128), F32),
         ],
-        in_specs=[VMEM] * 3 + [SMEM] * 2 + [VMEM] * 12,
+        in_specs=[VMEM] * 3 + [SMEM] + [VMEM] * 6,
+        cost=LONG,
     )
 
 
@@ -835,7 +877,7 @@
 def local(
     positions, species, pair_codes, pair_count, embed_table, ws1, wv1, ws2, wv2, ms, mv, m2, readout
 ):
-    first, own, last, own_list, radial, square = call(
+    first, radial, last, own_list, square = call(
         pack_kernel,
         (
             positions.transpose(0, 2, 1, 3), species, pair_codes, pair_count, embed_table, ws1, wv1,
@@ -843,21 +885,20 @@
         ),
         [
             ((1, 8, A), F32),
-            ((BX, 8, A), F32),
+            ((BX + 3, 8, A), F32),
             ((1, 8, A), F32),
             ((64,), jnp.int32),
-            ((24, C), F32),
             ((4 * C, C), BF16),
         ],
         [pltpu.VMEM((C, C), F32)],
         in_specs=[VMEM] * 2 + [SMEM] * 2 + [VMEM] * 9,
-        out_specs=[VMEM] * 3 + [SMEM] + [VMEM] * 2,
+        out_specs=[VMEM] * 3 + [SMEM, VMEM],
         params=pltpu.CompilerParams(vmem_limit_bytes=60 * 1024 * 1024),
     )
     left, right = both(last, first, "gx")
-    (acc,) = own_call(own, own_list, radial, square)
-    own, acc = lax.optimization_barrier((own, acc))
-    ext_mid = jnp.concatenate([left, own, right], axis=0)
+    (acc,) = own_call(radial, own_list, square)
+    radial, acc = lax.optimization_barrier((radial, acc))
+    ext_mid = jnp.concatenate([left, radial[:BX], right], axis=0)
     ext_lo, ext_hi = both(ext_mid, ext_mid, "gy")
     ext = (ext_lo, ext_mid, ext_hi)
     pre, feat, lo, hi, scaled_s, scaled_v, ready, col, list1, list2 = forward_call(
@@ -877,15 +918,20 @@
     )
     in_lo, in_hi = both(inner, inner, "gy")
     held = backward_outer_two_call(ext_mid, list2, inner_own, feat, col, radial, *held)
-    lo, mid, hi, inward = backward_call(
+    left, right, inward, down, across = backward_call(
         *ext, list1, list2, *held, feat, pre, in_lo, in_hi, scaled_s, scaled_v, col, radial, square
     )
+    left, right = both(right, left, "gx")
+    lo, mid, hi = backward_rows_call(
+        *ext, list1, scaled_s, scaled_v, col, inward, down, across
+    )
+    pad = lambda row: jnp.concatenate(
+        [left[row : row + 1], jnp.zeros((BX - 2, 3, A), F32), right[row : row + 1]], axis=0
+    )
+    lo, hi = lo + pad(0), hi + pad(2)
     below, above = both(hi, lo, "gy")
     (more,) = backward_inner_call(ext_mid, list1, scaled_s, scaled_v, col, inward)
-    total = mid + below + above
-    left, right = both(total[EX - 1 :], total[:1], "gx")
-    total = total[1 : BX + 1] + more[1 : BX + 1]
-    total = total + jnp.concatenate([left, jnp.zeros((BX - 2, 3, A), F32), right], axis=0)
+    total = mid + pad(1) + below + above + more[1 : BX + 1]
     return energy, -total.reshape(BX, 1, 3, A)
 
 

time: 143 us -> 141 us (0.986)
  waiting for transfers between devices: 11.3 us -> 3.12 us
  Pallas kernels: 57.3 us -> 61.6 us
    ppermute x14, waiting for transfers between devices: 11.3 us -> 3.12 us  [along(): lax.ppermute(block, axis, [(i, i + step) for i in range(size) if 0 <= i +...]
    pallas_call x9 -> x10, Pallas kernels: 57.3 us -> 61.6 us  [call(): pl.pallas_call(kernel, out_shape=[jax.ShapeDtypeStruct(s, d) for s, d in...]
    unnamed x15 -> x11, local copies, waits for them, and re-layouts: 3.62 us -> 2.94 us
  transfers between devices with their start and end apart: 14 -> 14, of which waited for: 8 -> 3; matrix products, arithmetic and copies ran while one was open for 0% -> 0% of each run, Pallas kernels for 13% -> 21%
where the time goes in v5:
time: 141 us; the launch traced here: 139 us
  starting transfers between devices  69.8 us (50%)
  Pallas kernels  61.6 us (44%)
  waiting for transfers between devices  3.12 us (2%)
  local copies, waits for them, and re-layouts  3.03 us (2%)
  between operations  1.61 us (1%)
    ppermute x14, starting transfers between devices, along(): lax.ppermute(block, axis, [(i, i + step) for i in range(size) if 0 <= i +...  69.8 us
    pallas_call x10, Pallas kernels, call(): pl.pallas_call(kernel, out_shape=[jax.ShapeDtypeStruct(s, d) for s, d in...  61.6 us
    ppermute x14, waiting for transfers between devices, along(): lax.ppermute(block, axis, [(i, i + step) for i in range(size) if 0 <= i +...  3.12 us
    unnamed x11, local copies, waits for them, and re-layouts  2.94 us
  transfers between devices with their start and end apart: 14, of which 3 were waited for; matrix products, arithmetic and copies ran while one was open for 0% of the time, Pallas kernels for 21%

profile of v5, /device:TPU:18, one launch (start us, length us, event | category | flops | bytes accessed | tf_op | source)
XLA Modules:
  0.0 139.3 jit_solution(11484174585507357967)
XLA Ops:
  1.3 1.9 %shard_map.140 = (f32[1,8,128]{2,1,0:T(8,128)}, f32[9,8,128]{2,1,0:T(8,128)}, f32[1,8,128]{2,1,0:T(8,128)}, s32[64]{0:T(128)}, bf16[512,128]{1,0:T(8,128)(2,1)}) custom-call(f32[6,3,1,128]{3,2,1,0:T(1,128)} %bitcast.4, s32[6,1,128]{2,1,0:T(1,128)} %species_ref.1, s32[1,1,26]{2,1,0:T(1,128)} %codes_ref.1, s32[1,1]{1,0:T(1,128)S(6)} %copy.16.count_ref, ...), custom_call_target="tpu_custom_call" | custom-call | tf_op jit(solution)/shard_map/pallas_call | solution.py:857
  3.1 9.1 %collective-permute-start = (f32[1,8,128]{2,1,0:T(8,128)}, f32[1,8,128]{2,1,0:T(8,128)S(1)}, u32[]{:S(2)}, u32[]{:S(2)}) collective-permute-start(f32[1,8,128]{2,1,0:T(8,128)} %get-tuple-element.38), channel_id=1, source_target_pairs={{0,32},{32,64},{64,96},{96,128},{128,160},{160,192},{192,224},{1,3... | collective-permute-start | bytes 12296 | tf_op jit(solution)/shard_map/ppermute | solution.py:870
  12.3 1.9 %collective-permute-start.1 = (f32[1,8,128]{2,1,0:T(8,128)}, f32[1,8,128]{2,1,0:T(8,128)S(1)}, u32[]{:S(2)}, u32[]{:S(2)}) collective-permute-start(f32[1,8,128]{2,1,0:T(8,128)} %get-tuple-element.43), channel_id=1, source_target_pairs={{32,0},{64,32},{96,64},{128,96},{160,128},{192,160},{224,192},{33,... | collective-permute-start | bytes 12296 | tf_op jit(solution)/shard_map/ppermute | solution.py:870
  14.2 0.0 copy-start
  14.2 0.9 copy-done
  15.1 0.8 copy-done.2
  15.9 0.7 copy-done.4
  16.5 4.0 %shard_map.141.acc_own_ref = f32[6,512,128]{2,1,0:T(8,128)S(1)} custom-call(f32[9,8,128]{2,1,0:T(8,128)S(1)} %copy-done.2, s32[64]{0:T(128)S(1)} %copy-done.4, bf16[512,128]{1,0:T(8,128)(2,1)S(1)} %copy-done), custom_call_target="tpu_custom_call" | custom-call | flops 4000000000 | bytes 1000000 | tf_op jit(solution)/shard_map/pallas_call | solution.py:857
  20.6 0.0 collective-permute-done
  20.6 1.3 collective-permute-done.1
  21.9 1.9 %collective-permute-start.2 = (f32[8,8,128]{2,1,0:T(8,128)S(1)}, f32[8,8,128]{2,1,0:T(8,128)S(1)}, u32[]{:S(2)}, u32[]{:S(2)}) collective-permute-start(f32[8,8,128]{2,1,0:T(8,128)S(1)} %pad_maximum_fusion.mid_ref.ext_mid_ref), channel_id=1, source_target_pairs={{0,1},{1,2},{2,3},{3,4},{4,5},{5,6},{6,7},{7,8},{8,9},{9,10},{10,1... | collective-permute-start | bytes 98312 | tf_op jit(solution)/shard_map/ppermute | solution.py:870
  23.8 6.3 %collective-permute-start.3 = (f32[8,8,128]{2,1,0:T(8,128)S(1)}, f32[8,8,128]{2,1,0:T(8,128)S(1)}, u32[]{:S(2)}, u32[]{:S(2)}) collective-permute-start(f32[8,8,128]{2,1,0:T(8,128)S(1)} %pad_maximum_fusion.mid_ref.ext_mid_ref), channel_id=1, source_target_pairs={{1,0},{2,1},{3,2},{4,3},{5,4},{6,5},{7,6},{8,7},{9,8},{10,9},{11,1... | collective-permute-start | bytes 98312 | tf_op jit(solution)/shard_map/ppermute | solution.py:870
  30.2 0.1 pad.7.clone
  30.3 0.0 collective-permute-done.2.lo_ref
  30.3 1.5 %collective-permute-done.3.hi_ref = f32[8,8,128]{2,1,0:T(8,128)S(1)} collective-permute-done((f32[8,8,128]{2,1,0:T(8,128)S(1)}, f32[8,8,128]{2,1,0:T(8,128)S(1)}, u32[]{:S(2)}, u32[]{:S(2)}) %collective-permute-start.3) | collective-permute-done | bytes 32800 | tf_op jit(solution)/shard_map/ppermute | solution.py:870
  31.7 17.3 %shard_map.142 = (f32[6,128,128]{2,1,0:T(8,128)S(1)}, bf16[6,512,128]{2,1,0:T(8,128)(2,1)S(1)}, bf16[8,128,128]{2,1,0:T(8,128)(2,1)S(1)}, bf16[8,128,128]{2,1,0:...) custom-call(f32[8,8,128]{2,1,0:T(8,128)S(1)} %collective-permute-don, ...), custom_call_target="tpu_custom_call" | custom-call | tf_op jit(solution)/shard_map/pallas_call | solution.py:857
  49.1 1.9 %collective-permute-start.4 = (bf16[8,128,128]{2,1,0:T(8,128)(2,1)S(1)}, bf16[8,128,128]{2,1,0:T(8,128)(2,1)S(1)}, u32[]{:S(2)}, u32[]{:S(2)}) collective-permute-start(bf16[8,128,128]{2,1,0:T(8,128)(2,1)S(1)} %get-tuple-element.48), channel_id=1, source_target_pairs={{0,1},{1,2},{2,3},{3,4},{4,5},{5,6},{6,7},{7,8},{8,9},{9,10},{10,1... | collective-permute-start | bytes 786440 | tf_op jit(solution)/shard_map/ppermute | solution.py:870
  51.0 8.4 %collective-permute-start.5 = (bf16[8,128,128]{2,1,0:T(8,128)(2,1)S(1)}, bf16[8,128,128]{2,1,0:T(8,128)(2,1)S(1)}, u32[]{:S(2)}, u32[]{:S(2)}) collective-permute-start(bf16[8,128,128]{2,1,0:T(8,128)(2,1)S(1)} %get-tuple-element.49), channel_id=1, source_target_pairs={{1,0},{2,1},{3,2},{4,3},{5,4},{6,5},{7,6},{8,7},{9,8},{10,9},{11,1... | collective-permute-start | bytes 786440 | tf_op jit(solution)/shard_map/ppermute | solution.py:870
  59.5 4.2 %shard_map.143.mid_ref = f32[8,128,128]{2,1,0:T(8,128)S(1)} custom-call(f32[8,8,128]{2,1,0:T(8,128)S(1)} %pad_maximum_fusion.mid_ref.ext_mid_ref, s32[64]{0:T(128)S(1)} %get-tuple-element.45.list2_ref, bf16[6,2048,128]{2,1,0:T(8,128)(2,1)S(1)} %get-tuple-element.46.ready_ref, f32[9,3,128,128]{3,2,1,0:T(8,128)S(1)} %get-tuple-element.47.col_ref), custom_call_target="tpu_custom_call" | custom-call | flops 4000000000 | bytes 1000000 | tf_op jit(solution)/shard_map/pallas_call | solution.py:857
  63.7 0.0 collective-permute-done.4.below_ref
  63.7 0.3 collective-permute-done.5.above_ref
  64.1 5.0 %collective-permute-start.6 = (bf16[2,128,128]{2,1,0:T(8,128)(2,1)S(1)}, bf16[2,128,128]{2,1,0:T(8,128)(2,1)S(1)}, u32[]{:S(2)}, u32[]{:S(2)}) collective-permute-start(bf16[2,128,128]{2,1,0:T(8,128)(2,1)S(1)} %get-tuple-element.77), channel_id=1, source_target_pairs={{0,32},{32,64},{64,96},{96,128},{128,160},{160,192},{192,224},{1,3... | collective-permute-start | bytes 196616 | tf_op jit(solution)/shard_map/ppermute | solution.py:870
  69.1 5.6 %collective-permute-start.7 = (bf16[2,128,128]{2,1,0:T(8,128)(2,1)S(1)}, bf16[2,128,128]{2,1,0:T(8,128)(2,1)S(1)}, u32[]{:S(2)}, u32[]{:S(2)}) collective-permute-start(bf16[2,128,128]{2,1,0:T(8,128)(2,1)S(1)} %get-tuple-element.76), channel_id=1, source_target_pairs={{32,0},{64,32},{96,64},{128,96},{160,128},{192,160},{224,192},{33,... | collective-permute-start | bytes 196616 | tf_op jit(solution)/shard_map/ppermute | solution.py:870
  74.7 0.0 copy-done.1
  74.7 0.0 copy-done.3
  74.8 5.2 %shard_map.144 = (f32[6,1,128]{2,1,0:T(1,128)S(1)}, bf16[8,128,128]{2,1,0:T(8,128)(2,1)S(1)}, f32[6,512,128]{2,1,0:T(8,128)S(1)}, f32[6,3,128,128]{3,2,1,0:T(8,128)S(1)}, f32[9,3,8,128]{3,2,1,0:T(8,128)S(1)}) custom-call(f32[8,128,128]{2,1,0:T(8,128)S(1)} %shard_map.143.mid_ref, bf16[8,128,128]{2,1,0:T(8,128)(2,1)S(1)} %collective-permute-done.4.below_ref, ...), custom_call_target="tpu_custom_call" | custom-call | flops 4000000000 | bytes 1000000 | tf_op jit(solution)/shard_map/pallas_call | solution.py:857
  79.9 0.0 collective-permute-done.6.left_ref
  79.9 0.0 collective-permute-done.7.right_ref
  80.0 1.0 shard_map.145
  81.0 1.9 %collective-permute-start.8 = (bf16[8,128,128]{2,1,0:T(8,128)(2,1)S(1)}, bf16[8,128,128]{2,1,0:T(8,128)(2,1)S(1)}, u32[]{:S(2)}, u32[]{:S(2)}) collective-permute-start(bf16[8,128,128]{2,1,0:T(8,128)(2,1)S(1)} %get-tuple-element.65), channel_id=1, source_target_pairs={{0,1},{1,2},{2,3},{3,4},{4,5},{5,6},{6,7},{7,8},{8,9},{9,10},{10,1... | collective-permute-start | bytes 786440 | tf_op jit(solution)/shard_map/ppermute | solution.py:870
  82.9 6.3 %collective-permute-start.9 = (bf16[8,128,128]{2,1,0:T(8,128)(2,1)S(1)}, bf16[8,128,128]{2,1,0:T(8,128)(2,1)S(1)}, u32[]{:S(2)}, u32[]{:S(2)}) collective-permute-start(bf16[8,128,128]{2,1,0:T(8,128)(2,1)S(1)} %get-tuple-element.65), channel_id=1, source_target_pairs={{1,0},{2,1},{3,2},{4,3},{5,4},{6,5},{7,6},{8,7},{9,8},{10,9},{11,1... | collective-permute-start | bytes 786440 | tf_op jit(solution)/shard_map/ppermute | solution.py:870
  89.3 3.9 %shard_map.146 = (f32[6,512,128]{2,1,0:T(8,128)S(1)}, f32[6,3,128,128]{3,2,1,0:T(8,128)S(1)}, f32[9,3,8,128]{3,2,1,0:T(8,128)S(1)}) custom-call(f32[8,8,128]{2,1,0:T(8,128)S(1)} %pad_maximum_fusion.mid_ref.ext_mid_ref, s32[64]{0:T(128)S(1)} %get-tuple-element.45.list2_ref, f32[8,128,128]{2,1,0:T(8,128)S(1)} %get-tuple-element.57.in_mid_ref, ...), custom_call_target="tpu_custom_call" | custom-call | flops 4000000000 | bytes 1000000 | tf_op jit(solution)/shard_map/pallas_call | solution.py:857
  93.1 0.0 collective-permute-done.8.in_lo_ref
  93.1 0.0 collective-permute-done.9.in_hi_ref
  93.1 12.5 %shard_map.147 = (f32[3,3,128]{2,1,0:T(4,128)S(1)}, f32[3,3,128]{2,1,0:T(4,128)S(1)}, bf16[6,512,128]{2,1,0:T(8,128)(2,1)S(1)}, f32[25,3,8,128]{3,2,1,0:T(8,128)S(1)}, f32[6,3,128,128]{3,2,1,0:T(8,128)S(1)}) custom-call(f32[8,8,128]{2,1,0:T(8,128)S(1)} %collective-permute-done.2.lo_ref, f32[8,8,128]{2,1,0:T(8,128)S(1)} %pad_maximum_fusion.mid_ref.ext_mid_ref, ...), custom_call_target="tpu_custom_call" | custom-call | tf_op jit(solution)/shard_map/pallas_call | solution.py:857
  105.7 3.2 %collective-permute-start.10 = (f32[3,3,128]{2,1,0:T(4,128)S(1)}, f32[3,3,128]{2,1,0:T(4,128)S(1)}, u32[]{:S(2)}, u32[]{:S(2)}) collective-permute-start(f32[3,3,128]{2,1,0:T(4,128)S(1)} %get-tuple-element.70), channel_id=1, source_target_pairs={{0,32},{32,64},{64,96},{96,128},{128,160},{160,192},{192,224},{1,3... | collective-permute-start | bytes 13832 | tf_op jit(solution)/shard_map/ppermute | solution.py:870
  108.9 7.4 %collective-permute-start.11 = (f32[3,3,128]{2,1,0:T(4,128)S(1)}, f32[3,3,128]{2,1,0:T(4,128)S(1)}, u32[]{:S(2)}, u32[]{:S(2)}) collective-permute-start(f32[3,3,128]{2,1,0:T(4,128)S(1)} %get-tuple-element.71), channel_id=1, source_target_pairs={{32,0},{64,32},{96,64},{128,96},{160,128},{192,160},{224,192},{33,... | collective-permute-start | bytes 13832 | tf_op jit(solution)/shard_map/ppermute | solution.py:870
  116.4 7.3 %shard_map.148 = (f32[6,3,128]{2,1,0:T(4,128)S(1)}, f32[6,3,128]{2,1,0:T(4,128)S(1)}, f32[6,3,128]{2,1,0:T(4,128)S(1)}) custom-call(f32[8,8,128]{2,1,0:T(8,128)S(1)} %collective-permute-done.2.lo_ref, f32[8,8,128]{2,1,0:T(8,128)S(1)} %pad_maximum_fusion.mid_ref.ext_mid_ref, f32[8,8,128]{2,1,0:T(8,128)S(1)} %collective-permute-done.3.hi_ref, ...), custom_call_target="tpu_custom_call" | custom-call | flops 4000000000 | bytes 1000000 | tf_op jit(solution)/shard_map/pallas_call | solution.py:857
  123.7 0.0 collective-permute-done.10
  123.7 0.0 collective-permute-done.11
  123.7 0.1 maximum_add_fusion.1
  123.8 1.9 %collective-permute-start.12 = (f32[6,3,128]{2,1,0:T(4,128)S(1)}, f32[6,3,128]{2,1,0:T(4,128)S(1)}, u32[]{:S(2)}, u32[]{:S(2)}) collective-permute-start(f32[6,3,128]{2,1,0:T(4,128)S(1)} %get-tuple-element.84), channel_id=1, source_target_pairs={{0,1},{1,2},{2,3},{3,4},{4,5},{5,6},{6,7},{7,8},{8,9},{9,10},{10,1... | collective-permute-start | bytes 27656 | tf_op jit(solution)/shard_map/ppermute | solution.py:870
  125.7 8.7 %collective-permute-start.13 = (f32[6,3,128]{2,1,0:T(4,128)S(1)}, f32[6,3,128]{2,1,0:T(4,128)S(1)}, u32[]{:S(2)}, u32[]{:S(2)}) collective-permute-start(f32[6,3,128]{2,1,0:T(4,128)S(1)} %get-tuple-element.85), channel_id=1, source_target_pairs={{1,0},{2,1},{3,2},{4,3},{5,4},{6,5},{7,6},{8,7},{9,8},{10,9},{11,1... | collective-permute-start | bytes 27656 | tf_op jit(solution)/shard_map/ppermute | solution.py:870
  134.4 4.2 %shard_map.149 = f32[8,3,128]{2,1,0:T(4,128)S(1)} custom-call(f32[8,8,128]{2,1,0:T(8,128)S(1)} %pad_maximum_fusion.mid_ref.ext_mid_ref, s32[64]{0:T(128)S(1)} %get-tuple-element.54.list1_ref, bf16[25,512,128]{2,1,0:T(8,128)(2,1)S(1)} %get-tuple-element.55.scaled_s_ref, bf16[25,512,128]{2,1,0:T(8,128)(2,1)S(1)} %get-tuple-element.56.scaled_v_ref, ...), custom_call_target="tpu_custom_call" | custom-call | flops 4000000000 | bytes 1000000 | tf_op jit(solution)/shard_map/pallas_call | solution.py:857
  138.6 0.0 collective-permute-done.12
  138.6 0.0 collective-permute-done.13
  138.6 0.1 fusion.5
  138.7 0.6 copy.15
  (10 shorter events, 0.1 us)
Async XLA Ops:
  3.1 17.4 %collective-permute-start = (f32[1,8,128]{2,1,0:T(8,128)}, f32[1,8,128]{2,1,0:T(8,128)S(1)}, u32[]{:S(2)}, u32[]{:S(2)}) collective-permute-start(f32[1,8,128]{2,1,0:T(8,128)} %get-tuple-element.38), channel_id=1, source_target_pairs={{0,32},{32,64},{64,96},{96,128},{128,160},{160,192},{192,224},{1,3... | collective-permute-start | bytes 12296 | tf_op jit(solution)/shard_map/ppermute | solution.py:870
  12.3 9.7 %collective-permute-start.1 = (f32[1,8,128]{2,1,0:T(8,128)}, f32[1,8,128]{2,1,0:T(8,128)S(1)}, u32[]{:S(2)}, u32[]{:S(2)}) collective-permute-start(f32[1,8,128]{2,1,0:T(8,128)} %get-tuple-element.43), channel_id=1, source_target_pairs={{32,0},{64,32},{96,64},{128,96},{160,128},{192,160},{224,192},{33,... | collective-permute-start | bytes 12296 | tf_op jit(solution)/shard_map/ppermute | solution.py:870
  14.2 0.9 copy-start
  15.1 0.8 copy-start.2
  15.9 0.7 copy-start.4
  21.9 8.4 %collective-permute-start.2 = (f32[8,8,128]{2,1,0:T(8,128)S(1)}, f32[8,8,128]{2,1,0:T(8,128)S(1)}, u32[]{:S(2)}, u32[]{:S(2)}) collective-permute-start(f32[8,8,128]{2,1,0:T(8,128)S(1)} %pad_maximum_fusion.mid_ref.ext_mid_ref), channel_id=1, source_target_pairs={{0,1},{1,2},{2,3},{3,4},{4,5},{5,6},{6,7},{7,8},{8,9},{9,10},{10,1... | collective-permute-start | bytes 98312 | tf_op jit(solution)/shard_map/ppermute | solution.py:870
  23.8 7.9 %collective-permute-start.3 = (f32[8,8,128]{2,1,0:T(8,128)S(1)}, f32[8,8,128]{2,1,0:T(8,128)S(1)}, u32[]{:S(2)}, u32[]{:S(2)}) collective-permute-start(f32[8,8,128]{2,1,0:T(8,128)S(1)} %pad_maximum_fusion.mid_ref.ext_mid_ref), channel_id=1, source_target_pairs={{1,0},{2,1},{3,2},{4,3},{5,4},{6,5},{7,6},{8,7},{9,8},{10,9},{11,1... | collective-permute-start | bytes 98312 | tf_op jit(solution)/shard_map/ppermute | solution.py:870
  49.1 14.6 %collective-permute-start.4 = (bf16[8,128,128]{2,1,0:T(8,128)(2,1)S(1)}, bf16[8,128,128]{2,1,0:T(8,128)(2,1)S(1)}, u32[]{:S(2)}, u32[]{:S(2)}) collective-permute-start(bf16[8,128,128]{2,1,0:T(8,128)(2,1)S(1)} %get-tuple-element.48), channel_id=1, source_target_pairs={{0,1},{1,2},{2,3},{3,4},{4,5},{5,6},{6,7},{7,8},{8,9},{9,10},{10,1... | collective-permute-start | bytes 786440 | tf_op jit(solution)/shard_map/ppermute | solution.py:870
  51.0 13.0 %collective-permute-start.5 = (bf16[8,128,128]{2,1,0:T(8,128)(2,1)S(1)}, bf16[8,128,128]{2,1,0:T(8,128)(2,1)S(1)}, u32[]{:S(2)}, u32[]{:S(2)}) collective-permute-start(bf16[8,128,128]{2,1,0:T(8,128)(2,1)S(1)} %get-tuple-element.49), channel_id=1, source_target_pairs={{1,0},{2,1},{3,2},{4,3},{5,4},{6,5},{7,6},{8,7},{9,8},{10,9},{11,1... | collective-permute-start | bytes 786440 | tf_op jit(solution)/shard_map/ppermute | solution.py:870
  59.4 15.3 %copy-start.1 = (bf16[512,128]{1,0:T(8,128)(2,1)S(1)}, bf16[512,128]{1,0:T(8,128)(2,1)}, u32[]{:S(2)}) copy-start(bf16[512,128]{1,0:T(8,128)(2,1)} %get-tuple-element.41.square_ref) | copy-start | bytes 393220
  59.5 15.3 %copy-start.3 = (f32[9,8,128]{2,1,0:T(8,128)S(1)}, f32[9,8,128]{2,1,0:T(8,128)}, u32[]{:S(2)}) copy-start(f32[9,8,128]{2,1,0:T(8,128)} %get-tuple-element.42.own_ref.radial_ref) | copy-start | bytes 110596
  64.1 15.9 %collective-permute-start.6 = (bf16[2,128,128]{2,1,0:T(8,128)(2,1)S(1)}, bf16[2,128,128]{2,1,0:T(8,128)(2,1)S(1)}, u32[]{:S(2)}, u32[]{:S(2)}) collective-permute-start(bf16[2,128,128]{2,1,0:T(8,128)(2,1)S(1)} %get-tuple-element.77), channel_id=1, source_target_pairs={{0,32},{32,64},{64,96},{96,128},{128,160},{160,192},{192,224},{1,3... | collective-permute-start | bytes 196616 | tf_op jit(solution)/shard_map/ppermute | solution.py:870
  69.1 10.9 %collective-permute-start.7 = (bf16[2,128,128]{2,1,0:T(8,128)(2,1)S(1)}, bf16[2,128,128]{2,1,0:T(8,128)(2,1)S(1)}, u32[]{:S(2)}, u32[]{:S(2)}) collective-permute-start(bf16[2,128,128]{2,1,0:T(8,128)(2,1)S(1)} %get-tuple-element.76), channel_id=1, source_target_pairs={{32,0},{64,32},{96,64},{128,96},{160,128},{192,160},{224,192},{33,... | collective-permute-start | bytes 196616 | tf_op jit(solution)/shard_map/ppermute | solution.py:870
  81.0 12.1 %collective-permute-start.8 = (bf16[8,128,128]{2,1,0:T(8,128)(2,1)S(1)}, bf16[8,128,128]{2,1,0:T(8,128)(2,1)S(1)}, u32[]{:S(2)}, u32[]{:S(2)}) collective-permute-start(bf16[8,128,128]{2,1,0:T(8,128)(2,1)S(1)} %get-tuple-element.65), channel_id=1, source_target_pairs={{0,1},{1,2},{2,3},{3,4},{4,5},{5,6},{6,7},{7,8},{8,9},{9,10},{10,1... | collective-permute-start | bytes 786440 | tf_op jit(solution)/shard_map/ppermute | solution.py:870
  82.9 10.2 %collective-permute-start.9 = (bf16[8,128,128]{2,1,0:T(8,128)(2,1)S(1)}, bf16[8,128,128]{2,1,0:T(8,128)(2,1)S(1)}, u32[]{:S(2)}, u32[]{:S(2)}) collective-permute-start(bf16[8,128,128]{2,1,0:T(8,128)(2,1)S(1)} %get-tuple-element.65), channel_id=1, source_target_pairs={{1,0},{2,1},{3,2},{4,3},{5,4},{6,5},{7,6},{8,7},{9,8},{10,9},{11,1... | collective-permute-start | bytes 786440 | tf_op jit(solution)/shard_map/ppermute | solution.py:870
  105.7 18.0 %collective-permute-start.10 = (f32[3,3,128]{2,1,0:T(4,128)S(1)}, f32[3,3,128]{2,1,0:T(4,128)S(1)}, u32[]{:S(2)}, u32[]{:S(2)}) collective-permute-start(f32[3,3,128]{2,1,0:T(4,128)S(1)} %get-tuple-element.70), channel_id=1, source_target_pairs={{0,32},{32,64},{64,96},{96,128},{128,160},{160,192},{192,224},{1,3... | collective-permute-start | bytes 13832 | tf_op jit(solution)/shard_map/ppermute | solution.py:870
  108.9 14.8 %collective-permute-start.11 = (f32[3,3,128]{2,1,0:T(4,128)S(1)}, f32[3,3,128]{2,1,0:T(4,128)S(1)}, u32[]{:S(2)}, u32[]{:S(2)}) collective-permute-start(f32[3,3,128]{2,1,0:T(4,128)S(1)} %get-tuple-element.71), channel_id=1, source_target_pairs={{32,0},{64,32},{96,64},{128,96},{160,128},{192,160},{224,192},{33,... | collective-permute-start | bytes 13832 | tf_op jit(solution)/shard_map/ppermute | solution.py:870
  123.8 14.8 %collective-permute-start.12 = (f32[6,3,128]{2,1,0:T(4,128)S(1)}, f32[6,3,128]{2,1,0:T(4,128)S(1)}, u32[]{:S(2)}, u32[]{:S(2)}) collective-permute-start(f32[6,3,128]{2,1,0:T(4,128)S(1)} %get-tuple-element.84), channel_id=1, source_target_pairs={{0,1},{1,2},{2,3},{3,4},{4,5},{5,6},{6,7},{7,8},{8,9},{9,10},{10,1... | collective-permute-start | bytes 27656 | tf_op jit(solution)/shard_map/ppermute | solution.py:870
  125.7 12.9 %collective-permute-start.13 = (f32[6,3,128]{2,1,0:T(4,128)S(1)}, f32[6,3,128]{2,1,0:T(4,128)S(1)}, u32[]{:S(2)}, u32[]{:S(2)}) collective-permute-start(f32[6,3,128]{2,1,0:T(4,128)S(1)} %get-tuple-element.85), channel_id=1, source_target_pairs={{1,0},{2,1},{3,2},{4,3},{5,4},{6,5},{7,6},{8,7},{9,8},{10,9},{11,1... | collective-permute-start | bytes 27656 | tf_op jit(solution)/shard_map/ppermute | solution.py:870

commit v6 on v5

--- a/solution.py
+++ b/solution.py
@@ -32,8 +32,12 @@
 ]
 
 
+EARLY = range(2, EX - 3)
+LATE = [0, 1, EX - 3, EX - 2, EX - 1]
+
+
 def far_part(e):
-    return 0 if e // EX != 1 else 1 if 2 <= e % EX < EX - 2 else 2
+    return 0 if e // EX != 1 else 1 if e % EX in EARLY else 2
 
 
 FAR_PAIRS = [
@@ -71,7 +75,7 @@
         square_ref[C * i : C * i + C, :] = ref[...]
     wide_ref[...] = jnp.zeros_like(wide_ref)
     wide_ref[0 : table_ref.shape[0], :] = table_ref[...].astype(F32)
-    square_ref[3 * C : 4 * C, :] = wide_ref[...].astype(BF16)
+    out_ref[BX + 3 : BX + 3 + C // 8] = wide_ref[...].reshape(C // 8, 8, C)
     n = jnp.int32(0)
     block_id = lax.broadcasted_iota(jnp.int32, (8, 128), 0)
     mask = jnp.zeros((8, 128), jnp.int32)
@@ -247,12 +251,12 @@
 
 
 def own_kernel(
-    own_ref, list_ref, square_ref,
+    own_ref, list_ref,
     acc_ref,
     ext_ref, col_ref, scaled_s_ref, scaled_v_ref, tile_a_ref, tile_b_ref,
 ):
     ws1_ref, wv1_ref, _, _, _ = radial_parts(own_ref)
-    table = square_parts(square_ref)[3][...]
+    table = table_part(own_ref)
     for h in range(BX):
         ext_ref[h] = own_ref[h]
     ext_ref[BX] = jnp.full((8, A), 1.0e4, F32)
@@ -286,7 +290,8 @@
     maskv_ref, masks_ref, sem,
 ):
     ws1_ref, wv1_ref, ws2_ref, wv2_ref, _ = radial_parts(radial_ref)
-    ms_ref, mv_ref, _, table_ref = square_parts(square_ref)
+    ms_ref, mv_ref, _ = square_parts(square_ref)
+    table = table_part(radial_ref)
     gather_ext(lo_ref, mid_ref, hi_ref, ext_ref)
     copy = send_masks(ext_ref, maskv_ref, masks_ref, sem)
     turned = turned_blocks(ext_ref)
@@ -302,17 +307,14 @@
             if EX <= e < 2 * EX:
                 keep_col_ref[e - EX, d] = column
         hot = (spread_lane(turned, e, 3) == lanes).astype(BF16)
-        init_ref[e] = dot(hot, table_ref[...]).astype(BF16)
+        initial = dot(hot, table).astype(BF16)
+        if EX < e <= EX + BX:
+            init_ref[e] = initial
+        for k in range(K):
+            scaled_s_ref[e, pl.ds(k * A, A), :] = scaled(initial, ws1_ref, k)
+            scaled_v_ref[e, pl.ds(k * A, A), :] = scaled(initial, wv1_ref, k)
     col_ref[E] = jnp.full((3, A, 128), 1.0e4, F32)
     keep_col_ref[EX] = jnp.full((3, A, 128), 1.0e4, F32)
-
-    def scale_block(e, carry):
-        for k in range(K):
-            scaled_s_ref[e, pl.ds(k * A, A), :] = scaled(init_ref[e], ws1_ref, k)
-            scaled_v_ref[e, pl.ds(k * A, A), :] = scaled(init_ref[e], wv1_ref, k)
-        return carry
-
-    lax.fori_loop(0, E, scale_block, 0)
     scaled_s_ref[E] = jnp.zeros((K * A, C), BF16)
     scaled_v_ref[E] = jnp.zeros((K * A, C), BF16)
     acc_ref[...] = acc_own_ref[...]
@@ -394,7 +396,11 @@
 
 
 def square_parts(ref):
-    return [ref.at[pl.ds(C * i, C), :] for i in range(4)]
+    return [ref.at[pl.ds(C * i, C), :] for i in range(3)]
+
+
+def table_part(ref):
+    return ref[BX + 3 : BX + 3 + C // 8].reshape(C, C).astype(BF16)
 
 
 def half(n):
@@ -440,7 +446,7 @@
     acc_ref[...] = jnp.zeros_like(acc_ref)
     down_ref[...] = jnp.zeros_like(down_ref)
     across_ref[...] = jnp.zeros_like(across_ref)
-    cotangents(second_ref, cot_s_ref, cot_v_ref, 0, ws2_ref, wv2_ref, INNER)
+    cotangents(second_ref, cot_s_ref, cot_v_ref, 0, ws2_ref, wv2_ref, EARLY)
     second_moves(
         list2_ref[MIDDLE], list2_ref[THIRD], list2_ref, col_ref, EX, lambda e: rows_of(ext_ref, e),
         feat_ref, cot_s_ref, cot_v_ref, acc_ref, across_ref, down_ref, tile_a_ref, tile_b_ref,
@@ -465,7 +471,7 @@
     for x in INNER:
         energy_ref[x - 1] = energy_part_ref[x - 1]
         second_in_ref[x] = second_part_ref[x]
-        second_own_ref[x] = jnp.zeros((A, C), F32)
+        second_own_ref[x] = second_part_ref[x].astype(F32)
 
 
 def move(across_ref, own, r, near, own_sign, grad_ref):
@@ -602,7 +608,7 @@
     acc_ref[...] = acc_in_ref[...]
     down_ref[...] = down_in_ref[...]
     across_ref[...] = across_in_ref[...]
-    cotangents(in_mid_ref, cot_s_ref, cot_v_ref, 0, ws2_ref, wv2_ref, OUTER)
+    cotangents(in_mid_ref, cot_s_ref, cot_v_ref, 0, ws2_ref, wv2_ref, LATE)
     second_moves(
         list2_ref[THIRD], list2_ref[END], list2_ref, col_ref, EX, lambda e: rows_of(ext_ref, e),
         feat_ref, cot_s_ref, cot_v_ref, acc_ref, across_ref, down_ref, tile_a_ref, tile_b_ref,
@@ -617,7 +623,7 @@
     ext_ref, cot_s_ref, cot_v_ref, acc_ref, tile_a_ref, tile_b_ref, grad_a_ref, grad_b_ref,
 ):
     _, _, ws2_ref, wv2_ref, readout_ref = radial_parts(radial_ref)
-    ms_ref, mv_ref, _, _ = square_parts(square_ref)
+    ms_ref, mv_ref, _ = square_parts(square_ref)
     gather_ext(lo_ref, mid_ref, hi_ref, ext_ref)
     acc_ref[...] = acc_in_ref[...]
     across_ref[...] = across_in_ref[...]
@@ -687,7 +693,7 @@
 
 VMEM = pl.BlockSpec(memory_space=pltpu.VMEM)
 SMEM = pl.BlockSpec(memory_space=pltpu.SMEM)
-PARAMS = pltpu.CompilerParams(vmem_limit_bytes=24 * 1024 * 1024)
+PARAMS = pltpu.CompilerParams(vmem_limit_bytes=28 * 1024 * 1024)
 
 
 SEM = pltpu.SemaphoreType.DMA
@@ -767,7 +773,7 @@
             pltpu.VMEM((4 * A, K * A), BF16),
             pltpu.VMEM((4 * A, K * A), BF16),
         ],
-        in_specs=[VMEM, SMEM, VMEM],
+        in_specs=[VMEM, SMEM],
         cost=LONG,
     )
 
@@ -885,10 +891,10 @@
         ),
         [
             ((1, 8, A), F32),
-            ((BX + 3, 8, A), F32),
+            ((BX + 3 + C // 8, 8, A), F32),
             ((1, 8, A), F32),
             ((64,), jnp.int32),
-            ((4 * C, C), BF16),
+            ((3 * C, C), BF16),
         ],
         [pltpu.VMEM((C, C), F32)],
         in_specs=[VMEM] * 2 + [SMEM] * 2 + [VMEM] * 9,
@@ -896,7 +902,7 @@
         params=pltpu.CompilerParams(vmem_limit_bytes=60 * 1024 * 1024),
     )
     left, right = both(last, first, "gx")
-    (acc,) = own_call(radial, own_list, square)
+    (acc,) = own_call(radial, own_list)
     radial, acc = lax.optimization_barrier((radial, acc))
     ext_mid = jnp.concatenate([left, radial[:BX], right], axis=0)
     ext_lo, ext_hi = both(ext_mid, ext_mid, "gy")

time: 141 us -> 140 us (level)
  the two profiles are of different devices: /device:TPU:18 before, /device:TPU:20 now
where the time goes in v6:
time: 140 us; the launch traced here: 138 us
  starting transfers between devices  66.8 us (48%)
  Pallas kernels  60.3 us (43%)
  waiting for transfers between devices  7.17 us (5%)
  local copies, waits for them, and re-layouts  2.25 us (2%)
  between operations  1.6 us (1%)
    ppermute x14, starting transfers between devices, along(): lax.ppermute(block, axis, [(i, i + step) for i in range(size) if 0 <= i +...  66.8 us
    pallas_call x10, Pallas kernels, call(): pl.pallas_call(kernel, out_shape=[jax.ShapeDtypeStruct(s, d) for s, d in...  60.3 us
    ppermute x14, waiting for transfers between devices, along(): lax.ppermute(block, axis, [(i, i + step) for i in range(size) if 0 <= i +...  7.17 us
  transfers between devices with their start and end apart: 14, of which 3 were waited for; matrix products, arithmetic and copies ran while one was open for 0% of the time, Pallas kernels for 23%

profile of v6, /device:TPU:20, one launch (start us, length us, event | category | flops | bytes accessed | tf_op | source)
XLA Modules:
  0.0 138.4 jit_solution(10005355765050618257)
XLA Ops:
  1.3 1.8 %shard_map.140 = (f32[1,8,128]{2,1,0:T(8,128)}, f32[25,8,128]{2,1,0:T(8,128)}, f32[1,8,128]{2,1,0:T(8,128)}, s32[64]{0:T(128)}, bf16[384,128]{1,0:T(8,128)(2,1)}) custom-call(f32[6,3,1,128]{3,2,1,0:T(1,128)} %bitcast.4, s32[6,1,128]{2,1,0:T(1,128)} %species_ref.1, s32[1,1,26]{2,1,0:T(1,128)} %codes_ref.1, s32[1,1]{1,0:T(1,128)S(6)} %copy.16.count_ref, ...), custom_call_target="tpu_custom_call" | custom-call | tf_op jit(solution)/shard_map/pallas_call | solution.py:863
  3.1 9.1 %collective-permute-start = (f32[1,8,128]{2,1,0:T(8,128)}, f32[1,8,128]{2,1,0:T(8,128)S(1)}, u32[]{:S(2)}, u32[]{:S(2)}) collective-permute-start(f32[1,8,128]{2,1,0:T(8,128)} %get-tuple-element.38), channel_id=1, source_target_pairs={{0,32},{32,64},{64,96},{96,128},{128,160},{160,192},{192,224},{1,3... | collective-permute-start | bytes 12296 | tf_op jit(solution)/shard_map/ppermute | solution.py:876
  12.2 1.9 %collective-permute-start.1 = (f32[1,8,128]{2,1,0:T(8,128)}, f32[1,8,128]{2,1,0:T(8,128)S(1)}, u32[]{:S(2)}, u32[]{:S(2)}) collective-permute-start(f32[1,8,128]{2,1,0:T(8,128)} %get-tuple-element.42), channel_id=1, source_target_pairs={{32,0},{64,32},{96,64},{128,96},{160,128},{192,160},{224,192},{33,... | collective-permute-start | bytes 12296 | tf_op jit(solution)/shard_map/ppermute | solution.py:876
  14.2 0.0 copy-start
  14.2 0.9 copy-done
  15.1 0.7 copy-done.3
  15.7 4.7 %shard_map.141.acc_own_ref = f32[6,512,128]{2,1,0:T(8,128)S(1)} custom-call(f32[25,8,128]{2,1,0:T(8,128)S(1)} %copy-done, s32[64]{0:T(128)S(1)} %copy-done.3), custom_call_target="tpu_custom_call" | custom-call | flops 4000000000 | bytes 1000000 | tf_op jit(solution)/shard_map/pallas_call | solution.py:863
  20.5 0.0 collective-permute-done
  20.5 1.4 %collective-permute-done.1 = f32[1,8,128]{2,1,0:T(8,128)S(1)} collective-permute-done((f32[1,8,128]{2,1,0:T(8,128)}, f32[1,8,128]{2,1,0:T(8,128)S(1)}, u32[]{:S(2)}, u32[]{:S(2)}) %collective-permute-start.1) | collective-permute-done | bytes 4128 | tf_op jit(solution)/shard_map/ppermute | solution.py:876
  21.9 1.9 %collective-permute-start.2 = (f32[8,8,128]{2,1,0:T(8,128)S(1)}, f32[8,8,128]{2,1,0:T(8,128)S(1)}, u32[]{:S(2)}, u32[]{:S(2)}) collective-permute-start(f32[8,8,128]{2,1,0:T(8,128)S(1)} %pad_maximum_fusion.mid_ref.ext_mid_ref), channel_id=1, source_target_pairs={{0,1},{1,2},{2,3},{3,4},{4,5},{5,6},{6,7},{7,8},{8,9},{9,10},{10,1... | collective-permute-start | bytes 98312 | tf_op jit(solution)/shard_map/ppermute | solution.py:876
  23.8 6.3 %collective-permute-start.3 = (f32[8,8,128]{2,1,0:T(8,128)S(1)}, f32[8,8,128]{2,1,0:T(8,128)S(1)}, u32[]{:S(2)}, u32[]{:S(2)}) collective-permute-start(f32[8,8,128]{2,1,0:T(8,128)S(1)} %pad_maximum_fusion.mid_ref.ext_mid_ref), channel_id=1, source_target_pairs={{1,0},{2,1},{3,2},{4,3},{5,4},{6,5},{7,6},{8,7},{9,8},{10,9},{11,1... | collective-permute-start | bytes 98312 | tf_op jit(solution)/shard_map/ppermute | solution.py:876
  30.2 0.1 pad.7.clone
  30.2 0.0 collective-permute-done.2.lo_ref
  30.2 1.5 %collective-permute-done.3.hi_ref = f32[8,8,128]{2,1,0:T(8,128)S(1)} collective-permute-done((f32[8,8,128]{2,1,0:T(8,128)S(1)}, f32[8,8,128]{2,1,0:T(8,128)S(1)}, u32[]{:S(2)}, u32[]{:S(2)}) %collective-permute-start.3) | collective-permute-done | bytes 32800 | tf_op jit(solution)/shard_map/ppermute | solution.py:876
  31.7 0.0 copy-done.2
  31.7 15.0 %shard_map.142 = (f32[6,128,128]{2,1,0:T(8,128)S(1)}, bf16[6,512,128]{2,1,0:T(8,128)(2,1)S(1)}, bf16[8,128,128]{2,1,0:T(8,128)(2,1)S(1)}, bf16[8,128,128]{2,1,0:...) custom-call(f32[8,8,128]{2,1,0:T(8,128)S(1)} %collective-permute-don, ...), custom_call_target="tpu_custom_call" | custom-call | tf_op jit(solution)/shard_map/pallas_call | solution.py:863
  46.8 3.1 %collective-permute-start.4 = (bf16[8,128,128]{2,1,0:T(8,128)(2,1)S(1)}, bf16[8,128,128]{2,1,0:T(8,128)(2,1)S(1)}, u32[]{:S(2)}, u32[]{:S(2)}) collective-permute-start(bf16[8,128,128]{2,1,0:T(8,128)(2,1)S(1)} %get-tuple-element.48), channel_id=1, source_target_pairs={{0,1},{1,2},{2,3},{3,4},{4,5},{5,6},{6,7},{7,8},{8,9},{9,10},{10,1... | collective-permute-start | bytes 786440 | tf_op jit(solution)/shard_map/ppermute | solution.py:876
  49.9 5.2 %collective-permute-start.5 = (bf16[8,128,128]{2,1,0:T(8,128)(2,1)S(1)}, bf16[8,128,128]{2,1,0:T(8,128)(2,1)S(1)}, u32[]{:S(2)}, u32[]{:S(2)}) collective-permute-start(bf16[8,128,128]{2,1,0:T(8,128)(2,1)S(1)} %get-tuple-element.49), channel_id=1, source_target_pairs={{1,0},{2,1},{3,2},{4,3},{5,4},{6,5},{7,6},{8,7},{9,8},{10,9},{11,1... | collective-permute-start | bytes 786440 | tf_op jit(solution)/shard_map/ppermute | solution.py:876
  55.1 0.0 copy-start.1
  55.1 4.9 %shard_map.143.mid_ref = f32[8,128,128]{2,1,0:T(8,128)S(1)} custom-call(f32[8,8,128]{2,1,0:T(8,128)S(1)} %pad_maximum_fusion.mid_ref.ext_mid_ref, s32[64]{0:T(128)S(1)} %get-tuple-element.45.list2_ref, bf16[6,2048,128]{2,1,0:T(8,128)(2,1)S(1)} %get-tuple-element.46.ready_ref, f32[9,3,128,128]{3,2,1,0:T(8,128)S(1)} %get-tuple-element.47.col_ref), custom_call_target="tpu_custom_call" | custom-call | flops 4000000000 | bytes 1000000 | tf_op jit(solution)/shard_map/pallas_call | solution.py:863
  60.0 0.0 collective-permute-done.4.below_ref
  60.0 0.0 collective-permute-done.5.above_ref
  60.0 0.1 fusion.1
  60.1 10.3 %collective-permute-start.6 = (bf16[2,128,128]{2,1,0:T(8,128)(2,1)S(1)}, bf16[2,128,128]{2,1,0:T(8,128)(2,1)S(1)}, u32[]{:S(2)}, u32[]{:S(2)}) collective-permute-start(bf16[2,128,128]{2,1,0:T(8,128)(2,1)S(1)} %get-tuple-element.77), channel_id=1, source_target_pairs={{0,32},{32,64},{64,96},{96,128},{128,160},{160,192},{192,224},{1,3... | collective-permute-start | bytes 196616 | tf_op jit(solution)/shard_map/ppermute | solution.py:876
  70.4 1.9 %collective-permute-start.7 = (bf16[2,128,128]{2,1,0:T(8,128)(2,1)S(1)}, bf16[2,128,128]{2,1,0:T(8,128)(2,1)S(1)}, u32[]{:S(2)}, u32[]{:S(2)}) collective-permute-start(bf16[2,128,128]{2,1,0:T(8,128)(2,1)S(1)} %get-tuple-element.76), channel_id=1, source_target_pairs={{32,0},{64,32},{96,64},{128,96},{160,128},{192,160},{224,192},{33,... | collective-permute-start | bytes 196616 | tf_op jit(solution)/shard_map/ppermute | solution.py:876
  72.3 4.0 %shard_map.144 = (f32[6,1,128]{2,1,0:T(1,128)S(1)}, bf16[8,128,128]{2,1,0:T(8,128)(2,1)S(1)}, f32[6,512,128]{2,1,0:T(8,128)S(1)}, f32[6,3,128,128]{3,2,1,0:T(8,128)S(1)}, f32[9,3,8,128]{3,2,1,0:T(8,128)S(1)}) custom-call(f32[8,128,128]{2,1,0:T(8,128)S(1)} %shard_map.143.mid_ref, bf16[8,128,128]{2,1,0:T(8,128)(2,1)S(1)} %collective-permute-done.4.below_ref, ...), custom_call_target="tpu_custom_call" | custom-call | flops 4000000000 | bytes 1000000 | tf_op jit(solution)/shard_map/pallas_call | solution.py:863
  76.3 0.0 collective-permute-done.6.left_ref
  76.3 4.2 %collective-permute-done.7.right_ref = bf16[2,128,128]{2,1,0:T(8,128)(2,1)S(1)} collective-permute-done((bf16[2,128,128]{2,1,0:T(8,128)(2,1)S(1)}, bf16[2,128,128]{2,1,0:T(8,128)(2,1)S(1)}, u32[]{:S(2)}, u32[]{:S(2)}) %collective-permute-start.7) | collective-permute-done | bytes 65568 | tf_op jit(solution)/shard_map/ppermute | solution.py:876
  80.5 1.0 shard_map.145
  81.6 1.9 %collective-permute-start.8 = (bf16[8,128,128]{2,1,0:T(8,128)(2,1)S(1)}, bf16[8,128,128]{2,1,0:T(8,128)(2,1)S(1)}, u32[]{:S(2)}, u32[]{:S(2)}) collective-permute-start(bf16[8,128,128]{2,1,0:T(8,128)(2,1)S(1)} %get-tuple-element.65), channel_id=1, source_target_pairs={{0,1},{1,2},{2,3},{3,4},{4,5},{5,6},{6,7},{7,8},{8,9},{9,10},{10,1... | collective-permute-start | bytes 786440 | tf_op jit(solution)/shard_map/ppermute | solution.py:876
  83.5 6.3 %collective-permute-start.9 = (bf16[8,128,128]{2,1,0:T(8,128)(2,1)S(1)}, bf16[8,128,128]{2,1,0:T(8,128)(2,1)S(1)}, u32[]{:S(2)}, u32[]{:S(2)}) collective-permute-start(bf16[8,128,128]{2,1,0:T(8,128)(2,1)S(1)} %get-tuple-element.65), channel_id=1, source_target_pairs={{1,0},{2,1},{3,2},{4,3},{5,4},{6,5},{7,6},{8,7},{9,8},{10,9},{11,1... | collective-permute-start | bytes 786440 | tf_op jit(solution)/shard_map/ppermute | solution.py:876
  89.8 6.1 %shard_map.146 = (f32[6,512,128]{2,1,0:T(8,128)S(1)}, f32[6,3,128,128]{3,2,1,0:T(8,128)S(1)}, f32[9,3,8,128]{3,2,1,0:T(8,128)S(1)}) custom-call(f32[8,8,128]{2,1,0:T(8,128)S(1)} %pad_maximum_fusion.mid_ref.ext_mid_ref, s32[64]{0:T(128)S(1)} %get-tuple-element.45.list2_ref, f32[8,128,128]{2,1,0:T(8,128)S(1)} %get-tuple-element.57.in_mid_ref, ...), custom_call_target="tpu_custom_call" | custom-call | flops 4000000000 | bytes 1000000 | tf_op jit(solution)/shard_map/pallas_call | solution.py:863
  95.9 0.0 collective-permute-done.8.in_lo_ref
  95.9 0.0 collective-permute-done.9.in_hi_ref
  95.9 11.2 %shard_map.147 = (f32[3,3,128]{2,1,0:T(4,128)S(1)}, f32[3,3,128]{2,1,0:T(4,128)S(1)}, bf16[6,512,128]{2,1,0:T(8,128)(2,1)S(1)}, f32[25,3,8,128]{3,2,1,0:T(8,128)S(1)}, f32[6,3,128,128]{3,2,1,0:T(8,128)S(1)}) custom-call(f32[8,8,128]{2,1,0:T(8,128)S(1)} %collective-permute-done.2.lo_ref, f32[8,8,128]{2,1,0:T(8,128)S(1)} %pad_maximum_fusion.mid_ref.ext_mid_ref, ...), custom_call_target="tpu_custom_call" | custom-call | tf_op jit(solution)/shard_map/pallas_call | solution.py:863
  107.1 2.7 %collective-permute-start.10 = (f32[3,3,128]{2,1,0:T(4,128)S(1)}, f32[3,3,128]{2,1,0:T(4,128)S(1)}, u32[]{:S(2)}, u32[]{:S(2)}) collective-permute-start(f32[3,3,128]{2,1,0:T(4,128)S(1)} %get-tuple-element.70), channel_id=1, source_target_pairs={{0,32},{32,64},{64,96},{96,128},{128,160},{160,192},{192,224},{1,3... | collective-permute-start | bytes 13832 | tf_op jit(solution)/shard_map/ppermute | solution.py:876
  109.9 7.9 %collective-permute-start.11 = (f32[3,3,128]{2,1,0:T(4,128)S(1)}, f32[3,3,128]{2,1,0:T(4,128)S(1)}, u32[]{:S(2)}, u32[]{:S(2)}) collective-permute-start(f32[3,3,128]{2,1,0:T(4,128)S(1)} %get-tuple-element.71), channel_id=1, source_target_pairs={{32,0},{64,32},{96,64},{128,96},{160,128},{192,160},{224,192},{33,... | collective-permute-start | bytes 13832 | tf_op jit(solution)/shard_map/ppermute | solution.py:876
  117.8 6.6 %shard_map.148 = (f32[6,3,128]{2,1,0:T(4,128)S(1)}, f32[6,3,128]{2,1,0:T(4,128)S(1)}, f32[6,3,128]{2,1,0:T(4,128)S(1)}) custom-call(f32[8,8,128]{2,1,0:T(8,128)S(1)} %collective-permute-done.2.lo_ref, f32[8,8,128]{2,1,0:T(8,128)S(1)} %pad_maximum_fusion.mid_ref.ext_mid_ref, f32[8,8,128]{2,1,0:T(8,128)S(1)} %collective-permute-done.3.hi_ref, ...), custom_call_target="tpu_custom_call" | custom-call | flops 4000000000 | bytes 1000000 | tf_op jit(solution)/shard_map/pallas_call | solution.py:863
  124.4 0.0 collective-permute-done.10
  124.4 0.0 collective-permute-done.11
  124.4 0.1 maximum_add_fusion.1
  124.5 1.9 %collective-permute-start.12 = (f32[6,3,128]{2,1,0:T(4,128)S(1)}, f32[6,3,128]{2,1,0:T(4,128)S(1)}, u32[]{:S(2)}, u32[]{:S(2)}) collective-permute-start(f32[6,3,128]{2,1,0:T(4,128)S(1)} %get-tuple-element.84), channel_id=1, source_target_pairs={{0,1},{1,2},{2,3},{3,4},{4,5},{5,6},{6,7},{7,8},{8,9},{9,10},{10,1... | collective-permute-start | bytes 27656 | tf_op jit(solution)/shard_map/ppermute | solution.py:876
  126.4 6.3 %collective-permute-start.13 = (f32[6,3,128]{2,1,0:T(4,128)S(1)}, f32[6,3,128]{2,1,0:T(4,128)S(1)}, u32[]{:S(2)}, u32[]{:S(2)}) collective-permute-start(f32[6,3,128]{2,1,0:T(4,128)S(1)} %get-tuple-element.85), channel_id=1, source_target_pairs={{1,0},{2,1},{3,2},{4,3},{5,4},{6,5},{7,6},{8,7},{9,8},{10,9},{11,1... | collective-permute-start | bytes 27656 | tf_op jit(solution)/shard_map/ppermute | solution.py:876
  132.7 4.9 %shard_map.149 = f32[8,3,128]{2,1,0:T(4,128)S(1)} custom-call(f32[8,8,128]{2,1,0:T(8,128)S(1)} %pad_maximum_fusion.mid_ref.ext_mid_ref, s32[64]{0:T(128)S(1)} %get-tuple-element.54.list1_ref, bf16[25,512,128]{2,1,0:T(8,128)(2,1)S(1)} %get-tuple-element.55.scaled_s_ref, bf16[25,512,128]{2,1,0:T(8,128)(2,1)S(1)} %get-tuple-element.56.scaled_v_ref, ...), custom_call_target="tpu_custom_call" | custom-call | flops 4000000000 | bytes 1000000 | tf_op jit(solution)/shard_map/pallas_call | solution.py:863
  137.7 0.0 collective-permute-done.12
  137.7 0.0 collective-permute-done.13
  137.7 0.1 fusion.5
  137.8 0.6 copy.15
  (8 shorter events, 0.0 us)
Async XLA Ops:
  3.1 17.3 %collective-permute-start = (f32[1,8,128]{2,1,0:T(8,128)}, f32[1,8,128]{2,1,0:T(8,128)S(1)}, u32[]{:S(2)}, u32[]{:S(2)}) collective-permute-start(f32[1,8,128]{2,1,0:T(8,128)} %get-tuple-element.38), channel_id=1, source_target_pairs={{0,32},{32,64},{64,96},{96,128},{128,160},{160,192},{192,224},{1,3... | collective-permute-start | bytes 12296 | tf_op jit(solution)/shard_map/ppermute | solution.py:876
  12.2 9.7 %collective-permute-start.1 = (f32[1,8,128]{2,1,0:T(8,128)}, f32[1,8,128]{2,1,0:T(8,128)S(1)}, u32[]{:S(2)}, u32[]{:S(2)}) collective-permute-start(f32[1,8,128]{2,1,0:T(8,128)} %get-tuple-element.42), channel_id=1, source_target_pairs={{32,0},{64,32},{96,64},{128,96},{160,128},{192,160},{224,192},{33,... | collective-permute-start | bytes 12296 | tf_op jit(solution)/shard_map/ppermute | solution.py:876
  14.2 0.9 copy-start
  15.1 0.7 copy-start.3
  15.7 16.0 %copy-start.2 = (bf16[384,128]{1,0:T(8,128)(2,1)S(1)}, bf16[384,128]{1,0:T(8,128)(2,1)}, u32[]{:S(2)}) copy-start(bf16[384,128]{1,0:T(8,128)(2,1)} %get-tuple-element.44.square_ref) | copy-start | bytes 294916
  21.9 8.4 %collective-permute-start.2 = (f32[8,8,128]{2,1,0:T(8,128)S(1)}, f32[8,8,128]{2,1,0:T(8,128)S(1)}, u32[]{:S(2)}, u32[]{:S(2)}) collective-permute-start(f32[8,8,128]{2,1,0:T(8,128)S(1)} %pad_maximum_fusion.mid_ref.ext_mid_ref), channel_id=1, source_target_pairs={{0,1},{1,2},{2,3},{3,4},{4,5},{5,6},{6,7},{7,8},{8,9},{9,10},{10,1... | collective-permute-start | bytes 98312 | tf_op jit(solution)/shard_map/ppermute | solution.py:876
  23.8 7.9 %collective-permute-start.3 = (f32[8,8,128]{2,1,0:T(8,128)S(1)}, f32[8,8,128]{2,1,0:T(8,128)S(1)}, u32[]{:S(2)}, u32[]{:S(2)}) collective-permute-start(f32[8,8,128]{2,1,0:T(8,128)S(1)} %pad_maximum_fusion.mid_ref.ext_mid_ref), channel_id=1, source_target_pairs={{1,0},{2,1},{3,2},{4,3},{5,4},{6,5},{7,6},{8,7},{9,8},{10,9},{11,1... | collective-permute-start | bytes 98312 | tf_op jit(solution)/shard_map/ppermute | solution.py:876
  46.8 13.2 %collective-permute-start.4 = (bf16[8,128,128]{2,1,0:T(8,128)(2,1)S(1)}, bf16[8,128,128]{2,1,0:T(8,128)(2,1)S(1)}, u32[]{:S(2)}, u32[]{:S(2)}) collective-permute-start(bf16[8,128,128]{2,1,0:T(8,128)(2,1)S(1)} %get-tuple-element.48), channel_id=1, source_target_pairs={{0,1},{1,2},{2,3},{3,4},{4,5},{5,6},{6,7},{7,8},{8,9},{9,10},{10,1... | collective-permute-start | bytes 786440 | tf_op jit(solution)/shard_map/ppermute | solution.py:876
  49.9 10.1 %collective-permute-start.5 = (bf16[8,128,128]{2,1,0:T(8,128)(2,1)S(1)}, bf16[8,128,128]{2,1,0:T(8,128)(2,1)S(1)}, u32[]{:S(2)}, u32[]{:S(2)}) collective-permute-start(bf16[8,128,128]{2,1,0:T(8,128)(2,1)S(1)} %get-tuple-element.49), channel_id=1, source_target_pairs={{1,0},{2,1},{3,2},{4,3},{5,4},{6,5},{7,6},{8,7},{9,8},{10,9},{11,1... | collective-permute-start | bytes 786440 | tf_op jit(solution)/shard_map/ppermute | solution.py:876
  55.1 17.2 %copy-start.1 = (f32[25,8,128]{2,1,0:T(8,128)S(1)}, f32[25,8,128]{2,1,0:T(8,128)}, u32[]{:S(2)}) copy-start(f32[25,8,128]{2,1,0:T(8,128)} %get-tuple-element.41.own_ref.radial_ref) | copy-start | bytes 307204
  60.1 16.2 %collective-permute-start.6 = (bf16[2,128,128]{2,1,0:T(8,128)(2,1)S(1)}, bf16[2,128,128]{2,1,0:T(8,128)(2,1)S(1)}, u32[]{:S(2)}, u32[]{:S(2)}) collective-permute-start(bf16[2,128,128]{2,1,0:T(8,128)(2,1)S(1)} %get-tuple-element.77), channel_id=1, source_target_pairs={{0,32},{32,64},{64,96},{96,128},{128,160},{160,192},{192,224},{1,3... | collective-permute-start | bytes 196616 | tf_op jit(solution)/shard_map/ppermute | solution.py:876
  70.4 10.2 %collective-permute-start.7 = (bf16[2,128,128]{2,1,0:T(8,128)(2,1)S(1)}, bf16[2,128,128]{2,1,0:T(8,128)(2,1)S(1)}, u32[]{:S(2)}, u32[]{:S(2)}) collective-permute-start(bf16[2,128,128]{2,1,0:T(8,128)(2,1)S(1)} %get-tuple-element.76), channel_id=1, source_target_pairs={{32,0},{64,32},{96,64},{128,96},{160,128},{192,160},{224,192},{33,... | collective-permute-start | bytes 196616 | tf_op jit(solution)/shard_map/ppermute | solution.py:876
  81.6 14.3 %collective-permute-start.8 = (bf16[8,128,128]{2,1,0:T(8,128)(2,1)S(1)}, bf16[8,128,128]{2,1,0:T(8,128)(2,1)S(1)}, u32[]{:S(2)}, u32[]{:S(2)}) collective-permute-start(bf16[8,128,128]{2,1,0:T(8,128)(2,1)S(1)} %get-tuple-element.65), channel_id=1, source_target_pairs={{0,1},{1,2},{2,3},{3,4},{4,5},{5,6},{6,7},{7,8},{8,9},{9,10},{10,1... | collective-permute-start | bytes 786440 | tf_op jit(solution)/shard_map/ppermute | solution.py:876
  83.5 12.4 %collective-permute-start.9 = (bf16[8,128,128]{2,1,0:T(8,128)(2,1)S(1)}, bf16[8,128,128]{2,1,0:T(8,128)(2,1)S(1)}, u32[]{:S(2)}, u32[]{:S(2)}) collective-permute-start(bf16[8,128,128]{2,1,0:T(8,128)(2,1)S(1)} %get-tuple-element.65), channel_id=1, source_target_pairs={{1,0},{2,1},{3,2},{4,3},{5,4},{6,5},{7,6},{8,7},{9,8},{10,9},{11,1... | collective-permute-start | bytes 786440 | tf_op jit(solution)/shard_map/ppermute | solution.py:876
  107.1 17.2 %collective-permute-start.10 = (f32[3,3,128]{2,1,0:T(4,128)S(1)}, f32[3,3,128]{2,1,0:T(4,128)S(1)}, u32[]{:S(2)}, u32[]{:S(2)}) collective-permute-start(f32[3,3,128]{2,1,0:T(4,128)S(1)} %get-tuple-element.70), channel_id=1, source_target_pairs={{0,32},{32,64},{64,96},{96,128},{128,160},{160,192},{192,224},{1,3... | collective-permute-start | bytes 13832 | tf_op jit(solution)/shard_map/ppermute | solution.py:876
  109.9 14.5 %collective-permute-start.11 = (f32[3,3,128]{2,1,0:T(4,128)S(1)}, f32[3,3,128]{2,1,0:T(4,128)S(1)}, u32[]{:S(2)}, u32[]{:S(2)}) collective-permute-start(f32[3,3,128]{2,1,0:T(4,128)S(1)} %get-tuple-element.71), channel_id=1, source_target_pairs={{32,0},{64,32},{96,64},{128,96},{160,128},{192,160},{224,192},{33,... | collective-permute-start | bytes 13832 | tf_op jit(solution)/shard_map/ppermute | solution.py:876
  124.5 13.2 %collective-permute-start.12 = (f32[6,3,128]{2,1,0:T(4,128)S(1)}, f32[6,3,128]{2,1,0:T(4,128)S(1)}, u32[]{:S(2)}, u32[]{:S(2)}) collective-permute-start(f32[6,3,128]{2,1,0:T(4,128)S(1)} %get-tuple-element.84), channel_id=1, source_target_pairs={{0,1},{1,2},{2,3},{3,4},{4,5},{5,6},{6,7},{7,8},{8,9},{9,10},{10,1... | collective-permute-start | bytes 27656 | tf_op jit(solution)/shard_map/ppermute | solution.py:876
  126.4 11.3 %collective-permute-start.13 = (f32[6,3,128]{2,1,0:T(4,128)S(1)}, f32[6,3,128]{2,1,0:T(4,128)S(1)}, u32[]{:S(2)}, u32[]{:S(2)}) collective-permute-start(f32[6,3,128]{2,1,0:T(4,128)S(1)} %get-tuple-element.85), channel_id=1, source_target_pairs={{1,0},{2,1},{3,2},{4,3},{5,4},{6,5},{7,6},{8,7},{9,8},{10,9},{11,1... | collective-permute-start | bytes 27656 | tf_op jit(solution)/shard_map/ppermute | solution.py:876
